TPU v7x, 256 devices: a whole 4x4x8 slice. The times are simulated.
256 devices in a mesh: dp: 16 (over z, y_lo), seq: 16 (over y_hi, x, core).
Axes of the slice: x: 4, y: 4 (y_hi: 2, y_lo: 2; y = y_hi * 2 + y_lo), z: 8, core: 2. Of those that a mesh axis runs over, the one named last changes fastest.
Arguments:
- query_proj: bfloat16 [16, 2048, 1536], P('dp', 'seq'), may hold values from -8 to 8
- key_proj: bfloat16 [16, 2048, 1536], P('dp', 'seq'), may hold values from -8 to 8
- value_proj: bfloat16 [16, 2048, 1536], P('dp', 'seq'), may hold values from -6 to 6
- residual: bfloat16 [16, 2048, 1536], P('dp', 'seq'), may hold values from -3 to 3
- lengths: int32 [16], P('dp'), may hold values from 512 to 2048, as said below
- out_weight: bfloat16 [1536, 1536], replicated, may hold values from -0.15625 to 0.15625
- conv_kernel: float32 [31, 1536], replicated, may hold values from -1 to 1
- cotangent: bfloat16 [16, 2048, 1536], P('dp', 'seq'), may hold values from -6 to 6
Outputs:
- block_out: bfloat16 [16, 2048, 1536], P('dp', 'seq')
- query_grad: bfloat16 [16, 2048, 1536], P('dp', 'seq')
- key_grad: bfloat16 [16, 2048, 1536], P('dp', 'seq')
- value_grad: bfloat16 [16, 2048, 1536], P('dp', 'seq')
- weight_grad: float32 [1536, 1536], P('seq')
- kernel_grad: float32 [31, 1536], replicated
Inputs may be any that keep to these rules, and one draw needn't show every extreme that they name: Frames lengths[b] and later of utterance b are padding.
All inputs are finite; a program needn't handle non-finite values.
Results may differ from a plain program's by a relative error of at most 0.028.
Values may be sent and summed in bfloat16 or wider, within the bound.
No kernel may reach another device: no remote copies, remote signals or barrier semaphores. Data moves between devices by JAX's collectives and lax.ppermute only.
A program may use at most 128 MiB of HBM per device.

v0:
```python
import math

import jax
import jax.numpy as jnp
from jax import lax
from jax.sharding import PartitionSpec as P

HEADS = 16


def padded_2(block, sides, width):
    for axis, dim in sides:
        count = lax.axis_size(axis)
        forward = [(i, i + 1) for i in range(count - 1)]
        backward = [(target, source) for source, target in forward]
        low = lax.ppermute(
            lax.slice_in_dim(block, block.shape[dim] - width, None, axis=dim), axis, forward
        )
        high = lax.ppermute(lax.slice_in_dim(block, 0, width, axis=dim), axis, backward)
        block = jnp.concatenate([low, block, high], axis=dim)
    return block


def block_weights(query_block, key_heads, valid_keys, score_scale):
    scores = (
        jnp.einsum("qhd,khd->hqk", query_block, key_heads, preferred_element_type=jnp.float32)
        * score_scale
    )
    scores = jnp.where(valid_keys[None, None, :], scores, -jnp.inf)
    shifted = jnp.exp(scores - jnp.max(scores, axis=-1, keepdims=True))
    return shifted / jnp.sum(shifted, axis=-1, keepdims=True)


def forward_heads(query_heads, key_heads, value_heads, length, block_rows, score_scale):
    frames, local_heads, head_size = query_heads.shape
    valid_keys = jnp.arange(frames, dtype=jnp.int32) < length
    query_blocks = query_heads.reshape(frames // block_rows, block_rows, local_heads, head_size)

    def forward_one_block(query_block):
        weights = block_weights(query_block, key_heads, valid_keys, score_scale).astype(
            jnp.bfloat16
        )
        mixed = jnp.einsum("hqk,khd->qhd", weights, value_heads, preferred_element_type=jnp.float32)
        return mixed.astype(jnp.bfloat16)

    return lax.map(forward_one_block, query_blocks).reshape(frames, local_heads, head_size)


def backward_heads(
    query_heads, key_heads, value_heads, grad_heads, length, block_rows, score_scale
):
    frames, local_heads, head_size = query_heads.shape
    valid_keys = jnp.arange(frames, dtype=jnp.int32) < length
    block_count = frames // block_rows
    query_blocks = query_heads.reshape(block_count, block_rows, local_heads, head_size)
    grad_blocks = grad_heads.reshape(block_count, block_rows, local_heads, head_size)

    def backward_one_block(totals, inputs):
        key_total, value_total = totals
        query_block, grad_block = inputs
        weights = block_weights(query_block, key_heads, valid_keys, score_scale)
        rounded = weights.astype(jnp.bfloat16)
        value_total = value_total + jnp.einsum(
            "hqk,qhd->khd", rounded, grad_block, preferred_element_type=jnp.float32
        )
        slope = jnp.einsum(
            "qhd,khd->hqk", grad_block, value_heads, preferred_element_type=jnp.float32
        )
        centre = jnp.sum(weights * slope, axis=-1, keepdims=True)
        score_grad = (weights * (slope - centre) * score_scale).astype(jnp.bfloat16)
        query_out = jnp.einsum(
            "hqk,khd->qhd", score_grad, key_heads, preferred_element_type=jnp.float32
        )
        key_total = key_total + jnp.einsum(
            "hqk,qhd->khd", score_grad, query_block, preferred_element_type=jnp.float32
        )
        return ((key_total, value_total), query_out.astype(jnp.bfloat16))

    zeros_heads = jnp.zeros((frames, local_heads, head_size), jnp.float32)
    totals, query_out = lax.scan(
        backward_one_block, (zeros_heads, zeros_heads), (query_blocks, grad_blocks)
    )
    return (
        query_out.reshape(frames, local_heads, head_size),
        totals[0].astype(jnp.bfloat16),
        totals[1].astype(jnp.bfloat16),
    )


def shards(query_proj, key_proj, value_proj, residual, lengths, out_weight, conv_kernel, cotangent):
    batch_dev, frames_dev, model_width = query_proj.shape
    seq_count = lax.axis_size("seq")
    frames = frames_dev * seq_count
    local_width = model_width // seq_count
    head_size = model_width // HEADS
    local_heads = local_width // head_size
    score_scale = 1.0 / math.sqrt(head_size)
    block_rows = min(512, frames)
    kernel_taps = conv_kernel.shape[0]
    halo_width = (kernel_taps - 1) // 2
    query_heads, key_heads, value_heads = (
        lax.all_to_all(query_proj, "seq", split_axis=2, concat_axis=1, tiled=True),
        lax.all_to_all(key_proj, "seq", split_axis=2, concat_axis=1, tiled=True),
        lax.all_to_all(value_proj, "seq", split_axis=2, concat_axis=1, tiled=True),
    )

    def forward_one(inputs):
        query_rows, key_rows, value_rows, length = inputs
        shape_heads = (frames, local_heads, head_size)
        mixed = forward_heads(
            query_rows.reshape(shape_heads),
            key_rows.reshape(shape_heads),
            value_rows.reshape(shape_heads),
            length,
            block_rows,
            score_scale,
        )
        return mixed.reshape(frames, local_width)

    attended_heads = lax.map(forward_one, (query_heads, key_heads, value_heads, lengths))
    attended = lax.all_to_all(attended_heads, "seq", split_axis=1, concat_axis=2, tiled=True)
    flat_attended = attended.reshape(batch_dev * frames_dev, model_width)
    projected = jnp.dot(flat_attended, out_weight, preferred_element_type=jnp.float32)
    block_in = residual.astype(jnp.float32) + projected.reshape(batch_dev, frames_dev, model_width)
    positions = lax.axis_index("seq") * frames_dev + jnp.arange(frames_dev, dtype=jnp.int32)
    frame_mask = (positions[None, :] < lengths[:, None]).astype(jnp.float32)[:, :, None]
    masked = (block_in * frame_mask).astype(jnp.bfloat16)
    padded = padded_2(masked, (("seq", 1),), halo_width)
    conv_out = jnp.zeros((batch_dev, frames_dev, model_width), jnp.float32)
    for offset in range(kernel_taps):
        conv_out = conv_out + conv_kernel[offset] * padded[:, offset : offset + frames_dev].astype(
            jnp.float32
        )
    gate_value = jax.nn.sigmoid(conv_out)
    block_out = (block_in + conv_out * gate_value).astype(jnp.bfloat16)
    silu_slope = gate_value * (1.0 + conv_out * (1.0 - gate_value))
    conv_grad = (cotangent.astype(jnp.float32) * silu_slope).astype(jnp.bfloat16)
    grad_pad = padded_2(conv_grad, (("seq", 1),), halo_width)
    grad_float = conv_grad.astype(jnp.float32)
    masked_grad = jnp.zeros((batch_dev, frames_dev, model_width), jnp.float32)
    kernel_rows = []
    for offset in range(kernel_taps):
        first_row = 2 * halo_width - offset
        masked_grad = masked_grad + conv_kernel[offset] * grad_pad[
            :, first_row : first_row + frames_dev
        ].astype(jnp.float32)
        kernel_rows.append(
            jnp.sum(
                grad_float * padded[:, offset : offset + frames_dev].astype(jnp.float32),
                axis=(0, 1),
            )
        )
    kernel_term = jnp.stack(kernel_rows)
    block_grad = (cotangent.astype(jnp.float32) + frame_mask * masked_grad).astype(jnp.bfloat16)
    flat_grad = block_grad.reshape(batch_dev * frames_dev, model_width)
    mixed_grad = jnp.einsum("nd,cd->nc", flat_grad, out_weight, preferred_element_type=jnp.float32)
    mixed_grad = mixed_grad.astype(jnp.bfloat16).reshape(batch_dev, frames_dev, model_width)
    grad_heads = lax.all_to_all(mixed_grad, "seq", split_axis=2, concat_axis=1, tiled=True)
    weight_rows = lax.psum_scatter(
        jnp.einsum(
            "nc,nd->cd", flat_attended, flat_grad, preferred_element_type=jnp.float32
        ).astype(jnp.bfloat16),
        "seq",
        scatter_dimension=0,
        tiled=True,
    )
    batch_all = batch_dev * lax.axis_size("dp")
    weight_sum = lax.psum(weight_rows, "dp").astype(jnp.float32)
    kernel_sum = lax.psum(kernel_term, ("dp", "seq"))

    def backward_one(inputs):
        query_rows, key_rows, value_rows, grad_rows, length = inputs
        shape_heads = (frames, local_heads, head_size)
        query_out, key_out, value_out = backward_heads(
            query_rows.reshape(shape_heads),
            key_rows.reshape(shape_heads),
            value_rows.reshape(shape_heads),
            grad_rows.reshape(shape_heads),
            length,
            block_rows,
            score_scale,
        )
        return (
            query_out.reshape(frames, local_width),
            key_out.reshape(frames, local_width),
            value_out.reshape(frames, local_width),
        )

    query_back, key_back, value_back = lax.map(
        backward_one, (query_heads, key_heads, value_heads, grad_heads, lengths)
    )
    query_grad, key_grad, value_grad = (
        lax.all_to_all(query_back, "seq", split_axis=1, concat_axis=2, tiled=True),
        lax.all_to_all(key_back, "seq", split_axis=1, concat_axis=2, tiled=True),
        lax.all_to_all(value_back, "seq", split_axis=1, concat_axis=2, tiled=True),
    )
    return (
        block_out,
        query_grad,
        key_grad,
        value_grad,
        weight_sum / batch_all,
        kernel_sum / batch_all,
    )


def solution(mesh):
    return jax.shard_map(
        shards,
        mesh=mesh,
        in_specs=(
            P("dp", "seq", None),
            P("dp", "seq", None),
            P("dp", "seq", None),
            P("dp", "seq", None),
            P("dp"),
            P(),
            P(),
            P("dp", "seq", None),
        ),
        out_specs=(
            P("dp", "seq", None),
            P("dp", "seq", None),
            P("dp", "seq", None),
            P("dp", "seq", None),
            P("seq", None),
            P(),
        ),
        check_vma=False,
    )
```

profile of v0, /device:TPU:2, one launch (start us, length us, event | category | flops | bytes accessed | tf_op | source)
XLA Modules:
  0.0 612.0 jit_solution(6614984874455094071)
XLA Ops:
  10.9 8.8 %reduce.72 = bf16[1536,128]{1,0:T(8,128)(2,1)S(1)} reduce(bf16[1536,1,128]{2,1,0:T(2,128)(2,1)S(1)} %bitcast.224, bf16[]{:T(256)} %broadcast.164), dimensions={1}, to_apply=%bitcast.147.reduce_sub_computation | reduce | bytes 786434
  20.5 7.5 %all-to-all-start = ((bf16[16,2,6144]{2,1,0:T(2,128)(2,1)}), bf16[16,2,6144]{2,1,0:T(2,128)(2,1)S(1)}, u32[]{:S(2)}, u32[]{:S(2)}) async-start(bf16[16,2,6144]{2,1,0:T(2,128)(2,1)} %reshape.316), calls=%async_computation | async-start | bytes 786432 | tf_op jit(solution)/shard_map/all_to_all | solution.py:102
  28.6 8.8 %reduce.73 = bf16[1536,128]{1,0:T(8,128)(2,1)S(1)} reduce(bf16[1536,1,128]{2,1,0:T(2,128)(2,1)S(1)} %bitcast.230, bf16[]{:T(256)} %broadcast.164), dimensions={1}, to_apply=%bitcast.149.reduce_sub_computation | reduce | bytes 786434
  38.3 7.5 %all-to-all-start.1 = ((bf16[16,2,6144]{2,1,0:T(2,128)(2,1)}), bf16[16,2,6144]{2,1,0:T(2,128)(2,1)S(1)}, u32[]{:S(2)}, u32[]{:S(2)}) async-start(bf16[16,2,6144]{2,1,0:T(2,128)(2,1)} %reshape.318), calls=%async_computation.1 | async-start | bytes 786432 | tf_op jit(solution)/shard_map/all_to_all | solution.py:103
  46.4 8.8 %reduce.74 = bf16[1536,128]{1,0:T(8,128)(2,1)S(1)} reduce(bf16[1536,1,128]{2,1,0:T(2,128)(2,1)S(1)} %bitcast.231, bf16[]{:T(256)} %broadcast.164), dimensions={1}, to_apply=%bitcast.151.reduce_sub_computation | reduce | bytes 786434
  56.1 7.2 %all-to-all-start.2 = ((bf16[16,2,6144]{2,1,0:T(2,128)(2,1)}), bf16[16,2,6144]{2,1,0:T(2,128)(2,1)S(1)}, u32[]{:S(2)}, u32[]{:S(2)}) async-start(bf16[16,2,6144]{2,1,0:T(2,128)(2,1)} %reshape.320), calls=%async_computation.2 | async-start | bytes 786432 | tf_op jit(solution)/shard_map/all_to_all | solution.py:104
  65.0 6.2 %all-to-all-done.2 = bf16[16,2,6144]{2,1,0:T(2,128)(2,1)S(1)} async-done(((bf16[16,2,6144]{2,1,0:T(2,128)(2,1)}), bf16[16,2,6144]{2,1,0:T(2,128)(2,1)S(1)}, u32[]{:S(2)}, u32[]{:S(2)}) %all-to-all-start.2) | async-done | bytes 393248 | tf_op jit(solution)/shard_map/all_to_all | solution.py:104
  72.8 18.8 %while.44 = (s32[]{:T(128)}, bf16[4,512,1,96]{1,3,2,0:T(8,128)(2,1)S(1)}, bf16[4,512,1,96]{1,3,2,0:T(8,128)(2,1)S(1)}, bf16[2048,1,96]{0,2,1:T(8,128)(2,1)S(1)},...) while((s32[]{:T(128)}, bf16[4,512,1,96]{1,3,2,0:T(8,128)(2,1)S(1)}, ...), condition=%wide.region_3.4_spmd.clone, body=%wide.region_0.3_spmd.clone.sunk | while | flops 415286272 | bytes 13584481 | solution.py:46
  92.2 11.6 %reduce.75 = bf16[2048,96]{1,0:T(8,128)(2,1)S(1)} reduce(bf16[2048,1,96]{2,1,0:T(2,128)(2,1)S(1)} %bitcast.217, bf16[]{:T(256)} %broadcast.164), dimensions={1}, to_apply=%bitcast.153.reduce_sub_computation | reduce | bytes 786434
  105.4 6.3 %all-to-all-start.3 = ((bf16[16,2,6144]{2,1,0:T(2,128)(2,1)}), bf16[16,2,6144]{2,1,0:T(2,128)(2,1)S(1)}, u32[]{:S(2)}, u32[]{:S(2)}) async-start(bf16[16,2,6144]{2,1,0:T(2,128)(2,1)} %reshape.322), calls=%async_computation.3 | async-start | bytes 786432 | tf_op jit(solution)/shard_map/all_to_all | solution.py:121
  113.1 6.5 %all-to-all-done.3 = bf16[16,2,6144]{2,1,0:T(2,128)(2,1)S(1)} async-done(((bf16[16,2,6144]{2,1,0:T(2,128)(2,1)}), bf16[16,2,6144]{2,1,0:T(2,128)(2,1)S(1)}, u32[]{:S(2)}, u32[]{:S(2)}) %all-to-all-start.3) | async-done | bytes 393248 | tf_op jit(solution)/shard_map/all_to_all | solution.py:121
  121.2 4.1 multiply_convert_fusion.1
  125.3 2.7 collective-permute-start
  128.0 3.2 collective-permute-start.1
  133.0 6.4 %fusion.124 = (f32[1536]{0:T(1024)}, f32[1536]{0:T(1024)}, f32[1536]{0:T(1024)}, f32[1536]{0:T(1024)}, f32[1536]{0:T(1024)}, /*index=5*/f32[1536]{0:T(1024)}, f3...) fusion(bf16[1,15,1536]{2,1,0:T(8,128)(2,1)S(1)} %collective-per, ...), kind=kLoop, calls=%fused_computation.257 | loop fusion | flops 47761920 | bytes 2304000 | tf_op jit(solution)/shard_map/reduce_sum | solution.py:148
  139.4 3.7 collective-permute-start.2
  145.0 3.5 collective-permute-done.3
  148.5 3.8 fusion.77
  152.3 3.5 convolution_convert_fusion.1
  157.7 4.0 fusion.45
  162.2 8.8 %reduce.76 = bf16[1536,128]{1,0:T(8,128)(2,1)S(1)} reduce(bf16[1536,1,128]{2,1,0:T(2,128)(2,1)S(1)} %bitcast.228, bf16[]{:T(256)} %broadcast.164), dimensions={1}, to_apply=%bitcast.155.reduce_sub_computation | reduce | bytes 786434
  171.9 15.4 %all-to-all-start.4 = ((bf16[16,2,6144]{2,1,0:T(2,128)(2,1)}), bf16[16,2,6144]{2,1,0:T(2,128)(2,1)S(1)}, u32[]{:S(2)}, u32[]{:S(2)}) async-start(bf16[16,2,6144]{2,1,0:T(2,128)(2,1)} %reshape.324), calls=%async_computation.4 | async-start | bytes 786432 | tf_op jit(solution)/shard_map/all_to_all | solution.py:158
  211.6 5.0 stack.127
  217.5 37.5 %while.45 = (s32[]{:T(128)}, f32[2048,1,96]{0,2,1:T(8,128)S(1)}, f32[2048,1,96]{0,2,1:T(8,128)S(1)}, bf16[4,512,1,96]{1,3,2,0:T(8,128)(2,1)S(1)}, bf16[4,512,1,9...) while((s32[]{:T(128)}, f32[2048,1,96]{0,2,1:T(8,128)S(1)}, ...), condition=%wide.region_8.9_spmd.clone, body=%wide.region_4.8_spmd.clone.sunk | while | flops 1034732032 | bytes 40503444 | solution.py:80
  255.9 11.8 %reduce.77 = bf16[2048,96]{1,0:T(8,128)(2,1)S(1)} reduce(bf16[2048,1,96]{2,1,0:T(2,128)(2,1)S(1)} %bitcast.219, bf16[]{:T(256)} %broadcast.164), dimensions={1}, to_apply=%bitcast.157.reduce_sub_computation | reduce | bytes 786434
  269.3 7.6 %all-to-all-start.5 = ((bf16[16,2,6144]{2,1,0:T(2,128)(2,1)}), bf16[16,2,6144]{2,1,0:T(2,128)(2,1)}, u32[]{:S(2)}, u32[]{:S(2)}) async-start(bf16[16,2,6144]{2,1,0:T(2,128)(2,1)} %reshape.326), calls=%async_computation.5 | async-start | bytes 786432 | tf_op jit(solution)/shard_map/all_to_all | solution.py:193
  279.0 11.6 %reduce.79 = bf16[2048,96]{1,0:T(8,128)(2,1)S(1)} reduce(bf16[2048,1,96]{2,1,0:T(2,128)(2,1)S(1)} %bitcast.220, bf16[]{:T(256)} %broadcast.164), dimensions={1}, to_apply=%bitcast.161.reduce_sub_computation | reduce | bytes 786434
  292.1 7.2 %all-to-all-start.7 = ((bf16[16,2,6144]{2,1,0:T(2,128)(2,1)}), bf16[16,2,6144]{2,1,0:T(2,128)(2,1)S(1)}, u32[]{:S(2)}, u32[]{:S(2)}) async-start(bf16[16,2,6144]{2,1,0:T(2,128)(2,1)} %reshape.330), calls=%async_computation.7 | async-start | bytes 786432 | tf_op jit(solution)/shard_map/all_to_all | solution.py:195
  301.4 11.6 %reduce.78 = bf16[2048,96]{1,0:T(8,128)(2,1)S(1)} reduce(bf16[2048,1,96]{2,1,0:T(2,128)(2,1)S(1)} %bitcast.216, bf16[]{:T(256)} %broadcast.164), dimensions={1}, to_apply=%bitcast.159.reduce_sub_computation | reduce | bytes 786434
  314.6 7.2 %all-to-all-start.6 = ((bf16[16,2,6144]{2,1,0:T(2,128)(2,1)}), bf16[16,2,6144]{2,1,0:T(2,128)(2,1)S(1)}, u32[]{:S(2)}, u32[]{:S(2)}) async-start(bf16[16,2,6144]{2,1,0:T(2,128)(2,1)} %reshape.328), calls=%async_computation.6 | async-start | bytes 786432 | tf_op jit(solution)/shard_map/all_to_all | solution.py:194
  321.9 143.7 %all-reduce.5.cloned.1.call-done = f32[31,1536]{1,0:T(8,128)} async-done(((f32[31,1536]{1,0:T(8,128)}), f32[31,1536]{1,0:T(8,128)}) %all-reduce.5.cloned.1.call-update) | async-done | bytes 190480 | tf_op jit(solution)/shard_map/psum | solution.py:169
  476.4 125.9 %all-reduce.3.cloned.1.call-done = bf16[96,1536]{1,0:T(8,128)(2,1)} async-done(((bf16[96,1536]{1,0:T(8,128)(2,1)}), bf16[96,1536]{1,0:T(8,128)(2,1)}) %all-reduce.3.cloned.1.call-update) | async-done | bytes 294928 | tf_op jit(solution)/shard_map/psum | solution.py:168
  (190 shorter events, 124.2 us)
Async XLA Ops:
  8.0 20.0 %copy-start.6 = (bf16[1,128,1536]{2,1,0:T(8,128)(2,1)S(1)}, bf16[1,128,1536]{2,1,0:T(8,128)(2,1)}, u32[]{:S(2)}) copy-start(bf16[1,128,1536]{2,1,0:T(8,128)(2,1)} %param.13) | copy-start | bytes 1179652
  8.0 37.8 %copy-start.7 = (bf16[1,128,1536]{2,1,0:T(8,128)(2,1)S(1)}, bf16[1,128,1536]{2,1,0:T(8,128)(2,1)}, u32[]{:S(2)}) copy-start(bf16[1,128,1536]{2,1,0:T(8,128)(2,1)} %param.14) | copy-start | bytes 1179652
  20.5 17.8 %all-to-all-start = ((bf16[16,2,6144]{2,1,0:T(2,128)(2,1)}), bf16[16,2,6144]{2,1,0:T(2,128)(2,1)S(1)}, u32[]{:S(2)}, u32[]{:S(2)}) async-start(bf16[16,2,6144]{2,1,0:T(2,128)(2,1)} %reshape.316), calls=%async_computation | async-start | bytes 786432 | tf_op jit(solution)/shard_map/all_to_all | solution.py:102
  38.3 17.8 %all-to-all-start.1 = ((bf16[16,2,6144]{2,1,0:T(2,128)(2,1)}), bf16[16,2,6144]{2,1,0:T(2,128)(2,1)S(1)}, u32[]{:S(2)}, u32[]{:S(2)}) async-start(bf16[16,2,6144]{2,1,0:T(2,128)(2,1)} %reshape.318), calls=%async_computation.1 | async-start | bytes 786432 | tf_op jit(solution)/shard_map/all_to_all | solution.py:103
  56.1 15.1 %all-to-all-start.2 = ((bf16[16,2,6144]{2,1,0:T(2,128)(2,1)}), bf16[16,2,6144]{2,1,0:T(2,128)(2,1)S(1)}, u32[]{:S(2)}, u32[]{:S(2)}) async-start(bf16[16,2,6144]{2,1,0:T(2,128)(2,1)} %reshape.320), calls=%async_computation.2 | async-start | bytes 786432 | tf_op jit(solution)/shard_map/all_to_all | solution.py:104
  91.6 21.2 %copy-start.10 = (f32[31,1536]{1,0:T(8,128)S(1)}, f32[31,1536]{1,0:T(8,128)}, u32[]{:S(2)}) copy-start(f32[31,1536]{1,0:T(8,128)} %param.18) | copy-start | bytes 571396
  92.1 29.1 %copy-start.8 = (bf16[1,128,1536]{2,1,0:T(8,128)(2,1)S(1)}, bf16[1,128,1536]{2,1,0:T(8,128)(2,1)}, u32[]{:S(2)}) copy-start(bf16[1,128,1536]{2,1,0:T(8,128)(2,1)} %param.15) | copy-start | bytes 1179652
  105.4 14.2 %all-to-all-start.3 = ((bf16[16,2,6144]{2,1,0:T(2,128)(2,1)}), bf16[16,2,6144]{2,1,0:T(2,128)(2,1)S(1)}, u32[]{:S(2)}, u32[]{:S(2)}) async-start(bf16[16,2,6144]{2,1,0:T(2,128)(2,1)} %reshape.322), calls=%async_computation.3 | async-start | bytes 786432 | tf_op jit(solution)/shard_map/all_to_all | solution.py:121
  111.7 202.9 %reduce-scatter.2.cloned.1.call-start = ((), (), s32[]{:S(2)}) async-start(), calls=%async_computation.9 | async-start | bytes 5013504 | tf_op jit(solution)/shard_map/reduce_scatter | solution.py:159
  121.0 11.9 %copy-start.2 = (bf16[1,128,1536]{2,1,0:T(8,128)(2,1)S(1)}, bf16[1,128,1536]{2,1,0:T(8,128)(2,1)}, u32[]{:S(2)}) copy-start(bf16[1,128,1536]{2,1,0:T(8,128)(2,1)} %param.19) | copy-start | bytes 1179652
  125.3 6.1 %collective-permute-start = (bf16[1,15,1536]{2,1,0:T(8,128)(2,1)S(1)}, bf16[1,15,1536]{2,1,0:T(8,128)(2,1)S(1)}, u32[]{:S(2)}, u32[]{:S(2)}) collective-permute-start(bf16[1,15,1536]{2,1,0:T(8,128)(2,1)S(1)} %get-tuple-element.370), channel_id=1, source_target_pairs={{0,1},{1,2},{2,3},{3,4},{4,5},{5,6},{6,7},{7,8},{8,9},{9,10},{10,1... | collective-permute-start | bytes 138248 | tf_op jit(solution)/shard_map/ppermute | solution.py:16
  128.0 4.9 collective-permute-start.1
  131.4 26.2 %copy-start.5 = (bf16[1,15,1536]{2,1,0:T(8,128)(2,1)}, bf16[1,15,1536]{2,1,0:T(8,128)(2,1)S(1)}, u32[]{:S(2)}) copy-start(bf16[1,15,1536]{2,1,0:T(8,128)(2,1)S(1)} %collective-permute-done) | copy-start | bytes 138244
  133.0 12.1 %copy-start.9 = (bf16[1,15,1536]{2,1,0:T(8,128)(2,1)}, bf16[1,15,1536]{2,1,0:T(8,128)(2,1)S(1)}, u32[]{:S(2)}) copy-start(bf16[1,15,1536]{2,1,0:T(8,128)(2,1)S(1)} %collective-permute-done.1) | copy-start | bytes 138244
  139.4 5.6 collective-permute-start.2
  143.1 5.4 collective-permute-start.3
  171.9 45.6 %copy-start.3 = (f32[2048,1,96]{0,2,1:T(8,128)S(1)}, f32[2048,1,96]{0,2,1:T(8,128)}, u32[]{:S(2)}) copy-start(f32[2048,1,96]{0,2,1:T(8,128)} %custom-call.1) | copy-start | bytes 2359300
  171.9 44.7 %all-to-all-start.4 = ((bf16[16,2,6144]{2,1,0:T(2,128)(2,1)}), bf16[16,2,6144]{2,1,0:T(2,128)(2,1)S(1)}, u32[]{:S(2)}, u32[]{:S(2)}) async-start(bf16[16,2,6144]{2,1,0:T(2,128)(2,1)} %reshape.324), calls=%async_computation.4 | async-start | bytes 786432 | tf_op jit(solution)/shard_map/all_to_all | solution.py:158
  187.3 278.2 %all-reduce.5.cloned.1.call-start = ((), (), s32[]{:S(2)}) async-start(), calls=%async_computation.11 | async-start | bytes 393216 | tf_op jit(solution)/shard_map/psum | solution.py:169
  255.0 0.9 copy-start.4
  267.7 31.7 %copy-start = (f32[1,128,1536]{2,1,0:T(8,128)S(1)}, f32[1,128,1536]{2,1,0:T(8,128)}, u32[]{:S(2)}) copy-start(f32[1,128,1536]{2,1,0:T(8,128)} %get-tuple-element.361) | copy-start | bytes 2359300
  267.7 31.7 %copy-start.1 = (f32[1,128,1536]{2,1,0:T(8,128)S(1)}, f32[1,128,1536]{2,1,0:T(8,128)}, u32[]{:S(2)}) copy-start(f32[1,128,1536]{2,1,0:T(8,128)} %get-tuple-element.373) | copy-start | bytes 2359300
  269.3 22.8 %all-to-all-start.5 = ((bf16[16,2,6144]{2,1,0:T(2,128)(2,1)}), bf16[16,2,6144]{2,1,0:T(2,128)(2,1)}, u32[]{:S(2)}, u32[]{:S(2)}) async-start(bf16[16,2,6144]{2,1,0:T(2,128)(2,1)} %reshape.326), calls=%async_computation.5 | async-start | bytes 786432 | tf_op jit(solution)/shard_map/all_to_all | solution.py:193
  292.1 22.5 %all-to-all-start.7 = ((bf16[16,2,6144]{2,1,0:T(2,128)(2,1)}), bf16[16,2,6144]{2,1,0:T(2,128)(2,1)S(1)}, u32[]{:S(2)}, u32[]{:S(2)}) async-start(bf16[16,2,6144]{2,1,0:T(2,128)(2,1)} %reshape.330), calls=%async_computation.7 | async-start | bytes 786432 | tf_op jit(solution)/shard_map/all_to_all | solution.py:195
  299.4 302.9 %all-reduce.3.cloned.1.call-start = ((), (), s32[]{:S(2)}) async-start(), calls=%async_computation.10 | async-start | bytes 589824 | tf_op jit(solution)/shard_map/psum | solution.py:168
  314.6 159.2 %all-to-all-start.6 = ((bf16[16,2,6144]{2,1,0:T(2,128)(2,1)}), bf16[16,2,6144]{2,1,0:T(2,128)(2,1)S(1)}, u32[]{:S(2)}, u32[]{:S(2)}) async-start(bf16[16,2,6144]{2,1,0:T(2,128)(2,1)} %reshape.328), calls=%async_computation.6 | async-start | bytes 786432 | tf_op jit(solution)/shard_map/all_to_all | solution.py:194
Sparse Core Ops, SparseCore 0:
  156.0 101.0 reduce-scatter.1
Sparse Core Ops, SparseCore 1:
  216.7 248.8 all-reduce.4
  468.2 133.9 all-reduce.2
where the time goes:
time: 621 us; the launch traced here: 612 us
  waiting for transfers between devices  287 us (46%)
  other arithmetic  123 us (20%)
  starting transfers between devices  78.2 us (13%)
  local copies, waits for them, and re-layouts  57.9 us (9%)
  matrix products  48 us (8%)
  between operations  17.4 us (3%)
    psum x1, waiting for transfers between devices, shards(): kernel_sum = lax.psum(kernel_term, ('dp', 'seq'))  144 us
    psum x1, waiting for transfers between devices, shards(): weight_sum = lax.psum(weight_rows, 'dp').astype(jnp.float32)  126 us
    unnamed x10, other arithmetic  82 us
    another operation x32, local copies, waits for them, and re-layouts, shards(): kernel_term = jnp.stack(kernel_rows)  25.2 us
    unnamed x55, local copies, waits for them, and re-layouts  23.7 us
    all_to_all x1, starting transfers between devices, shards(): lax.all_to_all(mixed_grad, 'seq', split_axis=2, concat_axis=1, tiled=True)  15.4 us
  transfers between devices with their start and end apart: 15, of which 6 were waited for; matrix products, arithmetic and copies ran while one was open for 26% of the time, Pallas kernels for 0%

commit v1 on v0

v1 whole, which is shorter than its diff:
```python
import math

import jax
import jax.numpy as jnp
from jax import lax
from jax.experimental import pallas as pl
from jax.experimental.pallas import tpu as pltpu
from jax.sharding import PartitionSpec as P

HEADS = 16
HEAD = 96
LANES = 128
TAPS = 31
HALF = 15
HALO = 32
QT = 512
KT = 256
BF = jnp.bfloat16
F32 = jnp.float32
MIB = 2**20


def params(mib):
    return pltpu.CompilerParams(vmem_limit_bytes=mib * MIB)


def cost(flops, moved):
    return pl.CostEstimate(flops=int(flops), bytes_accessed=int(moved), transcendentals=0)


def lane_iota(shape):
    return lax.broadcasted_iota(jnp.int32, shape, len(shape) - 1)


def row_iota(shape):
    return lax.broadcasted_iota(jnp.int32, shape, 0)


def dot(a, b):
    return jnp.dot(a, b, preferred_element_type=F32)


def pre_kernel(q_ref, k_ref, v_ref, o_ref):
    for part, ref in enumerate((q_ref, k_ref, v_ref)):
        turned = ref[...].T
        for h in range(HEADS):
            o_ref[h, part * HEAD : (part + 1) * HEAD, :] = turned[h * HEAD : (h + 1) * HEAD, :]


def pre(q, k, v):
    return pl.pallas_call(
        pre_kernel,
        out_shape=jax.ShapeDtypeStruct((HEADS, 3 * HEAD, LANES), BF),
        compiler_params=params(32),
        cost_estimate=cost(1e6, 3e6),
        name="pre",
    )(q, k, v)


def fwd_kernel(len_ref, x_ref, e_ref, o_ref, inv_ref, pay_ref, kaug, vaug, sbuf):
    step = pl.program_id(0)
    blocks = x_ref.shape[0]
    scale = math.log2(math.e) / math.sqrt(HEAD)

    @pl.when(step == 0)
    def _():
        length = len_ref[0]
        for j in range(blocks):
            rows = pl.ds(j * LANES, LANES)
            bias = jnp.where(j * LANES + lane_iota((32, LANES)) < length, 0.0, -1e30)
            bias = jnp.where(row_iota((32, LANES)) == 0, bias, 0.0)
            turned = jnp.concatenate([x_ref[j, HEAD : 2 * HEAD, :], bias.astype(BF)], axis=0).T
            kaug[rows, 0:LANES] = turned
            kaug[rows, LANES : 2 * LANES] = turned
            vaug[0:HEAD, rows] = x_ref[j, 2 * HEAD : 3 * HEAD, :]
            vaug[HEAD : HEAD + 16, rows] = jnp.where(row_iota((16, LANES)) == 0, 1.0, 0.0).astype(BF)

    per = QT // LANES
    qt = jnp.concatenate([x_ref[step * per + p, 0:HEAD, :] for p in range(per)], axis=1)
    qs = qt.astype(F32) * scale
    hi = qs.astype(BF)
    lo = (qs - hi.astype(F32)).astype(BF)
    one = jnp.where(row_iota((32, QT)) == 0, 1.0, 0.0).astype(BF)
    qaug = jnp.concatenate([hi, one, lo, jnp.zeros((32, QT), BF)], axis=0)
    tiles = kaug.shape[0] // KT
    top = None
    for t in range(tiles):
        s = dot(kaug[t * KT : (t + 1) * KT, :], qaug)
        sbuf[t * KT : (t + 1) * KT, :] = s
        part = jnp.max(s.reshape(KT // 8, 8, QT), axis=0)
        top = part if top is None else jnp.maximum(top, part)
    top = jnp.max(top, axis=0, keepdims=True)
    acc = jnp.zeros((HEAD + 16, QT), F32)
    for t in range(tiles):
        e = jnp.exp2(sbuf[t * KT : (t + 1) * KT, :] - top).astype(BF)
        e_ref[0, t * KT : (t + 1) * KT, :] = e
        acc = acc + dot(vaug[:, t * KT : (t + 1) * KT], e)
    inv = 1.0 / acc[HEAD : HEAD + 1, :]
    out = acc[0:HEAD, :] * inv
    o_ref[...] = out
    inv_ref[...] = jnp.broadcast_to(inv, (8, QT))
    rounded = out.astype(BF)
    for p in range(per):
        pay_ref[step * per + p, 0:HEAD, :] = rounded[:, p * LANES : (p + 1) * LANES]

    @pl.when(step == pl.num_programs(0) - 1)
    def _():
        left = lane_iota((HEAD, LANES)) < LANES // 2
        for j in range(blocks):
            after = pay_ref[min(j + 1, blocks - 1), 0:HEAD, :]
            before = pay_ref[max(j - 1, 0), 0:HEAD, :]
            pay_ref[j, HEAD : 2 * HEAD, :] = jnp.where(left, after, before)


def fwd(length, x):
    blocks = x.shape[0]
    frames = blocks * LANES
    steps = frames // QT
    return pl.pallas_call(
        fwd_kernel,
        grid=(steps,),
        out_shape=(
            jax.ShapeDtypeStruct((steps, frames, QT), BF),
            jax.ShapeDtypeStruct((HEAD, frames), F32),
            jax.ShapeDtypeStruct((8, frames), F32),
            jax.ShapeDtypeStruct((blocks, 2 * HEAD, LANES), BF),
        ),
        in_specs=[
            pl.BlockSpec(memory_space=pltpu.SMEM),
            pl.BlockSpec((blocks, 3 * HEAD, LANES), lambda i: (0, 0, 0)),
        ],
        out_specs=(
            pl.BlockSpec((1, frames, QT), lambda i: (i, 0, 0)),
            pl.BlockSpec((HEAD, QT), lambda i: (0, i)),
            pl.BlockSpec((8, QT), lambda i: (0, i)),
            pl.BlockSpec((blocks, 2 * HEAD, LANES), lambda i: (0, 0, 0)),
        ),
        scratch_shapes=[
            pltpu.VMEM((frames, 2 * LANES), BF),
            pltpu.VMEM((HEAD + 16, frames), BF),
            pltpu.VMEM((frames, QT), F32),
        ],
        compiler_params=params(40),
        cost_estimate=cost(9e9, 1e7),
        name="attend",
    )(length, x)


def conv_kernel_body(
    info_ref, att_ref, res_ref, cot_ref, left_ref, right_ref, w_ref, taps_ref,
    out_ref, pay_ref, bg_ref, send_ref, keep_ref,
    lhs, block_in, masked, cot, grad, taps_sum,
):
    rows = res_ref.shape[0]
    width = res_ref.shape[1]
    cols = width // LANES
    span = rows + 2 * HALO
    length = info_ref[0]
    first = info_ref[1]
    core = info_ref[2]
    for i in range(HEADS // 2):
        keep_ref[i] = att_ref[2 * i + core, 0:HEAD, :]
        send_ref[i] = att_ref[2 * i + 1 - core, 0:HEAD, :]
    main = jnp.concatenate([att_ref[h, 0:HEAD, :] for h in range(HEADS)], axis=0)
    halo = jnp.concatenate([att_ref[h, HEAD : 2 * HEAD, :] for h in range(HEADS)], axis=0)
    halo = halo.T
    lhs[0:HALO, :] = halo[LANES - HALO : LANES, :]
    lhs[HALO : HALO + rows, :] = main.T
    lhs[HALO + rows : span, :] = halo[0:HALO, :]
    frame = first - HALO + row_iota((span, LANES))
    valid = jnp.logical_and(frame >= 0, frame < length)
    for n in range(cols // 2):
        wide = slice(2 * n * LANES, 2 * (n + 1) * LANES)
        proj = dot(lhs[...], w_ref[:, wide])
        for m in range(2):
            c = 2 * n + m
            at = slice(c * LANES, (c + 1) * LANES)
            res = jnp.concatenate(
                [left_ref[0:HALO, at], res_ref[:, at], right_ref[0:HALO, at]], axis=0
            ).astype(F32)
            block = res + proj[:, m * LANES : (m + 1) * LANES]
            block_in[c] = block
            masked[c] = jnp.where(valid, block, 0.0).astype(BF).astype(F32)
            cot[c] = jnp.concatenate(
                [left_ref[HALO + 16 : 2 * HALO, at], cot_ref[:, at], right_ref[HALO : HALO + 16, at]],
                axis=0,
            ).astype(F32)
    mid = rows + 32

    @pl.loop(0, cols)
    def _(c):
        at = pl.ds(pl.multiple_of(c * LANES, LANES), LANES)
        acc = jnp.zeros((mid, LANES), F32)
        for r in range(TAPS):
            acc = acc + taps_ref[r : r + 1, at] * masked[c, 1 + r : 1 + r + mid, :]
        gate = jax.nn.sigmoid(acc)
        cg = (cot[c] * (gate * (1.0 + acc * (1.0 - gate)))).astype(BF).astype(F32)
        grad[...] = cg
        out_ref[:, at] = (
            block_in[c, HALO : HALO + rows, :] + (acc * gate)[16 : 16 + rows, :]
        ).astype(BF)
        own = cg[16 : 16 + rows, :]
        back = jnp.zeros((rows, LANES), F32)
        for r in range(TAPS):
            back = back + taps_ref[r : r + 1, at] * grad[31 - r : 31 - r + rows, :]
            prod = own * masked[c, 17 + r : 17 + r + rows, :]
            prod = jnp.sum(prod.reshape(rows // 8, 8, LANES), axis=0)
            taps_sum[r // 2, pl.ds((r % 2) * cols + c, 1), :] = jnp.sum(prod, axis=0, keepdims=True)
        own_valid = valid[HALO : HALO + rows, :]
        bg_ref[:, at] = (cot[c, 16 : 16 + rows, :] + jnp.where(own_valid, back, 0.0)).astype(BF)

    taps_sum[HEADS - 1, pl.ds(cols, cols), :] = jnp.zeros((cols, LANES), F32)
    taps_sum[:, pl.ds(2 * cols, 8), :] = jnp.zeros((HEADS, 8, LANES), F32)
    bg = bg_ref[...]
    for h in range(0, HEADS, 2):
        mixed = lax.dot_general(
            w_ref[h * HEAD : (h + 2) * HEAD, :], bg, (((1,), (1,)), ((), ())),
            preferred_element_type=F32,
        ).astype(BF)
        pay_ref[h, 0:HEAD, :] = mixed[0:HEAD]
        pay_ref[h + 1, 0:HEAD, :] = mixed[HEAD : 2 * HEAD]
    pay_ref[:, HEAD:LANES, :] = taps_sum[...].astype(BF)


def conv(info, att, res, cot, left, right, w, taps):
    rows, width = res.shape
    cols = width // LANES
    span = rows + 2 * HALO
    vm = pl.BlockSpec(memory_space=pltpu.VMEM)
    return pl.pallas_call(
        conv_kernel_body,
        out_shape=(
            jax.ShapeDtypeStruct((rows, width), BF),
            jax.ShapeDtypeStruct((HEADS, LANES, LANES), BF),
            jax.ShapeDtypeStruct((rows, width), BF),
            jax.ShapeDtypeStruct((HEADS // 2, HEAD, LANES), BF),
            jax.ShapeDtypeStruct((HEADS // 2, HEAD, LANES), BF),
        ),
        in_specs=[pl.BlockSpec(memory_space=pltpu.SMEM)] + [vm] * 7,
        out_specs=(vm,) * 5,
        scratch_shapes=[
            pltpu.VMEM((span, width), BF),
            pltpu.VMEM((cols, span, LANES), F32),
            pltpu.VMEM((cols, span, LANES), F32),
            pltpu.VMEM((cols, rows + 32, LANES), F32),
            pltpu.VMEM((rows + 32, LANES), F32),
            pltpu.VMEM((HEADS, 32, LANES), F32),
        ],
        compiler_params=params(40),
        cost_estimate=cost(9e9, 1e7),
        name="convolve",
    )(info, att, res, cot, left, right, w, taps)


def outer_kernel(a_ref, b_ref, g_ref, h_ref, o_ref):
    half = HEADS // 2
    lhs = jnp.concatenate(
        [a_ref[...].reshape(half * HEAD, LANES), b_ref[...].reshape(half * HEAD, LANES)], axis=1
    )
    width = g_ref.shape[1]
    for n in range(width // 256):
        at = slice(n * 256, (n + 1) * 256)
        rhs = jnp.concatenate([g_ref[:, at], h_ref[:, at]], axis=0)
        o_ref[:, :, at] = dot(lhs, rhs).astype(BF).reshape(half, HEAD, 256)


def outer(a, b, g, h):
    return pl.pallas_call(
        outer_kernel,
        out_shape=jax.ShapeDtypeStruct((HEADS // 2, HEAD, g.shape[1]), BF),
        compiler_params=params(32),
        cost_estimate=cost(1e9, 4e6),
        name="outer",
    )(a, b, g, h)


def bwd_kernel(x_ref, g_ref, e_ref, o_ref, inv_ref, pay_ref, vaug, kt, dk, dv):
    step = pl.program_id(0)
    blocks = x_ref.shape[0]
    scale = 1.0 / math.sqrt(HEAD)

    @pl.when(step == 0)
    def _():
        ones = jnp.where(row_iota((32, LANES)) < 3, 1.0, 0.0).astype(BF)
        for j in range(blocks):
            rows = pl.ds(j * LANES, LANES)
            turned = jnp.concatenate([x_ref[j, 2 * HEAD : 3 * HEAD, :], ones], axis=0).T
            vaug[rows, 0:LANES] = turned
            vaug[rows, LANES : 2 * LANES] = turned
            kt[:, rows] = x_ref[j, HEAD : 2 * HEAD, :]
        dk[...] = jnp.zeros_like(dk)
        dv[...] = jnp.zeros_like(dv)

    per = QT // LANES
    gt = jnp.concatenate([g_ref[step * per + p, 0:HEAD, :] for p in range(per)], axis=1).astype(F32)
    qt = jnp.concatenate([x_ref[step * per + p, 0:HEAD, :] for p in range(per)], axis=1)
    inv = inv_ref[0:1, :]
    centre = jnp.sum(gt * o_ref[...], axis=0, keepdims=True)
    ginv = gt * inv
    sg = ginv * scale
    hi = sg.astype(BF)
    lo = (sg - hi.astype(F32)).astype(BF)
    rest = centre * inv * (-scale)
    c0 = rest.astype(BF).astype(F32)
    c1 = (rest - c0).astype(BF).astype(F32)
    c2 = rest - c0 - c1
    at = row_iota((32, QT))
    crows = jnp.where(at == 0, c0, jnp.where(at == 1, c1, jnp.where(at == 2, c2, 0.0))).astype(BF)
    zeros = jnp.zeros((32, QT), BF)
    gaug = jnp.concatenate([hi, crows, lo, zeros], axis=0)
    gn = jnp.concatenate([ginv.astype(BF), zeros], axis=0).T
    qn = jnp.concatenate([qt, zeros], axis=0).T
    dq = jnp.zeros((HEAD, QT), F32)
    for t in range(kt.shape[1] // KT):
        rows = slice(t * KT, (t + 1) * KT)
        slope = dot(vaug[rows, :], gaug)
        e = e_ref[0, rows, :]
        ds = (e.astype(F32) * slope).astype(BF)
        dv[rows, :] += dot(e, gn)
        dk[rows, :] += dot(ds, qn)
        dq = dq + dot(kt[:, rows], ds)
    dq = dq.astype(BF)
    for p in range(per):
        pay_ref[step * per + p, 0:HEAD, :] = dq[:, p * LANES : (p + 1) * LANES]

    @pl.when(step == pl.num_programs(0) - 1)
    def _():
        total = jnp.zeros((32, LANES), F32)
        for j in range(blocks):
            total = total + g_ref[j, HEAD:LANES, :].astype(F32)
        total = total.astype(BF)
        for j in range(blocks):
            rows = pl.ds(j * LANES, LANES)
            pay_ref[j, HEAD : 2 * HEAD, :] = dk[rows, :].T[0:HEAD].astype(BF)
            pay_ref[j, 2 * HEAD : 3 * HEAD, :] = dv[rows, :].T[0:HEAD].astype(BF)
            pay_ref[j, 3 * HEAD : 3 * HEAD + 32, :] = total


def bwd(x, g, e, o, inv):
    blocks = x.shape[0]
    frames = blocks * LANES
    steps = frames // QT
    return pl.pallas_call(
        bwd_kernel,
        grid=(steps,),
        out_shape=jax.ShapeDtypeStruct((blocks, 3 * HEAD + 32, LANES), BF),
        in_specs=[
            pl.BlockSpec((blocks, 3 * HEAD, LANES), lambda i: (0, 0, 0)),
            pl.BlockSpec((blocks, LANES, LANES), lambda i: (0, 0, 0)),
            pl.BlockSpec((1, frames, QT), lambda i: (i, 0, 0)),
            pl.BlockSpec((HEAD, QT), lambda i: (0, i)),
            pl.BlockSpec((8, QT), lambda i: (0, i)),
        ],
        out_specs=pl.BlockSpec((blocks, 3 * HEAD + 32, LANES), lambda i: (0, 0, 0)),
        scratch_shapes=[
            pltpu.VMEM((frames, 2 * LANES), BF),
            pltpu.VMEM((HEAD, frames), BF),
            pltpu.VMEM((frames, LANES), F32),
            pltpu.VMEM((frames, LANES), F32),
        ],
        compiler_params=params(40),
        cost_estimate=cost(2e10, 1e7),
        name="attend_back",
    )(x, g, e, o, inv)


def post_kernel(x_ref, q_ref, k_ref, v_ref):
    for part, ref in enumerate((q_ref, k_ref, v_ref)):
        rows = slice(part * HEAD, (part + 1) * HEAD)
        ref[...] = jnp.concatenate([x_ref[h, rows, :] for h in range(HEADS)], axis=0).T


def post(x):
    shape = jax.ShapeDtypeStruct((LANES, HEADS * HEAD), BF)
    return pl.pallas_call(
        post_kernel,
        out_shape=(shape,) * 3,
        compiler_params=params(32),
        cost_estimate=cost(1e6, 3e6),
        name="post",
    )(x)


def pack_kernel(w_ref, x_ref, o_ref):
    width = w_ref.shape[2]
    cols = width // LANES
    share = (HEAD // 8) * cols // HEADS
    for d in range(HEADS):
        parts = []
        for n in range(d * share, (d + 1) * share):
            r, c = 8 * (n // cols), LANES * (n % cols)
            parts.append(
                jnp.sum(w_ref[:, r : r + 8, c : c + LANES].astype(F32), axis=0)
            )
        parts.append(x_ref[d, 3 * HEAD : 3 * HEAD + 24, :].astype(F32))
        o_ref[d] = jnp.concatenate(parts, axis=0).astype(BF)


def pack(w, x):
    return pl.pallas_call(
        pack_kernel,
        out_shape=jax.ShapeDtypeStruct((HEADS, HEAD, LANES), BF),
        compiler_params=params(32),
        cost_estimate=cost(1e6, 3e6),
        name="pack",
    )(w, x)


def total_kernel(x_ref, o_ref):
    total = jnp.sum(x_ref[...].astype(F32), axis=0) * (1.0 / x_ref.shape[0])
    o_ref[...] = jnp.broadcast_to(total.astype(BF)[None], o_ref.shape)


def total(x):
    return pl.pallas_call(
        total_kernel,
        out_shape=jax.ShapeDtypeStruct(x.shape, BF),
        compiler_params=params(32),
        cost_estimate=cost(1e6, 1e6),
        name="total",
    )(x)


def unpack_kernel(x_ref, w_ref, k_ref):
    cols = w_ref.shape[1] // LANES
    share = (HEAD // 8) * cols // HEADS
    for d in range(HEADS):
        x = x_ref[d].astype(F32)
        for i in range(share):
            n = d * share + i
            r, c = 8 * (n // cols), LANES * (n % cols)
            w_ref[r : r + 8, c : c + LANES] = x[8 * i : 8 * i + 8, :]
        for i in range(2):
            if 2 * d + i < TAPS:
                for c in range(cols):
                    k_ref[2 * d + i : 2 * d + i + 1, c * LANES : (c + 1) * LANES] = x[
                        8 * share + cols * i + c : 8 * share + cols * i + c + 1, :
                    ]


def unpack(x, width):
    return pl.pallas_call(
        unpack_kernel,
        out_shape=(
            jax.ShapeDtypeStruct((HEAD, width), F32),
            jax.ShapeDtypeStruct((TAPS, width), F32),
        ),
        compiler_params=params(32),
        cost_estimate=cost(1e6, 1e6),
        name="unpack",
    )(x)


def exchange(x, axis, groups=None):
    return lax.all_to_all(
        x, axis, split_axis=0, concat_axis=0, tiled=True, axis_index_groups=groups
    )


def shards(query_proj, key_proj, value_proj, residual, lengths, out_weight, conv_kernel, cotangent):
    rows, width = query_proj.shape[1:]
    count = lax.axis_size("seq")
    me = lax.axis_index("seq")
    res, cot = residual[0], cotangent[0]
    up = [(i, i + 1) for i in range(count - 1)]
    down = [(i + 1, i) for i in range(count - 1)]
    pairs = [(i, i ^ 1) for i in range(count)]
    same_core = [list(range(c, count, 2)) for c in range(2)]

    heads = exchange(pre(query_proj[0], key_proj[0], value_proj[0]), "seq")
    left = lax.ppermute(jnp.concatenate([res[-HALO:], cot[-HALO:]], axis=0), "seq", up)
    right = lax.ppermute(jnp.concatenate([res[:HALO], cot[:HALO]], axis=0), "seq", down)
    weights, mixed, inv, payload = fwd(lengths, heads)
    attended = exchange(payload, "seq")
    info = jnp.stack([lengths[0], me * rows, me % 2]).astype(jnp.int32)
    block_out, payload, block_grad, send, keep = conv(
        info, attended, res, cot, left, right, out_weight, conv_kernel
    )
    grads = exchange(payload, "seq")
    partner_att = lax.ppermute(send, "seq", pairs)
    partner_grad = lax.ppermute(block_grad, "seq", pairs)
    partial = outer(keep, partner_att, block_grad, partner_grad)
    partial = exchange(partial, "seq", same_core)
    payload = bwd(heads, grads, weights, mixed, inv)
    back = exchange(payload, "seq")
    query_grad, key_grad, value_grad = post(back)
    packed = exchange(pack(partial, back), "dp")
    final = exchange(total(packed), "dp")
    weight_grad, kernel_grad = unpack(final, width)
    return (
        block_out[None],
        query_grad[None],
        key_grad[None],
        value_grad[None],
        weight_grad,
        kernel_grad,
    )


def solution(mesh):
    split = P("dp", "seq", None)
    return jax.shard_map(
        shards,
        mesh=mesh,
        in_specs=(split, split, split, split, P("dp"), P(), P(), split),
        out_specs=(split, split, split, split, P("seq", None), P()),
        check_vma=False,
    )
```

time: 621 us -> 205 us (0.33); the launches traced: 612 us -> 204 us
  waiting for transfers between devices: 287 us -> 47.6 us
  other arithmetic: 123 us -> 0.78 us
  blocking collectives: 0 us -> 76.3 us
  matrix products: 48 us -> 0 us
  starting transfers between devices: 78.2 us -> 31.1 us
  local copies, waits for them, and re-layouts: 57.9 us -> 13.2 us
  Pallas kernels: 0 us -> 33.8 us
  between operations: 17.4 us -> 1.46 us
    psum x2 -> x0, waiting for transfers between devices: 270 us -> none  [the longest x1 144 us: shards(): kernel_sum = lax.psum(kernel_term, ('dp', 'seq'))]
    unnamed x10 -> x0, other arithmetic: 82 us -> none
    all_to_all x0 -> x3, blocking collectives: none -> 76.3 us  [exchange(): lax.all_to_all(x, axis, split_axis=0, concat_axis=0, tiled=True, axis_ind...]
    dot_general x31 -> x0, matrix products: 48 us -> none  [the longest x4 9.86 us: backward_one_block(): jnp.einsum('qhd,khd->hqk', grad_block, value_heads, preferred_element_typ...]
    all_to_all x8 -> x4, starting transfers between devices: 66.1 us -> 25.1 us  [exchange(): lax.all_to_all(x, axis, split_axis=0, concat_axis=0, tiled=True, axis_ind...]
    pallas_call x0 -> x9, Pallas kernels: none -> 33.8 us  [the longest x1 10.3 us: bwd(): pl.pallas_call(bwd_kernel, grid=(steps,), out_shape=jax.ShapeDtypeStruct(...]
    all_to_all x8 -> x4, waiting for transfers between devices: 12.7 us -> 40.5 us  [exchange(): lax.all_to_all(x, axis, split_axis=0, concat_axis=0, tiled=True, axis_ind...]
    another operation x34 -> x0, local copies, waits for them, and re-layouts: 25.3 us -> none  [the longest x32 25.2 us: shards(): kernel_term = jnp.stack(kernel_rows)]
  transfers between devices with their start and end apart: 15 -> 8, of which waited for: 6 -> 5; matrix products, arithmetic and copies ran while one was open for 26% -> 0% of each run, Pallas kernels for 0% -> 1%
where the time goes in v1:
time: 205 us; the launch traced here: 204 us
  blocking collectives  76.3 us (37%)
  waiting for transfers between devices  47.6 us (23%)
  Pallas kernels  33.8 us (16%)
  starting transfers between devices  31.1 us (15%)
  local copies, waits for them, and re-layouts  13.2 us (6%)
    all_to_all x3, blocking collectives, exchange(): lax.all_to_all(x, axis, split_axis=0, concat_axis=0, tiled=True, axis_ind...  76.3 us
    all_to_all x4, waiting for transfers between devices, exchange(): lax.all_to_all(x, axis, split_axis=0, concat_axis=0, tiled=True, axis_ind...  40.5 us
    all_to_all x4, starting transfers between devices, exchange(): lax.all_to_all(x, axis, split_axis=0, concat_axis=0, tiled=True, axis_ind...  25.1 us
    unnamed x40, local copies, waits for them, and re-layouts  13.2 us
    pallas_call x1, Pallas kernels, bwd(): pl.pallas_call(bwd_kernel, grid=(steps,), out_shape=jax.ShapeDtypeStruct(...  10.3 us
    pallas_call x1, Pallas kernels, conv(): pl.pallas_call(conv_kernel_body, out_shape=(jax.ShapeDtypeStruct((rows, w...  9.35 us
    pallas_call x1, Pallas kernels, fwd(): pl.pallas_call(fwd_kernel, grid=(steps,), out_shape=(jax.ShapeDtypeStruct...  8.71 us
    ppermute x1, waiting for transfers between devices, shards(): lax.ppermute(jnp.concatenate([res[-HALO:], cot[-HALO:]], axis=0), 'seq', up)  5.67 us
  transfers between devices with their start and end apart: 8, of which 5 were waited for; matrix products, arithmetic and copies ran while one was open for 0% of the time, Pallas kernels for 1%

profile of v1, /device:TPU:2, one launch (start us, length us, event | category | flops | bytes accessed | tf_op | source)
XLA Modules:
  0.0 204.3 jit_solution(10367961759969565109)
XLA Ops:
  0.6 1.0 copy-done.1
  1.6 1.0 copy-done.2
  2.6 1.0 copy-done.3
  3.6 1.4 pre.1
  5.0 7.5 %all-to-all-start = ((bf16[16,288,128]{2,1,0:T(8,128)(2,1)}), bf16[16,288,128]{2,1,0:T(8,128)(2,1)S(1)}, u32[]{:S(2)}, u32[]{:S(2)}) async-start(bf16[16,288,128]{2,1,0:T(8,128)(2,1)} %pre.1), calls=%async_computation | async-start | bytes 2359296 | tf_op jit(solution)/shard_map/all_to_all | solution.py:455
  13.2 15.7 %all-to-all-done.x_ref = bf16[16,288,128]{2,1,0:T(8,128)(2,1)S(1)} async-done(((bf16[16,288,128]{2,1,0:T(8,128)(2,1)}), bf16[16,288,128]{2,1,0:T(8,128)(2,1)S(1)}, u32[]{:S(2)}, u32[]{:S(2)}) %all-to-all-start) | async-done | bytes 1179680 | tf_op jit(solution)/shard_map/all_to_all | solution.py:455
  28.8 8.7 %attend.1 = (bf16[4,2048,512]{2,1,0:T(8,128)(2,1)S(1)}, f32[96,2048]{1,0:T(8,128)S(1)}, f32[8,2048]{1,0:T(8,128)S(1)}, bf16[16,192,128]{2,1,0:T(8,128)(2,1)}) custom-call(s32[1]{0:T(128)S(6)} %copy.14.len_ref, bf16[16,288,128]{2,1,0:T(8,128)(2,1)S(1)} %all-to-all-done.x_ref), custom_call_target="tpu_custom_call" | custom-call | flops 8999999488 | bytes 10000000 | tf_op jit(solution)/shard_map/attend/pallas_call | solution.py:119
  37.5 3.3 %copy-done.14 = bf16[4,2048,512]{2,1,0:T(8,128)(2,1)} copy-done((bf16[4,2048,512]{2,1,0:T(8,128)(2,1)}, bf16[4,2048,512]{2,1,0:T(8,128)(2,1)S(1)}, u32[]{:S(2)}) %copy-start.14) | copy-done | bytes 8388632
  40.8 0.9 copy-done.16
  42.3 6.7 %all-to-all-start.1 = ((bf16[16,192,128]{2,1,0:T(8,128)(2,1)}), bf16[16,192,128]{2,1,0:T(8,128)(2,1)S(1)}, u32[]{:S(2)}, u32[]{:S(2)}) async-start(bf16[16,192,128]{2,1,0:T(8,128)(2,1)} %get-tuple-element.20), calls=%async_computation.1 | async-start | bytes 1572864 | tf_op jit(solution)/shard_map/all_to_all | solution.py:455
  49.0 0.7 pad_maximum_fusion
  49.7 2.0 %collective-permute-start = (bf16[64,1536]{1,0:T(8,128)(2,1)}, bf16[64,1536]{1,0:T(8,128)(2,1)S(1)}, u32[]{:S(2)}, u32[]{:S(2)}) collective-permute-start(bf16[64,1536]{1,0:T(8,128)(2,1)} %pad_maximum_fusion), channel_id=1, source_target_pairs={{0,1},{1,2},{2,3},{3,4},{4,5},{5,6},{6,7},{7,8},{8,9},{9,10},{10,1... | collective-permute-start | bytes 589832 | tf_op jit(solution)/shard_map/ppermute | solution.py:471
  51.8 3.5 %collective-permute-start.1 = (bf16[64,1536]{1,0:T(8,128)(2,1)S(1)}, bf16[64,1536]{1,0:T(8,128)(2,1)S(1)}, u32[]{:S(2)}, u32[]{:S(2)}) collective-permute-start(bf16[64,1536]{1,0:T(8,128)(2,1)S(1)} %pad_maximum_fusion.1), channel_id=1, source_target_pairs={{1,0},{2,1},{3,2},{4,3},{5,4},{6,5},{7,6},{8,7},{9,8},{10,9},{11,1... | collective-permute-start | bytes 589832 | tf_op jit(solution)/shard_map/ppermute | solution.py:472
  55.4 5.7 %collective-permute-done.left_ref = bf16[64,1536]{1,0:T(8,128)(2,1)S(1)} collective-permute-done((bf16[64,1536]{1,0:T(8,128)(2,1)}, bf16[64,1536]{1,0:T(8,128)(2,1)S(1)}, u32[]{:S(2)}, u32[]{:S(2)}) %collective-permute-start) | collective-permute-done | bytes 196640 | tf_op jit(solution)/shard_map/ppermute | solution.py:471
  61.1 0.7 copy-done.8
  61.8 2.3 %copy-done.6 = bf16[1536,1536]{1,0:T(8,128)(2,1)S(1)} copy-done((bf16[1536,1536]{1,0:T(8,128)(2,1)S(1)}, bf16[1536,1536]{1,0:T(8,128)(2,1)}, u32[]{:S(2)}) %copy-start.6) | copy-done | bytes 4718616
  64.1 0.9 copy-done.9
  65.0 9.3 %convolve.1 = (bf16[128,1536]{1,0:T(8,128)(2,1)}, bf16[16,128,128]{2,1,0:T(8,128)(2,1)S(1)}, bf16[128,1536]{1,0:T(8,128)(2,1)S(1)}, bf16[8,96,128]{2,1,0:T(8,128)(2,1)S(1)}, bf16[8,96,128]{2,1,0:T(8,128)(2,1)S(1)}) custom-call(s32[3]{0:T(128)S(1)} %pad_add_fusion.info_ref, bf16[16,192,128]{2,1,0:T(8,128)(2,1)S(1)} %all-to-all-done.1.att_ref, ...), custom_call_target="tpu_custom_call" | custom-call | flops 8999999488 | bytes 10000000 | tf_op jit(solution)/shard_map/convolve/pallas_call | solution.py:230
  74.4 17.0 %all_to_all.35.g_ref = bf16[16,128,128]{2,1,0:T(8,128)(2,1)S(1)} all-to-all(bf16[16,128,128]{2,1,0:T(8,128)(2,1)S(1)} %get-tuple-element.22), channel_id=1, replica_groups=mesh['dp'=16,'seq'=16] {'seq'}, dimensions={0} | all-to-all | bytes 1048576 | tf_op jit(solution)/shard_map/all_to_all | solution.py:455
  91.4 10.3 %attend_back.1 = bf16[16,320,128]{2,1,0:T(8,128)(2,1)} custom-call(bf16[16,288,128]{2,1,0:T(8,128)(2,1)S(1)} %all-to-all-done.x_ref, bf16[16,128,128]{2,1,0:T(8,128)(2,1)S(1)} %all_to_all.35.g_ref, bf16[4,2048,512]{2,1,0:T(8,128)(2,1)S(1)} %copy-done.15, f32[96,2048]{1,0:T(8,128)S(1)} %copy-done.17, f32[8,2048]{1,0:T(8,128)S(1)} %copy-done.19), custom_call_target="tpu_custom_call" | custom-call | flops 20000000000 | bytes 10000000 | tf_op jit(solution)/shard_map/attend_back/pallas_call | solution.py:343
  101.7 7.4 %all-to-all-start.3 = ((bf16[16,320,128]{2,1,0:T(8,128)(2,1)}), bf16[16,320,128]{2,1,0:T(8,128)(2,1)S(1)}, u32[]{:S(2)}, u32[]{:S(2)}) async-start(bf16[16,320,128]{2,1,0:T(8,128)(2,1)} %attend_back.1), calls=%async_computation.3 | async-start | bytes 2621440 | tf_op jit(solution)/shard_map/all_to_all | solution.py:455
  109.6 1.5 collective-permute-done.2.b_ref
  111.1 0.8 outer.1
  111.9 1.4 copy-done
  113.3 13.6 %all-to-all-done.3.x_ref = bf16[16,320,128]{2,1,0:T(8,128)(2,1)S(1)} async-done(((bf16[16,320,128]{2,1,0:T(8,128)(2,1)}), bf16[16,320,128]{2,1,0:T(8,128)(2,1)S(1)}, u32[]{:S(2)}, u32[]{:S(2)}) %all-to-all-start.3) | async-done | bytes 1310752 | tf_op jit(solution)/shard_map/all_to_all | solution.py:455
  126.9 37.3 %all_to_all.36.w_ref = bf16[8,96,1536]{2,1,0:T(8,128)(2,1)S(1)} all-to-all(bf16[8,96,1536]{2,1,0:T(8,128)(2,1)} %copy-done), channel_id=1, replica_groups={{0,2,4,6,8,10,12,14},{1,3,5,7,9,11,13,15},{16,18,20,22,24,26,28,30},{17..., dimensions={0} | all-to-all | bytes 4718592 | tf_op jit(solution)/shard_map/all_to_all | solution.py:455
  164.5 22.0 %all_to_all.37.x_ref = bf16[16,96,128]{2,1,0:T(8,128)(2,1)S(1)} all-to-all(bf16[16,96,128]{2,1,0:T(8,128)(2,1)S(1)} %pack.1), channel_id=1, replica_groups=mesh['dp'=16,'seq'=16] {'dp'}, dimensions={0} | all-to-all | bytes 786432 | tf_op jit(solution)/shard_map/all_to_all | solution.py:455
  186.5 0.8 total.1
  187.3 3.6 %all-to-all-start.6 = ((bf16[16,96,128]{2,1,0:T(8,128)(2,1)}), bf16[16,96,128]{2,1,0:T(8,128)(2,1)S(1)}, u32[]{:S(2)}, u32[]{:S(2)}) async-start(bf16[16,96,128]{2,1,0:T(8,128)(2,1)} %total.1), calls=%async_computation.6 | async-start | bytes 786432 | tf_op jit(solution)/shard_map/all_to_all | solution.py:455
  190.8 1.2 post.1
  192.0 11.2 %all-to-all-done.6.x_ref = bf16[16,96,128]{2,1,0:T(8,128)(2,1)S(1)} async-done(((bf16[16,96,128]{2,1,0:T(8,128)(2,1)}), bf16[16,96,128]{2,1,0:T(8,128)(2,1)S(1)}, u32[]{:S(2)}, u32[]{:S(2)}) %all-to-all-start.6) | async-done | bytes 393248 | tf_op jit(solution)/shard_map/all_to_all | solution.py:455
  203.2 1.0 unpack.1
  (40 shorter events, 1.6 us)
Async XLA Ops:
  0.6 1.0 copy-start.1
  1.6 1.0 copy-start.2
  2.6 1.0 copy-start.3
  5.0 23.8 %all-to-all-start = ((bf16[16,288,128]{2,1,0:T(8,128)(2,1)}), bf16[16,288,128]{2,1,0:T(8,128)(2,1)S(1)}, u32[]{:S(2)}, u32[]{:S(2)}) async-start(bf16[16,288,128]{2,1,0:T(8,128)(2,1)} %pre.1), calls=%async_computation | async-start | bytes 2359296 | tf_op jit(solution)/shard_map/all_to_all | solution.py:455
  13.1 35.9 %copy-start.4 = (bf16[1,128,1536]{2,1,0:T(8,128)(2,1)S(1)}, bf16[1,128,1536]{2,1,0:T(8,128)(2,1)}, u32[]{:S(2)}) copy-start(bf16[1,128,1536]{2,1,0:T(8,128)(2,1)} %param.11) | copy-start | bytes 1179652
  13.1 35.9 %copy-start.5 = (bf16[1,128,1536]{2,1,0:T(8,128)(2,1)S(1)}, bf16[1,128,1536]{2,1,0:T(8,128)(2,1)}, u32[]{:S(2)}) copy-start(bf16[1,128,1536]{2,1,0:T(8,128)(2,1)} %param.15) | copy-start | bytes 1179652
  37.5 3.3 %copy-start.14 = (bf16[4,2048,512]{2,1,0:T(8,128)(2,1)}, bf16[4,2048,512]{2,1,0:T(8,128)(2,1)S(1)}, u32[]{:S(2)}) copy-start(bf16[4,2048,512]{2,1,0:T(8,128)(2,1)S(1)} %get-tuple-element.23.e_ref) | copy-start | bytes 25165828
  40.8 0.9 copy-start.16
  41.7 0.6 copy-start.18
  42.3 19.5 %copy-start.7 = (f32[31,1536]{1,0:T(8,128)S(1)}, f32[31,1536]{1,0:T(8,128)}, u32[]{:S(2)}) copy-start(f32[31,1536]{1,0:T(8,128)} %taps_ref.1) | copy-start | bytes 571396
  42.3 19.5 %all-to-all-start.1 = ((bf16[16,192,128]{2,1,0:T(8,128)(2,1)}), bf16[16,192,128]{2,1,0:T(8,128)(2,1)S(1)}, u32[]{:S(2)}, u32[]{:S(2)}) async-start(bf16[16,192,128]{2,1,0:T(8,128)(2,1)} %get-tuple-element.20), calls=%async_computation.1 | async-start | bytes 1572864 | tf_op jit(solution)/shard_map/all_to_all | solution.py:455
  49.7 11.3 %collective-permute-start = (bf16[64,1536]{1,0:T(8,128)(2,1)}, bf16[64,1536]{1,0:T(8,128)(2,1)S(1)}, u32[]{:S(2)}, u32[]{:S(2)}) collective-permute-start(bf16[64,1536]{1,0:T(8,128)(2,1)} %pad_maximum_fusion), channel_id=1, source_target_pairs={{0,1},{1,2},{2,3},{3,4},{4,5},{5,6},{6,7},{7,8},{8,9},{9,10},{10,1... | collective-permute-start | bytes 589832 | tf_op jit(solution)/shard_map/ppermute | solution.py:471
  51.8 9.3 %collective-permute-start.1 = (bf16[64,1536]{1,0:T(8,128)(2,1)S(1)}, bf16[64,1536]{1,0:T(8,128)(2,1)S(1)}, u32[]{:S(2)}, u32[]{:S(2)}) collective-permute-start(bf16[64,1536]{1,0:T(8,128)(2,1)S(1)} %pad_maximum_fusion.1), channel_id=1, source_target_pairs={{1,0},{2,1},{3,2},{4,3},{5,4},{6,5},{7,6},{8,7},{9,8},{10,9},{11,1... | collective-permute-start | bytes 589832 | tf_op jit(solution)/shard_map/ppermute | solution.py:472
  61.1 0.7 copy-start.8
  61.8 2.3 %copy-start.6 = (bf16[1536,1536]{1,0:T(8,128)(2,1)S(1)}, bf16[1536,1536]{1,0:T(8,128)(2,1)}, u32[]{:S(2)}) copy-start(bf16[1536,1536]{1,0:T(8,128)(2,1)} %w_ref.1) | copy-start | bytes 14155780
  64.1 0.9 copy-start.9
  65.0 26.4 %copy-start.15 = (bf16[4,2048,512]{2,1,0:T(8,128)(2,1)S(1)}, bf16[4,2048,512]{2,1,0:T(8,128)(2,1)}, u32[]{:S(2)}) copy-start(bf16[4,2048,512]{2,1,0:T(8,128)(2,1)} %copy-done.14) | copy-start | bytes 25165828
  65.0 26.4 %copy-start.17 = (f32[96,2048]{1,0:T(8,128)S(1)}, f32[96,2048]{1,0:T(8,128)}, u32[]{:S(2)}) copy-start(f32[96,2048]{1,0:T(8,128)} %copy-done.16) | copy-start | bytes 2359300
  65.0 26.4 %copy-start.19 = (f32[8,2048]{1,0:T(8,128)S(1)}, f32[8,2048]{1,0:T(8,128)}, u32[]{:S(2)}) copy-start(f32[8,2048]{1,0:T(8,128)} %copy-done.18) | copy-start | bytes 196612
  74.4 17.0 %copy-start.10 = (bf16[8,96,128]{2,1,0:T(8,128)(2,1)}, bf16[8,96,128]{2,1,0:T(8,128)(2,1)S(1)}, u32[]{:S(2)}) copy-start(bf16[8,96,128]{2,1,0:T(8,128)(2,1)S(1)} %get-tuple-element.30) | copy-start | bytes 589828
  74.4 17.0 %copy-start.12 = (bf16[8,96,128]{2,1,0:T(8,128)(2,1)}, bf16[8,96,128]{2,1,0:T(8,128)(2,1)S(1)}, u32[]{:S(2)}) copy-start(bf16[8,96,128]{2,1,0:T(8,128)(2,1)S(1)} %get-tuple-element.29.a_ref) | copy-start | bytes 589828
  101.7 7.5 %copy-start.11 = (bf16[8,96,128]{2,1,0:T(8,128)(2,1)S(1)}, bf16[8,96,128]{2,1,0:T(8,128)(2,1)}, u32[]{:S(2)}) copy-start(bf16[8,96,128]{2,1,0:T(8,128)(2,1)} %copy-done.10) | copy-start | bytes 589828
  101.7 9.4 %copy-start.13 = (bf16[8,96,128]{2,1,0:T(8,128)(2,1)S(1)}, bf16[8,96,128]{2,1,0:T(8,128)(2,1)}, u32[]{:S(2)}) copy-start(bf16[8,96,128]{2,1,0:T(8,128)(2,1)} %copy-done.12) | copy-start | bytes 589828
  101.7 25.1 %all-to-all-start.3 = ((bf16[16,320,128]{2,1,0:T(8,128)(2,1)}), bf16[16,320,128]{2,1,0:T(8,128)(2,1)S(1)}, u32[]{:S(2)}, u32[]{:S(2)}) async-start(bf16[16,320,128]{2,1,0:T(8,128)(2,1)} %attend_back.1), calls=%async_computation.3 | async-start | bytes 2621440 | tf_op jit(solution)/shard_map/all_to_all | solution.py:455
  109.1 2.0 collective-permute-start.3
  109.2 1.9 collective-permute-start.2
  111.9 1.4 copy-start
  187.3 16.0 %all-to-all-start.6 = ((bf16[16,96,128]{2,1,0:T(8,128)(2,1)}), bf16[16,96,128]{2,1,0:T(8,128)(2,1)S(1)}, u32[]{:S(2)}, u32[]{:S(2)}) async-start(bf16[16,96,128]{2,1,0:T(8,128)(2,1)} %total.1), calls=%async_computation.6 | async-start | bytes 786432 | tf_op jit(solution)/shard_map/all_to_all | solution.py:455

commit v2 on v1

--- a/solution.py
+++ b/solution.py
@@ -40,21 +40,43 @@
     return jnp.dot(a, b, preferred_element_type=F32)
 
 
-def pre_kernel(q_ref, k_ref, v_ref, o_ref):
-    for part, ref in enumerate((q_ref, k_ref, v_ref)):
-        turned = ref[...].T
+def pre_kernel(q_hbm, k_hbm, v_hbm, res_hbm, cot_hbm, o_ref, up_ref, down_ref, buf, sems):
+    rows = q_hbm.shape[0]
+    loads = [
+        pltpu.make_async_copy(ref, buf.at[i], sems.at[i])
+        for i, ref in enumerate((q_hbm, k_hbm, v_hbm))
+    ]
+    edges = [
+        pltpu.make_async_copy(ref.at[pl.ds(lo, HALO)], out.at[pl.ds(at, HALO)], sems.at[n])
+        for n, ref, lo, out, at in (
+            (3, res_hbm, rows - HALO, up_ref, 0),
+            (4, cot_hbm, rows - HALO, up_ref, HALO),
+            (5, res_hbm, 0, down_ref, 0),
+            (6, cot_hbm, 0, down_ref, HALO),
+        )
+    ]
+    for copy in loads + edges:
+        copy.start()
+    for part, copy in enumerate(loads):
+        copy.wait()
+        turned = buf[part].T
         for h in range(HEADS):
             o_ref[h, part * HEAD : (part + 1) * HEAD, :] = turned[h * HEAD : (h + 1) * HEAD, :]
-
-
-def pre(q, k, v):
+    for copy in edges:
+        copy.wait()
+
+
+def pre(q, k, v, res, cot):
+    edge = jax.ShapeDtypeStruct((2 * HALO, q.shape[1]), BF)
     return pl.pallas_call(
         pre_kernel,
-        out_shape=jax.ShapeDtypeStruct((HEADS, 3 * HEAD, LANES), BF),
-        compiler_params=params(32),
+        out_shape=(jax.ShapeDtypeStruct((HEADS, 3 * HEAD, LANES), BF), edge, edge),
+        in_specs=[pl.BlockSpec(memory_space=pltpu.HBM)] * 5,
+        scratch_shapes=[pltpu.VMEM((3,) + q.shape, BF), pltpu.SemaphoreType.DMA((7,))],
+        compiler_params=params(8),
         cost_estimate=cost(1e6, 3e6),
         name="pre",
-    )(q, k, v)
+    )(q, k, v, res, cot)
 
 
 def fwd_kernel(len_ref, x_ref, e_ref, o_ref, inv_ref, pay_ref, kaug, vaug, sbuf):
@@ -105,11 +127,17 @@
 
     @pl.when(step == pl.num_programs(0) - 1)
     def _():
-        left = lane_iota((HEAD, LANES)) < LANES // 2
+        low = HEAD // 2
+        lane = lane_iota((low, LANES))
+        left = lane < LANES // 2
+        outer_lanes = jnp.logical_or(lane < HALO, lane >= LANES - HALO)
         for j in range(blocks):
-            after = pay_ref[min(j + 1, blocks - 1), 0:HEAD, :]
-            before = pay_ref[max(j - 1, 0), 0:HEAD, :]
-            pay_ref[j, HEAD : 2 * HEAD, :] = jnp.where(left, after, before)
+            after = pay_ref[min(j + 1, blocks - 1), 0:HEAD, :].astype(F32)
+            before = pay_ref[max(j - 1, 0), 0:HEAD, :].astype(F32)
+            first = jnp.where(left, after[0:low], before[0:low])
+            second = jnp.where(left, after[low:HEAD], before[low:HEAD])
+            second = pltpu.roll(second, LANES // 2, 1)
+            pay_ref[j, HEAD : HEAD + low, :] = jnp.where(outer_lanes, first, second).astype(BF)
 
 
 def fwd(length, x):
@@ -120,10 +148,10 @@
         fwd_kernel,
         grid=(steps,),
         out_shape=(
-            jax.ShapeDtypeStruct((steps, frames, QT), BF),
-            jax.ShapeDtypeStruct((HEAD, frames), F32),
+            pltpu.HBM((steps, frames, QT), BF),
+            pltpu.HBM((HEAD, frames), F32),
             jax.ShapeDtypeStruct((8, frames), F32),
-            jax.ShapeDtypeStruct((blocks, 2 * HEAD, LANES), BF),
+            jax.ShapeDtypeStruct((blocks, HEAD + HEAD // 2, LANES), BF),
         ),
         in_specs=[
             pl.BlockSpec(memory_space=pltpu.SMEM),
@@ -133,45 +161,70 @@
             pl.BlockSpec((1, frames, QT), lambda i: (i, 0, 0)),
             pl.BlockSpec((HEAD, QT), lambda i: (0, i)),
             pl.BlockSpec((8, QT), lambda i: (0, i)),
-            pl.BlockSpec((blocks, 2 * HEAD, LANES), lambda i: (0, 0, 0)),
+            pl.BlockSpec((blocks, HEAD + HEAD // 2, LANES), lambda i: (0, 0, 0)),
         ),
         scratch_shapes=[
             pltpu.VMEM((frames, 2 * LANES), BF),
             pltpu.VMEM((HEAD + 16, frames), BF),
             pltpu.VMEM((frames, QT), F32),
         ],
-        compiler_params=params(40),
+        compiler_params=params(20),
         cost_estimate=cost(9e9, 1e7),
         name="attend",
     )(length, x)
 
 
 def conv_kernel_body(
-    info_ref, att_ref, res_ref, cot_ref, left_ref, right_ref, w_ref, taps_ref,
-    out_ref, pay_ref, bg_ref, send_ref, keep_ref,
-    lhs, block_in, masked, cot, grad, taps_sum,
+    info_ref, att_ref, res_hbm, cot_hbm, left_hbm, right_hbm, w_hbm, taps_hbm,
+    out_ref, pay_ref, keep_ref, send_ref,
+    lhs, block_in, masked, cot, grad, taps_sum, bg_ref,
+    res_ref, cot_ref, left_ref, right_ref, weight, taps_ref, sems,
 ):
-    rows = res_ref.shape[0]
-    width = res_ref.shape[1]
+    rows, width = res_ref.shape
     cols = width // LANES
     span = rows + 2 * HALO
     length = info_ref[0]
     first = info_ref[1]
-    core = info_ref[2]
-    for i in range(HEADS // 2):
-        keep_ref[i] = att_ref[2 * i + core, 0:HEAD, :]
-        send_ref[i] = att_ref[2 * i + 1 - core, 0:HEAD, :]
+    zbit = info_ref[3]
+    loads = [
+        pltpu.make_async_copy(
+            w_hbm.at[:, pl.ds(2 * n * LANES, 2 * LANES)],
+            weight.at[:, pl.ds(2 * n * LANES, 2 * LANES)],
+            sems.at[n],
+        )
+        for n in range(cols // 2)
+    ]
+    small = [
+        pltpu.make_async_copy(src, dst, sems.at[cols // 2 + n])
+        for n, (src, dst) in enumerate(
+            (
+                (res_hbm, res_ref),
+                (cot_hbm, cot_ref),
+                (left_hbm, left_ref),
+                (right_hbm, right_ref),
+                (taps_hbm, taps_ref),
+            )
+        )
+    ]
+    for load in small[0:4] + loads + small[4:]:
+        load.start()
     main = jnp.concatenate([att_ref[h, 0:HEAD, :] for h in range(HEADS)], axis=0)
-    halo = jnp.concatenate([att_ref[h, HEAD : 2 * HEAD, :] for h in range(HEADS)], axis=0)
+    packed = [att_ref[h, HEAD : HEAD + HEAD // 2, :].astype(F32) for h in range(HEADS)]
+    halo = jnp.concatenate(
+        [part for p in packed for part in (p, pltpu.roll(p, LANES // 2, 1))], axis=0
+    ).astype(BF)
     halo = halo.T
     lhs[0:HALO, :] = halo[LANES - HALO : LANES, :]
     lhs[HALO : HALO + rows, :] = main.T
     lhs[HALO + rows : span, :] = halo[0:HALO, :]
     frame = first - HALO + row_iota((span, LANES))
     valid = jnp.logical_and(frame >= 0, frame < length)
+    for load in small[0:4]:
+        load.wait()
     for n in range(cols // 2):
         wide = slice(2 * n * LANES, 2 * (n + 1) * LANES)
-        proj = dot(lhs[...], w_ref[:, wide])
+        loads[n].wait()
+        proj = dot(lhs[...], weight[:, wide])
         for m in range(2):
             c = 2 * n + m
             at = slice(c * LANES, (c + 1) * LANES)
@@ -186,6 +239,7 @@
                 axis=0,
             ).astype(F32)
     mid = rows + 32
+    small[4].wait()
 
     @pl.loop(0, cols)
     def _(c):
@@ -211,10 +265,13 @@
 
     taps_sum[HEADS - 1, pl.ds(cols, cols), :] = jnp.zeros((cols, LANES), F32)
     taps_sum[:, pl.ds(2 * cols, 8), :] = jnp.zeros((HEADS, 8, LANES), F32)
+    half = width // 2
+    keep_ref[...] = bg_ref[:, pl.ds(pl.multiple_of(zbit * half, LANES), half)]
+    send_ref[...] = bg_ref[:, pl.ds(pl.multiple_of((1 - zbit) * half, LANES), half)]
     bg = bg_ref[...]
     for h in range(0, HEADS, 2):
         mixed = lax.dot_general(
-            w_ref[h * HEAD : (h + 2) * HEAD, :], bg, (((1,), (1,)), ((), ())),
+            weight[h * HEAD : (h + 2) * HEAD, :], bg, (((1,), (1,)), ((), ())),
             preferred_element_type=F32,
         ).astype(BF)
         pay_ref[h, 0:HEAD, :] = mixed[0:HEAD]
@@ -226,18 +283,19 @@
     rows, width = res.shape
     cols = width // LANES
     span = rows + 2 * HALO
-    vm = pl.BlockSpec(memory_space=pltpu.VMEM)
+    vm = pl.BlockSpec()
     return pl.pallas_call(
         conv_kernel_body,
         out_shape=(
             jax.ShapeDtypeStruct((rows, width), BF),
-            jax.ShapeDtypeStruct((HEADS, LANES, LANES), BF),
-            jax.ShapeDtypeStruct((rows, width), BF),
-            jax.ShapeDtypeStruct((HEADS // 2, HEAD, LANES), BF),
-            jax.ShapeDtypeStruct((HEADS // 2, HEAD, LANES), BF),
+            pltpu.HBM((HEADS, LANES, LANES), BF),
+            pltpu.HBM((rows, width // 2), BF),
+            pltpu.HBM((rows, width // 2), BF),
         ),
-        in_specs=[pl.BlockSpec(memory_space=pltpu.SMEM)] + [vm] * 7,
-        out_specs=(vm,) * 5,
+        in_specs=[pl.BlockSpec(memory_space=pltpu.SMEM)]
+        + [vm]
+        + [pl.BlockSpec(memory_space=pl.ANY)] * 6,
+        out_specs=(vm,) * 4,
         scratch_shapes=[
             pltpu.VMEM((span, width), BF),
             pltpu.VMEM((cols, span, LANES), F32),
@@ -245,33 +303,58 @@
             pltpu.VMEM((cols, rows + 32, LANES), F32),
             pltpu.VMEM((rows + 32, LANES), F32),
             pltpu.VMEM((HEADS, 32, LANES), F32),
+            pltpu.VMEM((rows, width), BF),
+            pltpu.VMEM((rows, width), BF),
+            pltpu.VMEM((rows, width), BF),
+            pltpu.VMEM((2 * HALO, width), BF),
+            pltpu.VMEM((2 * HALO, width), BF),
+            pltpu.VMEM((width, width), BF),
+            pltpu.VMEM((TAPS, width), F32),
+            pltpu.SemaphoreType.DMA((cols // 2 + 5,)),
         ],
-        compiler_params=params(40),
+        compiler_params=params(20),
         cost_estimate=cost(9e9, 1e7),
         name="convolve",
     )(info, att, res, cot, left, right, w, taps)
 
 
-def outer_kernel(a_ref, b_ref, g_ref, h_ref, o_ref):
-    half = HEADS // 2
-    lhs = jnp.concatenate(
-        [a_ref[...].reshape(half * HEAD, LANES), b_ref[...].reshape(half * HEAD, LANES)], axis=1
-    )
-    width = g_ref.shape[1]
-    for n in range(width // 256):
-        at = slice(n * 256, (n + 1) * 256)
-        rhs = jnp.concatenate([g_ref[:, at], h_ref[:, at]], axis=0)
-        o_ref[:, :, at] = dot(lhs, rhs).astype(BF).reshape(half, HEAD, 256)
-
-
-def outer(a, b, g, h):
+def outer_kernel(info_ref, g_ref, *refs):
+    o_ref = refs[-1]
+    taps = jnp.sum(g_ref[:, HEAD:LANES, :].astype(F32), axis=0).astype(BF)
+    core = info_ref[2]
+    tall, wide = refs[0:4], refs[4:8]
+    part = wide[0].shape[1] // 2
+    at = pl.ds(pl.multiple_of(core * part, LANES), part)
+    rhs = jnp.concatenate([ref[:, at] for ref in wide], axis=0)
+    below = part // LANES * HEAD
+    for h in range(HEADS):
+        o_ref[h, below : below + 32, :] = taps
+    for h in range(0, HEADS, 4):
+        lhs = jnp.concatenate(
+            [
+                jnp.concatenate([ref[g, 0:HEAD, :] for ref in tall], axis=1)
+                for g in range(h, h + 4)
+            ],
+            axis=0,
+        )
+        full = dot(lhs, rhs).astype(BF)
+        for g in range(4):
+            for c in range(part // LANES):
+                o_ref[h + g, c * HEAD : (c + 1) * HEAD, :] = full[
+                    g * HEAD : (g + 1) * HEAD, c * LANES : (c + 1) * LANES
+                ]
+
+
+def outer(info, g, tall, wide):
+    part = wide[0].shape[1] // 2
     return pl.pallas_call(
         outer_kernel,
-        out_shape=jax.ShapeDtypeStruct((HEADS // 2, HEAD, g.shape[1]), BF),
-        compiler_params=params(32),
+        out_shape=jax.ShapeDtypeStruct((HEADS, part // LANES * HEAD + 32, LANES), BF),
+        in_specs=[pl.BlockSpec(memory_space=pltpu.SMEM)] + [pl.BlockSpec()] * 9,
+        compiler_params=params(20),
         cost_estimate=cost(1e9, 4e6),
         name="outer",
-    )(a, b, g, h)
+    )(info, g, *tall, *wide)
 
 
 def bwd_kernel(x_ref, g_ref, e_ref, o_ref, inv_ref, pay_ref, vaug, kt, dk, dv):
@@ -325,15 +408,10 @@
 
     @pl.when(step == pl.num_programs(0) - 1)
     def _():
-        total = jnp.zeros((32, LANES), F32)
-        for j in range(blocks):
-            total = total + g_ref[j, HEAD:LANES, :].astype(F32)
-        total = total.astype(BF)
         for j in range(blocks):
             rows = pl.ds(j * LANES, LANES)
             pay_ref[j, HEAD : 2 * HEAD, :] = dk[rows, :].T[0:HEAD].astype(BF)
             pay_ref[j, 2 * HEAD : 3 * HEAD, :] = dv[rows, :].T[0:HEAD].astype(BF)
-            pay_ref[j, 3 * HEAD : 3 * HEAD + 32, :] = total
 
 
 def bwd(x, g, e, o, inv):
@@ -343,7 +421,7 @@
     return pl.pallas_call(
         bwd_kernel,
         grid=(steps,),
-        out_shape=jax.ShapeDtypeStruct((blocks, 3 * HEAD + 32, LANES), BF),
+        out_shape=jax.ShapeDtypeStruct((blocks, 3 * HEAD, LANES), BF),
         in_specs=[
             pl.BlockSpec((blocks, 3 * HEAD, LANES), lambda i: (0, 0, 0)),
             pl.BlockSpec((blocks, LANES, LANES), lambda i: (0, 0, 0)),
@@ -351,14 +429,14 @@
             pl.BlockSpec((HEAD, QT), lambda i: (0, i)),
             pl.BlockSpec((8, QT), lambda i: (0, i)),
         ],
-        out_specs=pl.BlockSpec((blocks, 3 * HEAD + 32, LANES), lambda i: (0, 0, 0)),
+        out_specs=pl.BlockSpec((blocks, 3 * HEAD, LANES), lambda i: (0, 0, 0)),
         scratch_shapes=[
             pltpu.VMEM((frames, 2 * LANES), BF),
             pltpu.VMEM((HEAD, frames), BF),
             pltpu.VMEM((frames, LANES), F32),
             pltpu.VMEM((frames, LANES), F32),
         ],
-        compiler_params=params(40),
+        compiler_params=params(30),
         cost_estimate=cost(2e10, 1e7),
         name="attend_back",
     )(x, g, e, o, inv)
@@ -375,67 +453,80 @@
     return pl.pallas_call(
         post_kernel,
         out_shape=(shape,) * 3,
-        compiler_params=params(32),
+        compiler_params=params(12),
         cost_estimate=cost(1e6, 3e6),
         name="post",
     )(x)
 
 
-def pack_kernel(w_ref, x_ref, o_ref):
-    width = w_ref.shape[2]
-    cols = width // LANES
-    share = (HEAD // 8) * cols // HEADS
-    for d in range(HEADS):
-        parts = []
-        for n in range(d * share, (d + 1) * share):
-            r, c = 8 * (n // cols), LANES * (n % cols)
-            parts.append(
-                jnp.sum(w_ref[:, r : r + 8, c : c + LANES].astype(F32), axis=0)
-            )
-        parts.append(x_ref[d, 3 * HEAD : 3 * HEAD + 24, :].astype(F32))
-        o_ref[d] = jnp.concatenate(parts, axis=0).astype(BF)
-
-
-def pack(w, x):
+GROUP = 8
+
+
+def pack_kernel(x_ref, o_ref, buf):
+    cols = x_ref.shape[1] // HEAD
+    below = cols * HEAD
+    for r in range(HEAD // 16):
+        for c in range(2 * cols):
+            at = (c % cols) * HEAD + 16 * r
+            tiles = [x_ref[2 * i + c // cols, at : at + 16, :].astype(F32) for i in range(HEADS // 2)]
+            both = sum(tiles[1:], tiles[0])
+            for e in range(2):
+                n = (2 * r + e) * 2 * cols + c
+                buf[8 * n : 8 * n + 8, :] = both[8 * e : 8 * e + 8, :]
+    share = buf.shape[0] // GROUP
+    for j in range(GROUP):
+        taps = [x_ref[2 * j + e, below : below + 32, :].astype(F32)[0:24] for e in range(2)]
+        rest = jnp.zeros((o_ref.shape[1] - share - 48, LANES), F32)
+        o_ref[j] = jnp.concatenate(
+            [buf[share * j : share * (j + 1), :]] + taps + [rest], axis=0
+        ).astype(BF)
+
+
+def pack(x):
+    units = x.shape[1] // HEAD * HEAD * 2
     return pl.pallas_call(
         pack_kernel,
-        out_shape=jax.ShapeDtypeStruct((HEADS, HEAD, LANES), BF),
-        compiler_params=params(32),
+        out_shape=jax.ShapeDtypeStruct((GROUP, LANES, LANES), BF),
+        scratch_shapes=[pltpu.VMEM((units, LANES), F32)],
+        compiler_params=params(12),
         cost_estimate=cost(1e6, 3e6),
         name="pack",
-    )(w, x)
+    )(x)
 
 
 def total_kernel(x_ref, o_ref):
-    total = jnp.sum(x_ref[...].astype(F32), axis=0) * (1.0 / x_ref.shape[0])
+    total = jnp.sum(x_ref[...].astype(F32), axis=0) * (1.0 / o_ref.shape[0])
     o_ref[...] = jnp.broadcast_to(total.astype(BF)[None], o_ref.shape)
 
 
-def total(x):
+def total(x, batch):
     return pl.pallas_call(
         total_kernel,
-        out_shape=jax.ShapeDtypeStruct(x.shape, BF),
-        compiler_params=params(32),
+        out_shape=jax.ShapeDtypeStruct((batch,) + x.shape[1:], BF),
+        compiler_params=params(12),
         cost_estimate=cost(1e6, 1e6),
         name="total",
     )(x)
 
 
 def unpack_kernel(x_ref, w_ref, k_ref):
-    cols = w_ref.shape[1] // LANES
-    share = (HEAD // 8) * cols // HEADS
-    for d in range(HEADS):
-        x = x_ref[d].astype(F32)
-        for i in range(share):
-            n = d * share + i
-            r, c = 8 * (n // cols), LANES * (n % cols)
-            w_ref[r : r + 8, c : c + LANES] = x[8 * i : 8 * i + 8, :]
-        for i in range(2):
-            if 2 * d + i < TAPS:
+    width = w_ref.shape[1]
+    cols = width // LANES
+    share = HEAD // 8 * cols // 2 // GROUP
+    for z in range(2):
+        for j in range(GROUP):
+            x = x_ref[4 * (j // 2) + 2 * z + j % 2].astype(F32)
+            for i in range(share):
+                n = j * share + i
+                r, c = 8 * (n // (cols // 2)), width // 2 * z + LANES * (n % (cols // 2))
+                w_ref[r : r + 8, c : c + LANES] = x[8 * i : 8 * i + 8, :]
+    for j in range(GROUP):
+        x = x_ref[4 * (j // 2) + j % 2].astype(F32) + x_ref[4 * (j // 2) + 2 + j % 2].astype(F32)
+        for i in range(4):
+            if 4 * j + i < TAPS:
                 for c in range(cols):
-                    k_ref[2 * d + i : 2 * d + i + 1, c * LANES : (c + 1) * LANES] = x[
-                        8 * share + cols * i + c : 8 * share + cols * i + c + 1, :
-                    ]
+                    at = 8 * share + cols * i + c
+                    k_ref[4 * j + i : 4 * j + i + 1, c * LANES : (c + 1) * LANES] = x[at : at + 1, :]
 
 
 def unpack(x, width):
@@ -445,10 +536,14 @@
             jax.ShapeDtypeStruct((HEAD, width), F32),
             jax.ShapeDtypeStruct((TAPS, width), F32),
         ),
-        compiler_params=params(32),
+        compiler_params=params(12),
         cost_estimate=cost(1e6, 1e6),
         name="unpack",
     )(x)
+
+
+def in_hbm(x):
+    return pltpu.with_memory_space_constraint(x, pltpu.HBM)
 
 
 def exchange(x, axis, groups=None):
@@ -464,28 +559,44 @@
     res, cot = residual[0], cotangent[0]
     up = [(i, i + 1) for i in range(count - 1)]
     down = [(i + 1, i) for i in range(count - 1)]
-    pairs = [(i, i ^ 1) for i in range(count)]
-    same_core = [list(range(c, count, 2)) for c in range(2)]
-
-    heads = exchange(pre(query_proj[0], key_proj[0], value_proj[0]), "seq")
-    left = lax.ppermute(jnp.concatenate([res[-HALO:], cot[-HALO:]], axis=0), "seq", up)
-    right = lax.ppermute(jnp.concatenate([res[:HALO], cot[:HALO]], axis=0), "seq", down)
+    cores = [(i, i ^ 1) for i in range(count)]
+    batch = lax.axis_size("dp")
+    depth = lax.axis_index("dp")
+    levels = [(i, i ^ 2) for i in range(batch)]
+    same_level = [[i for i in range(batch) if (i // 2) % 2 == z] for z in range(2)]
+    query, key, value, res, cot, out_weight, conv_kernel = (
+        in_hbm(x)
+        for x in (query_proj[0], key_proj[0], value_proj[0], res, cot, out_weight, conv_kernel)
+    )
+    payload, edge_up, edge_down = pre(query, key, value, res, cot)
+    heads = exchange(payload, "seq")
+    left = lax.ppermute(edge_up, "seq", up)
+    right = lax.ppermute(edge_down, "seq", down)
+    heads, left, right = lax.optimization_barrier((heads, left, right))
     weights, mixed, inv, payload = fwd(lengths, heads)
     attended = exchange(payload, "seq")
-    info = jnp.stack([lengths[0], me * rows, me % 2]).astype(jnp.int32)
-    block_out, payload, block_grad, send, keep = conv(
-        info, attended, res, cot, left, right, out_weight, conv_kernel
+    att_level = lax.ppermute(attended, "dp", levels)
+    att_core = lax.ppermute(attended, "seq", cores)
+    info = jnp.stack([lengths[0], me * rows, me % 2, depth // 2 % 2]).astype(jnp.int32)
+    block_out, payload, keep, send = conv(
+        info, attended, res, cot, in_hbm(left), in_hbm(right), out_weight, conv_kernel
     )
+    att_level, payload = lax.optimization_barrier((att_level, payload))
+    att_both = lax.ppermute(att_level, "seq", cores)
     grads = exchange(payload, "seq")
-    partner_att = lax.ppermute(send, "seq", pairs)
-    partner_grad = lax.ppermute(block_grad, "seq", pairs)
-    partial = outer(keep, partner_att, block_grad, partner_grad)
-    partial = exchange(partial, "seq", same_core)
-    payload = bwd(heads, grads, weights, mixed, inv)
+    level = lax.ppermute(send, "dp", levels)
+    partner = lax.ppermute(keep, "seq", cores)
+    both = lax.ppermute(level, "seq", cores)
+    partial = outer(
+        info, grads, (attended, att_core, att_level, att_both), (keep, partner, level, both)
+    )
+    partial = exchange(partial, "seq")
+    payload = bwd(heads, grads, in_hbm(weights), in_hbm(mixed), inv)
+    payload, partial = lax.optimization_barrier((payload, partial))
     back = exchange(payload, "seq")
     query_grad, key_grad, value_grad = post(back)
-    packed = exchange(pack(partial, back), "dp")
-    final = exchange(total(packed), "dp")
+    packed = exchange(pack(partial), "dp", same_level)
+    final = exchange(total(packed, batch), "dp")
     weight_grad, kernel_grad = unpack(final, width)
     return (
         block_out[None],

time: 205 us -> 182 us (0.89)
  blocking collectives: 76.3 us -> 18.7 us
  waiting for transfers between devices: 47.6 us -> 66.8 us
  starting transfers between devices: 31.1 us -> 47.5 us
  local copies, waits for them, and re-layouts: 13.2 us -> 2.53 us
  Pallas kernels: 33.8 us -> 43.6 us
    all_to_all x3 -> x1, blocking collectives: 76.3 us -> 18.7 us  [exchange(): lax.all_to_all(x, axis, split_axis=0, concat_axis=0, tiled=True, axis_ind...]
    all_to_all x4 -> x6, starting transfers between devices: 25.1 us -> 38.4 us  [exchange(): lax.all_to_all(x, axis, split_axis=0, concat_axis=0, tiled=True, axis_ind...]
    ppermute x4 -> x8, waiting for transfers between devices: 7.16 us -> 19.1 us  [the longest x1 11.2 us: shards(): left = lax.ppermute(edge_up, 'seq', up)]
    unnamed x40 -> x10, local copies, waits for them, and re-layouts: 13.2 us -> 2.53 us
    all_to_all x4 -> x6, waiting for transfers between devices: 40.5 us -> 47.6 us  [exchange(): lax.all_to_all(x, axis, split_axis=0, concat_axis=0, tiled=True, axis_ind...]
    pallas_call x5, Pallas kernels: 12 us -> 16.3 us  [the longest x1 9.4 us: fwd(): pl.pallas_call(fwd_kernel, grid=(steps,), out_shape=(pltpu.HBM((steps, fr...]
    pallas_call x1, Pallas kernels: 9.35 us -> 13.4 us  [conv(): pl.pallas_call(conv_kernel_body, out_shape=(jax.ShapeDtypeStruct((rows, w...]
    ppermute x4 -> x8, starting transfers between devices: 6.06 us -> 9.08 us  [the longest x1 3.51 us: shards(): right = lax.ppermute(edge_down, 'seq', down)]
  transfers between devices with their start and end apart: 8 -> 14, of which waited for: 5 -> 7; matrix products, arithmetic and copies ran while one was open for 0% -> 0% of each run, Pallas kernels for 1% -> 15%
where the time goes in v2:
time: 182 us; the launch traced here: 180 us
  waiting for transfers between devices  66.8 us (37%)
  starting transfers between devices  47.5 us (26%)
  Pallas kernels  43.6 us (24%)
  blocking collectives  18.7 us (10%)
  local copies, waits for them, and re-layouts  2.53 us (1%)
    all_to_all x6, waiting for transfers between devices, exchange(): lax.all_to_all(x, axis, split_axis=0, concat_axis=0, tiled=True, axis_ind...  47.6 us
    all_to_all x6, starting transfers between devices, exchange(): lax.all_to_all(x, axis, split_axis=0, concat_axis=0, tiled=True, axis_ind...  38.4 us
    all_to_all x1, blocking collectives, exchange(): lax.all_to_all(x, axis, split_axis=0, concat_axis=0, tiled=True, axis_ind...  18.7 us
    pallas_call x1, Pallas kernels, conv(): pl.pallas_call(conv_kernel_body, out_shape=(jax.ShapeDtypeStruct((rows, w...  13.4 us
    pallas_call x1, Pallas kernels, bwd(): pl.pallas_call(bwd_kernel, grid=(steps,), out_shape=jax.ShapeDtypeStruct(...  11.8 us
    ppermute x1, waiting for transfers between devices, shards(): left = lax.ppermute(edge_up, 'seq', up)  11.2 us
    pallas_call x1, Pallas kernels, fwd(): pl.pallas_call(fwd_kernel, grid=(steps,), out_shape=(pltpu.HBM((steps, fr...  9.4 us
    ppermute x1, waiting for transfers between devices, shards(): level = lax.ppermute(send, 'dp', levels)  6.47 us
  transfers between devices with their start and end apart: 14, of which 7 were waited for; matrix products, arithmetic and copies ran while one was open for 0% of the time, Pallas kernels for 15%

profile of v2, /device:TPU:2, one launch (start us, length us, event | category | flops | bytes accessed | tf_op | source)
XLA Modules:
  0.0 180.5 jit_solution(6074376823576446962)
XLA Ops:
  0.6 2.6 %pre.1 = (bf16[16,288,128]{2,1,0:T(8,128)(2,1)}, bf16[64,1536]{1,0:T(8,128)(2,1)S(1)}, bf16[64,1536]{1,0:T(8,128)(2,1)S(1)}) custom-call(bf16[128,1536]{1,0:T(8,128)(2,1)} %bitcast.12, bf16[128,1536]{1,0:T(8,128)(2,1)} %bitcast.13, bf16[128,1536]{1,0:T(8,128)(2,1)} %bitcast.14, bf16[128,1536]{1,0:T(8,128)(2,1)} %bitcast.15, bf16[128,1536]{1,0:T(8,128)(2,1)} %bitcast.17), custom_call_target="tpu_custom_call" | custom-call | flops 1000000 | bytes 3000000 | tf_op jit(solution)/shard_map/pre/pallas_call | solution.py:71
  3.2 7.5 %all-to-all-start = ((bf16[16,288,128]{2,1,0:T(8,128)(2,1)}), bf16[16,288,128]{2,1,0:T(8,128)(2,1)S(1)}, u32[]{:S(2)}, u32[]{:S(2)}) async-start(bf16[16,288,128]{2,1,0:T(8,128)(2,1)} %get-tuple-element.29), calls=%async_computation | async-start | bytes 2359296 | tf_op jit(solution)/shard_map/all_to_all | solution.py:550
  10.7 2.0 %collective-permute-start = (bf16[64,1536]{1,0:T(8,128)(2,1)S(1)}, bf16[64,1536]{1,0:T(8,128)(2,1)S(1)}, u32[]{:S(2)}, u32[]{:S(2)}) collective-permute-start(bf16[64,1536]{1,0:T(8,128)(2,1)S(1)} %get-tuple-element.30), channel_id=1, source_target_pairs={{0,1},{1,2},{2,3},{3,4},{4,5},{5,6},{6,7},{7,8},{8,9},{9,10},{10,1... | collective-permute-start | bytes 589832 | tf_op jit(solution)/shard_map/ppermute | solution.py:573
  12.7 3.5 %collective-permute-start.1 = (bf16[64,1536]{1,0:T(8,128)(2,1)S(1)}, bf16[64,1536]{1,0:T(8,128)(2,1)S(1)}, u32[]{:S(2)}, u32[]{:S(2)}) collective-permute-start(bf16[64,1536]{1,0:T(8,128)(2,1)S(1)} %get-tuple-element.31), channel_id=1, source_target_pairs={{1,0},{2,1},{3,2},{4,3},{5,4},{6,5},{7,6},{8,7},{9,8},{10,9},{11,1... | collective-permute-start | bytes 589832 | tf_op jit(solution)/shard_map/ppermute | solution.py:574
  16.9 11.2 %collective-permute-done.left_hbm = bf16[64,1536]{1,0:T(8,128)(2,1)S(1)} collective-permute-done((bf16[64,1536]{1,0:T(8,128)(2,1)S(1)}, bf16[64,1536]{1,0:T(8,128)(2,1)S(1)}, u32[]{:S(2)}, u32[]{:S(2)}) %collective-permute-start) | collective-permute-done | bytes 196640 | tf_op jit(solution)/shard_map/ppermute | solution.py:573
  28.1 9.4 %attend.1 = (bf16[4,2048,512]{2,1,0:T(8,128)(2,1)}, f32[96,2048]{1,0:T(8,128)}, f32[8,2048]{1,0:T(8,128)S(1)}, bf16[16,144,128]{2,1,0:T(8,128)(2,1)}) custom-call(s32[1]{0:T(128)S(6)} %copy.14.len_ref, bf16[16,288,128]{2,1,0:T(8,128)(2,1)S(1)} %all-to-all-done.x_ref), custom_call_target="tpu_custom_call" | custom-call | flops 8999999488 | bytes 10000000 | tf_op jit(solution)/shard_map/attend/pallas_call | solution.py:147
  37.5 6.4 %all-to-all-start.1 = ((bf16[16,144,128]{2,1,0:T(8,128)(2,1)}), bf16[16,144,128]{2,1,0:T(8,128)(2,1)S(1)}, u32[]{:S(2)}, u32[]{:S(2)}) async-start(bf16[16,144,128]{2,1,0:T(8,128)(2,1)} %get-tuple-element.33), calls=%async_computation.1 | async-start | bytes 1179648 | tf_op jit(solution)/shard_map/all_to_all | solution.py:550
  44.1 9.1 %all-to-all-done.1.att_ref.refs_0_ = bf16[16,144,128]{2,1,0:T(8,128)(2,1)S(1)} async-done(((bf16[16,144,128]{2,1,0:T(8,128)(2,1)}), bf16[16,144,128]{2,1,0:T(8,128)(2,1)S(1)}, u32[]{:S(2)}, u32[]{:S(2)}) %all-to-all-start.1) | async-done | bytes 589856 | tf_op jit(solution)/shard_map/all_to_all | solution.py:550
  53.2 1.9 %collective-permute-start.2 = (bf16[16,144,128]{2,1,0:T(8,128)(2,1)S(1)}, bf16[16,144,128]{2,1,0:T(8,128)(2,1)S(1)}, u32[]{:S(2)}, u32[]{:S(2)}) collective-permute-start(bf16[16,144,128]{2,1,0:T(8,128)(2,1)S(1)} %all-to-all-done.1.att_ref.refs_0_), channel_id=1, source_target_pairs={{0,32},{16,48},{32,0},{48,16},{64,96},{80,112},{96,64},{112,80},{1... | collective-permute-start | bytes 1769480 | tf_op jit(solution)/shard_map/ppermute | solution.py:578
  55.1 0.8 collective-permute-start.3
  55.9 13.4 %convolve.1 = (bf16[128,1536]{1,0:T(8,128)(2,1)}, bf16[16,128,128]{2,1,0:T(8,128)(2,1)}, bf16[128,768]{1,0:T(8,128)(2,1)}, bf16[128,768]{1,0:T(8,128)(2,1)}) custom-call(s32[4]{0:T(128)S(1)} %pad_add_fusion.info_ref, bf16[16,144,128]{2,1,0:T(8,128)(2,1)S(1)} %all-to-all-done.1.att_ref.refs_0_, bf16[128,1536]{1,0:T(8,128)(2,1)} %bitcast.16, ...), custom_call_target="tpu_custom_call" | custom-call | flops 8999999488 | bytes 10000000 | tf_op jit(solution)/shard_map/convolve/pallas_call | solution.py:287
  69.4 0.1 collective-permute-start.4
  69.5 7.0 %all-to-all-start.2 = ((bf16[16,128,128]{2,1,0:T(8,128)(2,1)}), bf16[16,128,128]{2,1,0:T(8,128)(2,1)S(1)}, u32[]{:S(2)}, u32[]{:S(2)}) async-start(bf16[16,128,128]{2,1,0:T(8,128)(2,1)} %get-tuple-element.38), calls=%async_computation.2 | async-start | bytes 1048576 | tf_op jit(solution)/shard_map/all_to_all | solution.py:550
  76.5 0.7 collective-permute-start.6
  77.2 6.5 %collective-permute-done.6.refs_6_ = bf16[128,768]{1,0:T(8,128)(2,1)S(1)} collective-permute-done((bf16[128,768]{1,0:T(8,128)(2,1)}, bf16[128,768]{1,0:T(8,128)(2,1)S(1)}, u32[]{:S(2)}, u32[]{:S(2)}) %collective-permute-start.6) | collective-permute-done | bytes 196640 | tf_op jit(solution)/shard_map/ppermute | solution.py:587
  83.6 1.4 collective-permute-done.7.refs_7_
  85.1 0.7 copy-done.1
  85.8 0.9 copy-done
  86.7 0.9 copy-done.2
  87.6 3.4 %outer.1 = bf16[16,320,128]{2,1,0:T(8,128)(2,1)} custom-call(s32[4]{0:T(128)S(1)} %pad_add_fusion.info_ref, bf16[16,128,128]{2,1,0:T(8,128)(2,1)S(1)} %all-to-all-done.2.g_ref, bf16[16,144,128]{2,1,0:T(8,128)(2,1)S(1)} %all-to-all-done.1.att_ref.refs_0_, bf16[16,144,128]{2,1,0:T(8,128)(2,1)} %collective-permute-done.3.refs_1_, ...), custom_call_target="tpu_custom_call" | custom-call | flops 1000000000 | bytes 4000000 | tf_op jit(solution)/shard_map/outer/pallas_call | solution.py:350
  91.0 7.3 %all-to-all-start.3 = ((bf16[16,320,128]{2,1,0:T(8,128)(2,1)}), bf16[16,320,128]{2,1,0:T(8,128)(2,1)S(1)}, u32[]{:S(2)}, u32[]{:S(2)}) async-start(bf16[16,320,128]{2,1,0:T(8,128)(2,1)} %outer.1), calls=%async_computation.3 | async-start | bytes 2621440 | tf_op jit(solution)/shard_map/all_to_all | solution.py:550
  98.3 11.8 %attend_back.1 = bf16[16,288,128]{2,1,0:T(8,128)(2,1)} custom-call(bf16[16,288,128]{2,1,0:T(8,128)(2,1)S(1)} %all-to-all-done.x_ref, bf16[16,128,128]{2,1,0:T(8,128)(2,1)S(1)} %all-to-all-done.2.g_ref, bf16[4,2048,512]{2,1,0:T(8,128)(2,1)} %get-tuple-element.39.e_ref, f32[96,2048]{1,0:T(8,128)} %get-tuple-element.40.o_ref, ...), custom_call_target="tpu_custom_call" | custom-call | flops 20000000000 | bytes 10000000 | tf_op jit(solution)/shard_map/attend_back/pallas_call | solution.py:421
  110.0 6.0 %all-to-all-done.3.x_ref = bf16[16,320,128]{2,1,0:T(8,128)(2,1)S(1)} async-done(((bf16[16,320,128]{2,1,0:T(8,128)(2,1)}), bf16[16,320,128]{2,1,0:T(8,128)(2,1)S(1)}, u32[]{:S(2)}, u32[]{:S(2)}) %all-to-all-start.3) | async-done | bytes 1310752 | tf_op jit(solution)/shard_map/all_to_all | solution.py:550
  116.0 0.2 pack.1
  116.2 18.7 %all_to_all.35.x_ref = bf16[8,128,128]{2,1,0:T(8,128)(2,1)S(1)} all-to-all(bf16[8,128,128]{2,1,0:T(8,128)(2,1)S(1)} %pack.1), channel_id=1, replica_groups={{0,16,64,80,128,144,192,208},{32,48,96,112,160,176,224,240},{1,17,65,81..., dimensions={0} | all-to-all | bytes 524288 | tf_op jit(solution)/shard_map/all_to_all | solution.py:550
  134.8 6.4 %all-to-all-start.4 = ((bf16[16,288,128]{2,1,0:T(8,128)(2,1)}), bf16[16,288,128]{2,1,0:T(8,128)(2,1)S(1)}, u32[]{:S(2)}, u32[]{:S(2)}) async-start(bf16[16,288,128]{2,1,0:T(8,128)(2,1)} %attend_back.1), calls=%async_computation.4 | async-start | bytes 2359296 | tf_op jit(solution)/shard_map/all_to_all | solution.py:550
  141.3 0.9 total.1
  142.1 15.5 %all-to-all-done.4.x_ref = bf16[16,288,128]{2,1,0:T(8,128)(2,1)S(1)} async-done(((bf16[16,288,128]{2,1,0:T(8,128)(2,1)}), bf16[16,288,128]{2,1,0:T(8,128)(2,1)S(1)}, u32[]{:S(2)}, u32[]{:S(2)}) %all-to-all-start.4) | async-done | bytes 1179680 | tf_op jit(solution)/shard_map/all_to_all | solution.py:550
  157.6 3.8 %all-to-all-start.6 = ((bf16[16,128,128]{2,1,0:T(8,128)(2,1)}), bf16[16,128,128]{2,1,0:T(8,128)(2,1)S(1)}, u32[]{:S(2)}, u32[]{:S(2)}) async-start(bf16[16,128,128]{2,1,0:T(8,128)(2,1)} %total.1), calls=%async_computation.6 | async-start | bytes 1048576 | tf_op jit(solution)/shard_map/all_to_all | solution.py:550
  161.4 1.2 post.1
  162.5 17.0 %all-to-all-done.6.x_ref = bf16[16,128,128]{2,1,0:T(8,128)(2,1)S(1)} async-done(((bf16[16,128,128]{2,1,0:T(8,128)(2,1)}), bf16[16,128,128]{2,1,0:T(8,128)(2,1)S(1)}, u32[]{:S(2)}, u32[]{:S(2)}) %all-to-all-start.6) | async-done | bytes 524320 | tf_op jit(solution)/shard_map/all_to_all | solution.py:550
  179.6 0.9 unpack.1
  (17 shorter events, 0.1 us)
Async XLA Ops:
  3.2 24.9 %all-to-all-start = ((bf16[16,288,128]{2,1,0:T(8,128)(2,1)}), bf16[16,288,128]{2,1,0:T(8,128)(2,1)S(1)}, u32[]{:S(2)}, u32[]{:S(2)}) async-start(bf16[16,288,128]{2,1,0:T(8,128)(2,1)} %get-tuple-element.29), calls=%async_computation | async-start | bytes 2359296 | tf_op jit(solution)/shard_map/all_to_all | solution.py:550
  10.7 17.4 %collective-permute-start = (bf16[64,1536]{1,0:T(8,128)(2,1)S(1)}, bf16[64,1536]{1,0:T(8,128)(2,1)S(1)}, u32[]{:S(2)}, u32[]{:S(2)}) collective-permute-start(bf16[64,1536]{1,0:T(8,128)(2,1)S(1)} %get-tuple-element.30), channel_id=1, source_target_pairs={{0,1},{1,2},{2,3},{3,4},{4,5},{5,6},{6,7},{7,8},{8,9},{9,10},{10,1... | collective-permute-start | bytes 589832 | tf_op jit(solution)/shard_map/ppermute | solution.py:573
  12.7 15.4 %collective-permute-start.1 = (bf16[64,1536]{1,0:T(8,128)(2,1)S(1)}, bf16[64,1536]{1,0:T(8,128)(2,1)S(1)}, u32[]{:S(2)}, u32[]{:S(2)}) collective-permute-start(bf16[64,1536]{1,0:T(8,128)(2,1)S(1)} %get-tuple-element.31), channel_id=1, source_target_pairs={{1,0},{2,1},{3,2},{4,3},{5,4},{6,5},{7,6},{8,7},{9,8},{10,9},{11,1... | collective-permute-start | bytes 589832 | tf_op jit(solution)/shard_map/ppermute | solution.py:574
  28.1 9.4 %copy-start.3 = (bf16[64,1536]{1,0:T(8,128)(2,1)}, bf16[64,1536]{1,0:T(8,128)(2,1)S(1)}, u32[]{:S(2)}) copy-start(bf16[64,1536]{1,0:T(8,128)(2,1)S(1)} %collective-permute-done.left_hbm) | copy-start | bytes 589828
  28.1 9.4 %copy-start.4 = (bf16[64,1536]{1,0:T(8,128)(2,1)}, bf16[64,1536]{1,0:T(8,128)(2,1)S(1)}, u32[]{:S(2)}) copy-start(bf16[64,1536]{1,0:T(8,128)(2,1)S(1)} %collective-permute-done.1.right_hbm) | copy-start | bytes 589828
  37.5 15.7 %all-to-all-start.1 = ((bf16[16,144,128]{2,1,0:T(8,128)(2,1)}), bf16[16,144,128]{2,1,0:T(8,128)(2,1)S(1)}, u32[]{:S(2)}, u32[]{:S(2)}) async-start(bf16[16,144,128]{2,1,0:T(8,128)(2,1)} %get-tuple-element.33), calls=%async_computation.1 | async-start | bytes 1179648 | tf_op jit(solution)/shard_map/all_to_all | solution.py:550
  53.2 16.2 %collective-permute-start.2 = (bf16[16,144,128]{2,1,0:T(8,128)(2,1)S(1)}, bf16[16,144,128]{2,1,0:T(8,128)(2,1)S(1)}, u32[]{:S(2)}, u32[]{:S(2)}) collective-permute-start(bf16[16,144,128]{2,1,0:T(8,128)(2,1)S(1)} %all-to-all-done.1.att_ref.refs_0_), channel_id=1, source_target_pairs={{0,32},{16,48},{32,0},{48,16},{64,96},{80,112},{96,64},{112,80},{1... | collective-permute-start | bytes 1769480 | tf_op jit(solution)/shard_map/ppermute | solution.py:578
  55.1 30.6 %collective-permute-start.3 = (bf16[16,144,128]{2,1,0:T(8,128)(2,1)S(1)}, bf16[16,144,128]{2,1,0:T(8,128)(2,1)}, u32[]{:S(2)}, u32[]{:S(2)}) collective-permute-start(bf16[16,144,128]{2,1,0:T(8,128)(2,1)S(1)} %all-to-all-done.1.att_ref.refs_0_), channel_id=1, source_target_pairs={{0,1},{1,0},{2,3},{3,2},{4,5},{5,4},{6,7},{7,6},{8,9},{9,8},{10,11... | collective-permute-start | bytes 1769480 | tf_op jit(solution)/shard_map/ppermute | solution.py:579
  69.4 16.4 %collective-permute-start.4 = (bf16[16,144,128]{2,1,0:T(8,128)(2,1)S(1)}, bf16[16,144,128]{2,1,0:T(8,128)(2,1)}, u32[]{:S(2)}, u32[]{:S(2)}) collective-permute-start(bf16[16,144,128]{2,1,0:T(8,128)(2,1)S(1)} %collective-permute-done.2.refs_2_), channel_id=1, source_target_pairs={{0,1},{1,0},{2,3},{3,2},{4,5},{5,4},{6,7},{7,6},{8,9},{9,8},{10,11... | collective-permute-start | bytes 1769480 | tf_op jit(solution)/shard_map/ppermute | solution.py:585
  69.5 16.3 %all-to-all-start.2 = ((bf16[16,128,128]{2,1,0:T(8,128)(2,1)}), bf16[16,128,128]{2,1,0:T(8,128)(2,1)S(1)}, u32[]{:S(2)}, u32[]{:S(2)}) async-start(bf16[16,128,128]{2,1,0:T(8,128)(2,1)} %get-tuple-element.38), calls=%async_computation.2 | async-start | bytes 1048576 | tf_op jit(solution)/shard_map/all_to_all | solution.py:550
  76.5 7.2 %collective-permute-start.6 = (bf16[128,768]{1,0:T(8,128)(2,1)}, bf16[128,768]{1,0:T(8,128)(2,1)S(1)}, u32[]{:S(2)}, u32[]{:S(2)}) collective-permute-start(bf16[128,768]{1,0:T(8,128)(2,1)} %get-tuple-element.44), channel_id=1, source_target_pairs={{0,32},{16,48},{32,0},{48,16},{64,96},{80,112},{96,64},{112,80},{1... | collective-permute-start | bytes 589832 | tf_op jit(solution)/shard_map/ppermute | solution.py:587
  77.2 6.5 %collective-permute-start.5 = (bf16[128,768]{1,0:T(8,128)(2,1)}, bf16[128,768]{1,0:T(8,128)(2,1)S(1)}, u32[]{:S(2)}, u32[]{:S(2)}) collective-permute-start(bf16[128,768]{1,0:T(8,128)(2,1)} %get-tuple-element.43.refs_4_), channel_id=1, source_target_pairs={{0,1},{1,0},{2,3},{3,2},{4,5},{5,4},{6,7},{7,6},{8,9},{9,8},{10,11... | collective-permute-start | bytes 589832 | tf_op jit(solution)/shard_map/ppermute | solution.py:588
  83.6 1.4 collective-permute-start.7
  85.1 0.7 copy-start.1
  85.8 0.9 copy-start
  86.7 0.9 copy-start.2
  91.0 25.0 %all-to-all-start.3 = ((bf16[16,320,128]{2,1,0:T(8,128)(2,1)}), bf16[16,320,128]{2,1,0:T(8,128)(2,1)S(1)}, u32[]{:S(2)}, u32[]{:S(2)}) async-start(bf16[16,320,128]{2,1,0:T(8,128)(2,1)} %outer.1), calls=%async_computation.3 | async-start | bytes 2621440 | tf_op jit(solution)/shard_map/all_to_all | solution.py:550
  134.8 22.8 %all-to-all-start.4 = ((bf16[16,288,128]{2,1,0:T(8,128)(2,1)}), bf16[16,288,128]{2,1,0:T(8,128)(2,1)S(1)}, u32[]{:S(2)}, u32[]{:S(2)}) async-start(bf16[16,288,128]{2,1,0:T(8,128)(2,1)} %attend_back.1), calls=%async_computation.4 | async-start | bytes 2359296 | tf_op jit(solution)/shard_map/all_to_all | solution.py:550
  157.6 22.0 %all-to-all-start.6 = ((bf16[16,128,128]{2,1,0:T(8,128)(2,1)}), bf16[16,128,128]{2,1,0:T(8,128)(2,1)S(1)}, u32[]{:S(2)}, u32[]{:S(2)}) async-start(bf16[16,128,128]{2,1,0:T(8,128)(2,1)} %total.1), calls=%async_computation.6 | async-start | bytes 1048576 | tf_op jit(solution)/shard_map/all_to_all | solution.py:550

commit v3 on v2

--- a/solution.py
+++ b/solution.py
@@ -178,7 +178,7 @@
     info_ref, att_ref, res_hbm, cot_hbm, left_hbm, right_hbm, w_hbm, taps_hbm,
     out_ref, pay_ref, keep_ref, send_ref,
     lhs, block_in, masked, cot, grad, taps_sum, bg_ref,
-    res_ref, cot_ref, left_ref, right_ref, weight, taps_ref, sems,
+    res_ref, cot_ref, left_ref, right_ref, weight, taps_ref, proj, sems,
 ):
     rows, width = res_ref.shape
     cols = width // LANES
@@ -186,16 +186,15 @@
     length = info_ref[0]
     first = info_ref[1]
     zbit = info_ref[3]
-    loads = [
-        pltpu.make_async_copy(
-            w_hbm.at[:, pl.ds(2 * n * LANES, 2 * LANES)],
-            weight.at[:, pl.ds(2 * n * LANES, 2 * LANES)],
-            sems.at[n],
-        )
-        for n in range(cols // 2)
-    ]
+    pieces = cols // 2
+    wide = 2 * LANES
+
+    def chunk(n):
+        at = pl.ds(pl.multiple_of(n * wide, wide), wide)
+        return pltpu.make_async_copy(w_hbm.at[:, at], weight.at[:, at], sems.at[n])
+
     small = [
-        pltpu.make_async_copy(src, dst, sems.at[cols // 2 + n])
+        pltpu.make_async_copy(src, dst, sems.at[pieces + n])
         for n, (src, dst) in enumerate(
             (
                 (res_hbm, res_ref),
@@ -206,8 +205,11 @@
             )
         )
     ]
-    for load in small[0:4] + loads + small[4:]:
+    chunk(0).start()
+    for load in small:
         load.start()
+    for n in range(1, pieces):
+        chunk(n).start()
     main = jnp.concatenate([att_ref[h, 0:HEAD, :] for h in range(HEADS)], axis=0)
     packed = [att_ref[h, HEAD : HEAD + HEAD // 2, :].astype(F32) for h in range(HEADS)]
     halo = jnp.concatenate(
@@ -219,15 +221,16 @@
     lhs[HALO + rows : span, :] = halo[0:HALO, :]
     frame = first - HALO + row_iota((span, LANES))
     valid = jnp.logical_and(frame >= 0, frame < length)
-    for load in small[0:4]:
-        load.wait()
-    for n in range(cols // 2):
-        wide = slice(2 * n * LANES, 2 * (n + 1) * LANES)
-        loads[n].wait()
-        proj = dot(lhs[...], weight[:, wide])
+    mid = rows + 32
+
+    def project(n):
+        at = pl.ds(pl.multiple_of(n * wide, wide), wide)
+        proj[...] = dot(lhs[...], weight[:, at])
+
+    def place(n):
         for m in range(2):
             c = 2 * n + m
-            at = slice(c * LANES, (c + 1) * LANES)
+            at = pl.ds(pl.multiple_of(c * LANES, LANES), LANES)
             res = jnp.concatenate(
                 [left_ref[0:HALO, at], res_ref[:, at], right_ref[0:HALO, at]], axis=0
             ).astype(F32)
@@ -235,14 +238,17 @@
             block_in[c] = block
             masked[c] = jnp.where(valid, block, 0.0).astype(BF).astype(F32)
             cot[c] = jnp.concatenate(
-                [left_ref[HALO + 16 : 2 * HALO, at], cot_ref[:, at], right_ref[HALO : HALO + 16, at]],
+                [left_ref[HALO : 2 * HALO, at], cot_ref[:, at], right_ref[HALO : 2 * HALO, at]],
                 axis=0,
-            ).astype(F32)
-    mid = rows + 32
-    small[4].wait()
-
-    @pl.loop(0, cols)
-    def _(c):
+            ).astype(F32)[16 : 16 + mid, :]
+
+    for load in small:
+        load.wait()
+    chunk(0).wait()
+    project(0)
+    place(0)
+
+    def channels(c):
         at = pl.ds(pl.multiple_of(c * LANES, LANES), LANES)
         acc = jnp.zeros((mid, LANES), F32)
         for r in range(TAPS):
@@ -262,6 +268,18 @@
             taps_sum[r // 2, pl.ds((r % 2) * cols + c, 1), :] = jnp.sum(prod, axis=0, keepdims=True)
         own_valid = valid[HALO : HALO + rows, :]
         bg_ref[:, at] = (cot[c, 16 : 16 + rows, :] + jnp.where(own_valid, back, 0.0)).astype(BF)
+
+    @pl.loop(0, pieces)
+    def _(n):
+        @pl.when(n < pieces - 1)
+        def _():
+            chunk(n + 1).wait()
+
+        after = lax.rem(n + 1, pieces)
+        project(after)
+        channels(2 * n)
+        channels(2 * n + 1)
+        place(after)
 
     taps_sum[HEADS - 1, pl.ds(cols, cols), :] = jnp.zeros((cols, LANES), F32)
     taps_sum[:, pl.ds(2 * cols, 8), :] = jnp.zeros((HEADS, 8, LANES), F32)
@@ -310,6 +328,7 @@
             pltpu.VMEM((2 * HALO, width), BF),
             pltpu.VMEM((width, width), BF),
             pltpu.VMEM((TAPS, width), F32),
+            pltpu.VMEM((span, 2 * LANES), F32),
             pltpu.SemaphoreType.DMA((cols // 2 + 5,)),
         ],
         compiler_params=params(20),
@@ -318,17 +337,13 @@
     )(info, att, res, cot, left, right, w, taps)
 
 
-def outer_kernel(info_ref, g_ref, *refs):
+def outer_kernel(info_ref, *refs):
     o_ref = refs[-1]
-    taps = jnp.sum(g_ref[:, HEAD:LANES, :].astype(F32), axis=0).astype(BF)
     core = info_ref[2]
     tall, wide = refs[0:4], refs[4:8]
     part = wide[0].shape[1] // 2
     at = pl.ds(pl.multiple_of(core * part, LANES), part)
     rhs = jnp.concatenate([ref[:, at] for ref in wide], axis=0)
-    below = part // LANES * HEAD
-    for h in range(HEADS):
-        o_ref[h, below : below + 32, :] = taps
     for h in range(0, HEADS, 4):
         lhs = jnp.concatenate(
             [
@@ -345,16 +360,43 @@
                 ]
 
 
-def outer(info, g, tall, wide):
+def outer(info, tall, wide):
     part = wide[0].shape[1] // 2
     return pl.pallas_call(
         outer_kernel,
-        out_shape=jax.ShapeDtypeStruct((HEADS, part // LANES * HEAD + 32, LANES), BF),
-        in_specs=[pl.BlockSpec(memory_space=pltpu.SMEM)] + [pl.BlockSpec()] * 9,
+        out_shape=pltpu.HBM((HEADS, part // LANES * HEAD + 32, LANES), BF),
+        in_specs=[pl.BlockSpec(memory_space=pltpu.SMEM)] + [pl.BlockSpec()] * 8,
         compiler_params=params(20),
         cost_estimate=cost(1e9, 4e6),
         name="outer",
-    )(info, g, *tall, *wide)
+    )(info, *tall, *wide)
+
+
+def tail_kernel(g_ref, w_ref, o_ref, taps, sems):
+    taps[...] = jnp.sum(g_ref[:, HEAD:LANES, :].astype(F32), axis=0).astype(BF)
+    base = o_ref.shape[1] - 32
+    copies = [
+        pltpu.make_async_copy(taps, o_ref.at[h, pl.ds(base, 32), :], sems.at[h])
+        for h in range(HEADS)
+    ]
+    for copy in copies:
+        copy.start()
+    for copy in copies:
+        copy.wait()
+
+
+def tail(g, w):
+    return pl.pallas_call(
+        tail_kernel,
+        out_shape=pltpu.HBM(w.shape, BF),
+        in_specs=[pl.BlockSpec(), pl.BlockSpec(memory_space=pl.ANY)],
+        out_specs=pl.BlockSpec(memory_space=pl.ANY),
+        scratch_shapes=[pltpu.VMEM((32, LANES), BF), pltpu.SemaphoreType.DMA((HEADS,))],
+        input_output_aliases={1: 0},
+        compiler_params=params(8),
+        cost_estimate=cost(1e6, 1e6),
+        name="tail",
+    )(g, w)
 
 
 def bwd_kernel(x_ref, g_ref, e_ref, o_ref, inv_ref, pay_ref, vaug, kt, dk, dv):
@@ -421,7 +463,7 @@
     return pl.pallas_call(
         bwd_kernel,
         grid=(steps,),
-        out_shape=jax.ShapeDtypeStruct((blocks, 3 * HEAD, LANES), BF),
+        out_shape=pltpu.HBM((blocks, 3 * HEAD, LANES), BF),
         in_specs=[
             pl.BlockSpec((blocks, 3 * HEAD, LANES), lambda i: (0, 0, 0)),
             pl.BlockSpec((blocks, LANES, LANES), lambda i: (0, 0, 0)),
@@ -462,7 +504,8 @@
 GROUP = 8
 
 
-def pack_kernel(x_ref, o_ref, buf):
+def pack_kernel(info_ref, x_ref, *refs):
+    outs, buf = refs[:GROUP], refs[GROUP]
     cols = x_ref.shape[1] // HEAD
     below = cols * HEAD
     for r in range(HEAD // 16):
@@ -474,39 +517,43 @@
                 n = (2 * r + e) * 2 * cols + c
                 buf[8 * n : 8 * n + 8, :] = both[8 * e : 8 * e + 8, :]
     share = buf.shape[0] // GROUP
-    for j in range(GROUP):
+    for k in range(GROUP):
+        j = jnp.bitwise_xor(info_ref[4], k)
         taps = [x_ref[2 * j + e, below : below + 32, :].astype(F32)[0:24] for e in range(2)]
-        rest = jnp.zeros((o_ref.shape[1] - share - 48, LANES), F32)
-        o_ref[j] = jnp.concatenate(
-            [buf[share * j : share * (j + 1), :]] + taps + [rest], axis=0
+        rest = jnp.zeros((outs[k].shape[0] - share - 48, LANES), F32)
+        outs[k][...] = jnp.concatenate(
+            [buf[pl.ds(pl.multiple_of(share * j, 8), share), :]] + taps + [rest], axis=0
         ).astype(BF)
 
 
-def pack(x):
+def pack(info, x):
     units = x.shape[1] // HEAD * HEAD * 2
     return pl.pallas_call(
         pack_kernel,
-        out_shape=jax.ShapeDtypeStruct((GROUP, LANES, LANES), BF),
+        out_shape=(pltpu.HBM((LANES, LANES), BF),) * GROUP,
+        in_specs=[pl.BlockSpec(memory_space=pltpu.SMEM), pl.BlockSpec()],
         scratch_shapes=[pltpu.VMEM((units, LANES), F32)],
         compiler_params=params(12),
         cost_estimate=cost(1e6, 3e6),
         name="pack",
-    )(x)
-
-
-def total_kernel(x_ref, o_ref):
-    total = jnp.sum(x_ref[...].astype(F32), axis=0) * (1.0 / o_ref.shape[0])
+    )(info, x)
+
+
+def total_kernel(*refs):
+    o_ref = refs[-1]
+    total = sum([ref[...].astype(F32) for ref in refs[1:-1]], refs[0][...].astype(F32))
+    total = total * (1.0 / o_ref.shape[0])
     o_ref[...] = jnp.broadcast_to(total.astype(BF)[None], o_ref.shape)
 
 
-def total(x, batch):
+def total(xs, batch):
     return pl.pallas_call(
         total_kernel,
-        out_shape=jax.ShapeDtypeStruct((batch,) + x.shape[1:], BF),
+        out_shape=pltpu.HBM((batch,) + xs[0].shape, BF),
         compiler_params=params(12),
         cost_estimate=cost(1e6, 1e6),
         name="total",
-    )(x)
+    )(*xs)
 
 
 def unpack_kernel(x_ref, w_ref, k_ref):
@@ -563,7 +610,10 @@
     batch = lax.axis_size("dp")
     depth = lax.axis_index("dp")
     levels = [(i, i ^ 2) for i in range(batch)]
-    same_level = [[i for i in range(batch) if (i // 2) % 2 == z] for z in range(2)]
+
+    def hop(k):
+        return [(i, i ^ (4 * (k // 2) + k % 2)) for i in range(batch)]
+
     query, key, value, res, cot, out_weight, conv_kernel = (
         in_hbm(x)
         for x in (query_proj[0], key_proj[0], value_proj[0], res, cot, out_weight, conv_kernel)
@@ -577,7 +627,8 @@
     attended = exchange(payload, "seq")
     att_level = lax.ppermute(attended, "dp", levels)
     att_core = lax.ppermute(attended, "seq", cores)
-    info = jnp.stack([lengths[0], me * rows, me % 2, depth // 2 % 2]).astype(jnp.int32)
+    member = depth // 4 * 2 + depth % 2
+    info = jnp.stack([lengths[0], me * rows, me % 2, depth // 2 % 2, member]).astype(jnp.int32)
     block_out, payload, keep, send = conv(
         info, attended, res, cot, in_hbm(left), in_hbm(right), out_weight, conv_kernel
     )
@@ -588,15 +639,17 @@
     partner = lax.ppermute(keep, "seq", cores)
     both = lax.ppermute(level, "seq", cores)
     partial = outer(
-        info, grads, (attended, att_core, att_level, att_both), (keep, partner, level, both)
+        info, (attended, att_core, att_level, att_both), (keep, partner, level, both)
     )
-    partial = exchange(partial, "seq")
+    partial = exchange(tail(grads, partial), "seq")
     payload = bwd(heads, grads, in_hbm(weights), in_hbm(mixed), inv)
     payload, partial = lax.optimization_barrier((payload, partial))
     back = exchange(payload, "seq")
+    packed = pack(info, partial)
+    packed = [packed[0]] + [lax.ppermute(packed[k], "dp", hop(k)) for k in range(1, GROUP)]
+    summed, back = lax.optimization_barrier((total(packed, batch), back))
+    final = exchange(summed, "dp")
     query_grad, key_grad, value_grad = post(back)
-    packed = exchange(pack(partial), "dp", same_level)
-    final = exchange(total(packed, batch), "dp")
     weight_grad, kernel_grad = unpack(final, width)
     return (
         block_out[None],

time: 182 us -> 174 us (0.956)
  starting transfers between devices: 47.5 us -> 67.4 us
  blocking collectives: 18.7 us -> 0 us
  waiting for transfers between devices: 66.8 us -> 58.1 us
    ppermute x0 -> x7, starting transfers between devices: none -> 19.1 us  [shards(): lax.ppermute(packed[k], 'dp', hop(k))]
    all_to_all x1 -> x0, blocking collectives: 18.7 us -> none  [exchange(): lax.all_to_all(x, axis, split_axis=0, concat_axis=0, tiled=True, axis_ind...]
    all_to_all x6, waiting for transfers between devices: 47.6 us -> 29.6 us  [exchange(): lax.all_to_all(x, axis, split_axis=0, concat_axis=0, tiled=True, axis_ind...]
    ppermute x0 -> x7, waiting for transfers between devices: none -> 9.37 us  [shards(): lax.ppermute(packed[k], 'dp', hop(k))]
    pallas_call x4 -> x5, Pallas kernels: 16.1 us -> 18.2 us  [the longest x1 11.8 us: bwd(): pl.pallas_call(bwd_kernel, grid=(steps,), out_shape=pltpu.HBM((blocks, 3...]
  transfers between devices with their start and end apart: 14 -> 21, of which waited for: 7 -> 10; matrix products, arithmetic and copies ran while one was open for 0% -> 0% of each run, Pallas kernels for 15% -> 18%
where the time goes in v3:
time: 174 us; the launch traced here: 173 us
  starting transfers between devices  67.4 us (39%)
  waiting for transfers between devices  58.1 us (33%)
  Pallas kernels  44.3 us (25%)
  local copies, waits for them, and re-layouts  1.78 us (1%)
    all_to_all x6, starting transfers between devices, exchange(): lax.all_to_all(x, axis, split_axis=0, concat_axis=0, tiled=True, axis_ind...  38.1 us
    all_to_all x6, waiting for transfers between devices, exchange(): lax.all_to_all(x, axis, split_axis=0, concat_axis=0, tiled=True, axis_ind...  29.6 us
    ppermute x7, starting transfers between devices, shards(): lax.ppermute(packed[k], 'dp', hop(k))  19.1 us
    pallas_call x1, Pallas kernels, conv(): pl.pallas_call(conv_kernel_body, out_shape=(jax.ShapeDtypeStruct((rows, w...  12.1 us
    pallas_call x1, Pallas kernels, bwd(): pl.pallas_call(bwd_kernel, grid=(steps,), out_shape=pltpu.HBM((blocks, 3...  11.8 us
    ppermute x1, waiting for transfers between devices, shards(): left = lax.ppermute(edge_up, 'seq', up)  11.2 us
    pallas_call x1, Pallas kernels, fwd(): pl.pallas_call(fwd_kernel, grid=(steps,), out_shape=(pltpu.HBM((steps, fr...  9.4 us
    ppermute x7, waiting for transfers between devices, shards(): lax.ppermute(packed[k], 'dp', hop(k))  9.37 us
  transfers between devices with their start and end apart: 21, of which 10 were waited for; matrix products, arithmetic and copies ran while one was open for 0% of the time, Pallas kernels for 18%

profile of v3, /device:TPU:2, one launch (start us, length us, event | category | flops | bytes accessed | tf_op | source)
XLA Modules:
  0.0 173.0 jit_solution(13054432307403307827)
XLA Ops:
  0.6 2.6 %pre.1 = (bf16[16,288,128]{2,1,0:T(8,128)(2,1)}, bf16[64,1536]{1,0:T(8,128)(2,1)S(1)}, bf16[64,1536]{1,0:T(8,128)(2,1)S(1)}) custom-call(bf16[128,1536]{1,0:T(8,128)(2,1)} %bitcast.13, bf16[128,1536]{1,0:T(8,128)(2,1)} %bitcast.14, bf16[128,1536]{1,0:T(8,128)(2,1)} %bitcast.15, bf16[128,1536]{1,0:T(8,128)(2,1)} %bitcast.16, bf16[128,1536]{1,0:T(8,128)(2,1)} %bitcast.18), custom_call_target="tpu_custom_call" | custom-call | flops 1000000 | bytes 3000000 | tf_op jit(solution)/shard_map/pre/pallas_call | solution.py:71
  3.2 7.5 %all-to-all-start = ((bf16[16,288,128]{2,1,0:T(8,128)(2,1)}), bf16[16,288,128]{2,1,0:T(8,128)(2,1)S(1)}, u32[]{:S(2)}, u32[]{:S(2)}) async-start(bf16[16,288,128]{2,1,0:T(8,128)(2,1)} %get-tuple-element.39), calls=%async_computation | async-start | bytes 2359296 | tf_op jit(solution)/shard_map/all_to_all | solution.py:597
  10.7 2.0 %collective-permute-start = (bf16[64,1536]{1,0:T(8,128)(2,1)S(1)}, bf16[64,1536]{1,0:T(8,128)(2,1)S(1)}, u32[]{:S(2)}, u32[]{:S(2)}) collective-permute-start(bf16[64,1536]{1,0:T(8,128)(2,1)S(1)} %get-tuple-element.40), channel_id=1, source_target_pairs={{0,1},{1,2},{2,3},{3,4},{4,5},{5,6},{6,7},{7,8},{8,9},{9,10},{10,1... | collective-permute-start | bytes 589832 | tf_op jit(solution)/shard_map/ppermute | solution.py:623
  12.7 3.5 %collective-permute-start.1 = (bf16[64,1536]{1,0:T(8,128)(2,1)S(1)}, bf16[64,1536]{1,0:T(8,128)(2,1)S(1)}, u32[]{:S(2)}, u32[]{:S(2)}) collective-permute-start(bf16[64,1536]{1,0:T(8,128)(2,1)S(1)} %get-tuple-element.41), channel_id=1, source_target_pairs={{1,0},{2,1},{3,2},{4,3},{5,4},{6,5},{7,6},{8,7},{9,8},{10,9},{11,1... | collective-permute-start | bytes 589832 | tf_op jit(solution)/shard_map/ppermute | solution.py:624
  16.9 11.2 %collective-permute-done.left_hbm = bf16[64,1536]{1,0:T(8,128)(2,1)S(1)} collective-permute-done((bf16[64,1536]{1,0:T(8,128)(2,1)S(1)}, bf16[64,1536]{1,0:T(8,128)(2,1)S(1)}, u32[]{:S(2)}, u32[]{:S(2)}) %collective-permute-start) | collective-permute-done | bytes 196640 | tf_op jit(solution)/shard_map/ppermute | solution.py:623
  28.1 9.4 %attend.1 = (bf16[4,2048,512]{2,1,0:T(8,128)(2,1)}, f32[96,2048]{1,0:T(8,128)}, f32[8,2048]{1,0:T(8,128)S(1)}, bf16[16,144,128]{2,1,0:T(8,128)(2,1)}) custom-call(s32[1]{0:T(128)S(6)} %copy.16.len_ref, bf16[16,288,128]{2,1,0:T(8,128)(2,1)S(1)} %all-to-all-done.x_ref), custom_call_target="tpu_custom_call" | custom-call | flops 8999999488 | bytes 10000000 | tf_op jit(solution)/shard_map/attend/pallas_call | solution.py:147
  37.5 6.4 %all-to-all-start.1 = ((bf16[16,144,128]{2,1,0:T(8,128)(2,1)}), bf16[16,144,128]{2,1,0:T(8,128)(2,1)S(1)}, u32[]{:S(2)}, u32[]{:S(2)}) async-start(bf16[16,144,128]{2,1,0:T(8,128)(2,1)} %get-tuple-element.43), calls=%async_computation.1 | async-start | bytes 1179648 | tf_op jit(solution)/shard_map/all_to_all | solution.py:597
  44.1 9.1 %all-to-all-done.1.att_ref.refs_0_ = bf16[16,144,128]{2,1,0:T(8,128)(2,1)S(1)} async-done(((bf16[16,144,128]{2,1,0:T(8,128)(2,1)}), bf16[16,144,128]{2,1,0:T(8,128)(2,1)S(1)}, u32[]{:S(2)}, u32[]{:S(2)}) %all-to-all-start.1) | async-done | bytes 589856 | tf_op jit(solution)/shard_map/all_to_all | solution.py:597
  53.2 1.9 %collective-permute-start.2 = (bf16[16,144,128]{2,1,0:T(8,128)(2,1)S(1)}, bf16[16,144,128]{2,1,0:T(8,128)(2,1)S(1)}, u32[]{:S(2)}, u32[]{:S(2)}) collective-permute-start(bf16[16,144,128]{2,1,0:T(8,128)(2,1)S(1)} %all-to-all-done.1.att_ref.refs_0_), channel_id=1, source_target_pairs={{0,32},{16,48},{32,0},{48,16},{64,96},{80,112},{96,64},{112,80},{1... | collective-permute-start | bytes 1769480 | tf_op jit(solution)/shard_map/ppermute | solution.py:628
  55.9 12.1 %convolve.1 = (bf16[128,1536]{1,0:T(8,128)(2,1)}, bf16[16,128,128]{2,1,0:T(8,128)(2,1)}, bf16[128,768]{1,0:T(8,128)(2,1)}, bf16[128,768]{1,0:T(8,128)(2,1)}) custom-call(s32[5]{0:T(128)S(1)} %stack.19.info_ref, bf16[16,144,128]{2,1,0:T(8,128)(2,1)S(1)} %all-to-all-done.1.att_ref.refs_0_, bf16[128,1536]{1,0:T(8,128)(2,1)} %bitcast.17, ...), custom_call_target="tpu_custom_call" | custom-call | flops 8999999488 | bytes 10000000 | tf_op jit(solution)/shard_map/convolve/pallas_call | solution.py:305
  68.0 1.1 collective-permute-done.2.refs_2_
  69.2 6.2 %all-to-all-start.2 = ((bf16[16,128,128]{2,1,0:T(8,128)(2,1)}), bf16[16,128,128]{2,1,0:T(8,128)(2,1)S(1)}, u32[]{:S(2)}, u32[]{:S(2)}) async-start(bf16[16,128,128]{2,1,0:T(8,128)(2,1)} %get-tuple-element.48), calls=%async_computation.2 | async-start | bytes 1048576 | tf_op jit(solution)/shard_map/all_to_all | solution.py:597
  75.4 1.7 %collective-permute-start.6 = (bf16[128,768]{1,0:T(8,128)(2,1)}, bf16[128,768]{1,0:T(8,128)(2,1)S(1)}, u32[]{:S(2)}, u32[]{:S(2)}) collective-permute-start(bf16[128,768]{1,0:T(8,128)(2,1)} %get-tuple-element.54), channel_id=1, source_target_pairs={{0,32},{16,48},{32,0},{48,16},{64,96},{80,112},{96,64},{112,80},{1... | collective-permute-start | bytes 589832 | tf_op jit(solution)/shard_map/ppermute | solution.py:638
  77.1 5.4 %collective-permute-done.6.refs_6_ = bf16[128,768]{1,0:T(8,128)(2,1)S(1)} collective-permute-done((bf16[128,768]{1,0:T(8,128)(2,1)}, bf16[128,768]{1,0:T(8,128)(2,1)S(1)}, u32[]{:S(2)}, u32[]{:S(2)}) %collective-permute-start.6) | collective-permute-done | bytes 196640 | tf_op jit(solution)/shard_map/ppermute | solution.py:638
  82.6 1.4 collective-permute-done.7.refs_7_
  84.0 0.9 copy-done
  84.9 3.3 %outer.1.w_ref = bf16[16,320,128]{2,1,0:T(8,128)(2,1)} custom-call(s32[5]{0:T(128)S(1)} %stack.19.info_ref, bf16[16,144,128]{2,1,0:T(8,128)(2,1)S(1)} %all-to-all-done.1.att_ref.refs_0_, bf16[16,144,128]{2,1,0:T(8,128)(2,1)} %collective-permute-done.3.refs_1_, bf16[16,144,128]{2,1,0:T(8,128)(2,1)S(1)} %collective-permute-done.2.refs_2_, ...), custom_call_target="tpu_custom_call" | custom-call | flops 1000000000 | bytes 4000000 | tf_op jit(solution)/shard_map/outer/pallas_call | solution.py:365
  89.1 7.3 %all-to-all-start.3 = ((bf16[16,320,128]{2,1,0:T(8,128)(2,1)}), bf16[16,320,128]{2,1,0:T(8,128)(2,1)S(1)}, u32[]{:S(2)}, u32[]{:S(2)}) async-start(bf16[16,320,128]{2,1,0:T(8,128)(2,1)} %tail.1), calls=%async_computation.3 | async-start | bytes 2621440 | tf_op jit(solution)/shard_map/all_to_all | solution.py:597
  96.4 11.8 %attend_back.1 = bf16[16,288,128]{2,1,0:T(8,128)(2,1)} custom-call(bf16[16,288,128]{2,1,0:T(8,128)(2,1)S(1)} %all-to-all-done.x_ref, bf16[16,128,128]{2,1,0:T(8,128)(2,1)S(1)} %all-to-all-done.2.g_ref, bf16[4,2048,512]{2,1,0:T(8,128)(2,1)} %get-tuple-element.49.e_ref, f32[96,2048]{1,0:T(8,128)} %get-tuple-element.50.o_ref, ...), custom_call_target="tpu_custom_call" | custom-call | flops 20000000000 | bytes 10000000 | tf_op jit(solution)/shard_map/attend_back/pallas_call | solution.py:463
  108.2 6.0 %all-to-all-done.3.x_ref = bf16[16,320,128]{2,1,0:T(8,128)(2,1)S(1)} async-done(((bf16[16,320,128]{2,1,0:T(8,128)(2,1)}), bf16[16,320,128]{2,1,0:T(8,128)(2,1)S(1)}, u32[]{:S(2)}, u32[]{:S(2)}) %all-to-all-start.3) | async-done | bytes 1310752 | tf_op jit(solution)/shard_map/all_to_all | solution.py:597
  114.2 6.6 %all-to-all-start.4 = ((bf16[16,288,128]{2,1,0:T(8,128)(2,1)}), bf16[16,288,128]{2,1,0:T(8,128)(2,1)S(1)}, u32[]{:S(2)}, u32[]{:S(2)}) async-start(bf16[16,288,128]{2,1,0:T(8,128)(2,1)} %attend_back.1), calls=%async_computation.4 | async-start | bytes 2359296 | tf_op jit(solution)/shard_map/all_to_all | solution.py:597
  120.8 1.4 pack.1
  122.9 3.3 %collective-permute-start.9 = (bf16[128,128]{1,0:T(8,128)(2,1)}, bf16[128,128]{1,0:T(8,128)(2,1)S(1)}, u32[]{:S(2)}, u32[]{:S(2)}) collective-permute-start(bf16[128,128]{1,0:T(8,128)(2,1)} %get-tuple-element.58), channel_id=1, source_target_pairs={{0,64},{16,80},{32,96},{48,112},{64,0},{80,16},{96,32},{112,48},{1... | collective-permute-start | bytes 98312 | tf_op jit(solution)/shard_map/ppermute | solution.py:649
  126.9 6.7 %collective-permute-start.11 = (bf16[128,128]{1,0:T(8,128)(2,1)}, bf16[128,128]{1,0:T(8,128)(2,1)S(1)}, u32[]{:S(2)}, u32[]{:S(2)}) collective-permute-start(bf16[128,128]{1,0:T(8,128)(2,1)} %get-tuple-element.60), channel_id=1, source_target_pairs={{0,128},{16,144},{32,160},{48,176},{64,192},{80,208},{96,224},{112... | collective-permute-start | bytes 98312 | tf_op jit(solution)/shard_map/ppermute | solution.py:649
  133.7 3.0 %collective-permute-done.8.refs_1_ = bf16[128,128]{1,0:T(8,128)(2,1)S(1)} collective-permute-done((bf16[128,128]{1,0:T(8,128)(2,1)}, bf16[128,128]{1,0:T(8,128)(2,1)S(1)}, u32[]{:S(2)}, u32[]{:S(2)}) %collective-permute-start.8) | collective-permute-done | bytes 32800 | tf_op jit(solution)/shard_map/ppermute | solution.py:649
  136.8 6.8 %collective-permute-start.13 = (bf16[128,128]{1,0:T(8,128)(2,1)}, bf16[128,128]{1,0:T(8,128)(2,1)S(1)}, u32[]{:S(2)}, u32[]{:S(2)}) collective-permute-start(bf16[128,128]{1,0:T(8,128)(2,1)} %get-tuple-element.62), channel_id=1, source_target_pairs={{0,192},{16,208},{32,224},{48,240},{64,128},{80,144},{96,160},{112... | collective-permute-start | bytes 98312 | tf_op jit(solution)/shard_map/ppermute | solution.py:649
  144.4 1.3 collective-permute-done.13.refs_6_
  145.7 5.0 %collective-permute-done.14.refs_7_ = bf16[128,128]{1,0:T(8,128)(2,1)S(1)} collective-permute-done((bf16[128,128]{1,0:T(8,128)(2,1)}, bf16[128,128]{1,0:T(8,128)(2,1)S(1)}, u32[]{:S(2)}, u32[]{:S(2)}) %collective-permute-start.14) | collective-permute-done | bytes 32800 | tf_op jit(solution)/shard_map/ppermute | solution.py:649
  152.3 4.1 %all-to-all-start.5 = ((bf16[16,128,128]{2,1,0:T(8,128)(2,1)}), bf16[16,128,128]{2,1,0:T(8,128)(2,1)S(1)}, u32[]{:S(2)}, u32[]{:S(2)}) async-start(bf16[16,128,128]{2,1,0:T(8,128)(2,1)} %total.1), calls=%async_computation.5 | async-start | bytes 1048576 | tf_op jit(solution)/shard_map/all_to_all | solution.py:597
  156.4 1.2 post.1
  157.6 14.5 %all-to-all-done.5.x_ref = bf16[16,128,128]{2,1,0:T(8,128)(2,1)S(1)} async-done(((bf16[16,128,128]{2,1,0:T(8,128)(2,1)}), bf16[16,128,128]{2,1,0:T(8,128)(2,1)S(1)}, u32[]{:S(2)}, u32[]{:S(2)}) %all-to-all-start.5) | async-done | bytes 524320 | tf_op jit(solution)/shard_map/all_to_all | solution.py:597
  172.1 0.9 unpack.1
  (29 shorter events, 5.9 us)
Async XLA Ops:
  3.2 24.9 %all-to-all-start = ((bf16[16,288,128]{2,1,0:T(8,128)(2,1)}), bf16[16,288,128]{2,1,0:T(8,128)(2,1)S(1)}, u32[]{:S(2)}, u32[]{:S(2)}) async-start(bf16[16,288,128]{2,1,0:T(8,128)(2,1)} %get-tuple-element.39), calls=%async_computation | async-start | bytes 2359296 | tf_op jit(solution)/shard_map/all_to_all | solution.py:597
  10.7 17.4 %collective-permute-start = (bf16[64,1536]{1,0:T(8,128)(2,1)S(1)}, bf16[64,1536]{1,0:T(8,128)(2,1)S(1)}, u32[]{:S(2)}, u32[]{:S(2)}) collective-permute-start(bf16[64,1536]{1,0:T(8,128)(2,1)S(1)} %get-tuple-element.40), channel_id=1, source_target_pairs={{0,1},{1,2},{2,3},{3,4},{4,5},{5,6},{6,7},{7,8},{8,9},{9,10},{10,1... | collective-permute-start | bytes 589832 | tf_op jit(solution)/shard_map/ppermute | solution.py:623
  12.7 15.4 %collective-permute-start.1 = (bf16[64,1536]{1,0:T(8,128)(2,1)S(1)}, bf16[64,1536]{1,0:T(8,128)(2,1)S(1)}, u32[]{:S(2)}, u32[]{:S(2)}) collective-permute-start(bf16[64,1536]{1,0:T(8,128)(2,1)S(1)} %get-tuple-element.41), channel_id=1, source_target_pairs={{1,0},{2,1},{3,2},{4,3},{5,4},{6,5},{7,6},{8,7},{9,8},{10,9},{11,1... | collective-permute-start | bytes 589832 | tf_op jit(solution)/shard_map/ppermute | solution.py:624
  28.1 9.4 %copy-start.2 = (bf16[64,1536]{1,0:T(8,128)(2,1)}, bf16[64,1536]{1,0:T(8,128)(2,1)S(1)}, u32[]{:S(2)}) copy-start(bf16[64,1536]{1,0:T(8,128)(2,1)S(1)} %collective-permute-done.left_hbm) | copy-start | bytes 589828
  28.1 9.4 %copy-start.3 = (bf16[64,1536]{1,0:T(8,128)(2,1)}, bf16[64,1536]{1,0:T(8,128)(2,1)S(1)}, u32[]{:S(2)}) copy-start(bf16[64,1536]{1,0:T(8,128)(2,1)S(1)} %collective-permute-done.1.right_hbm) | copy-start | bytes 589828
  37.5 15.7 %all-to-all-start.1 = ((bf16[16,144,128]{2,1,0:T(8,128)(2,1)}), bf16[16,144,128]{2,1,0:T(8,128)(2,1)S(1)}, u32[]{:S(2)}, u32[]{:S(2)}) async-start(bf16[16,144,128]{2,1,0:T(8,128)(2,1)} %get-tuple-element.43), calls=%async_computation.1 | async-start | bytes 1179648 | tf_op jit(solution)/shard_map/all_to_all | solution.py:597
  53.2 15.9 %collective-permute-start.2 = (bf16[16,144,128]{2,1,0:T(8,128)(2,1)S(1)}, bf16[16,144,128]{2,1,0:T(8,128)(2,1)S(1)}, u32[]{:S(2)}, u32[]{:S(2)}) collective-permute-start(bf16[16,144,128]{2,1,0:T(8,128)(2,1)S(1)} %all-to-all-done.1.att_ref.refs_0_), channel_id=1, source_target_pairs={{0,32},{16,48},{32,0},{48,16},{64,96},{80,112},{96,64},{112,80},{1... | collective-permute-start | bytes 1769480 | tf_op jit(solution)/shard_map/ppermute | solution.py:628
  55.1 28.9 %collective-permute-start.3 = (bf16[16,144,128]{2,1,0:T(8,128)(2,1)S(1)}, bf16[16,144,128]{2,1,0:T(8,128)(2,1)}, u32[]{:S(2)}, u32[]{:S(2)}) collective-permute-start(bf16[16,144,128]{2,1,0:T(8,128)(2,1)S(1)} %all-to-all-done.1.att_ref.refs_0_), channel_id=1, source_target_pairs={{0,1},{1,0},{2,3},{3,2},{4,5},{5,4},{6,7},{7,6},{8,9},{9,8},{10,11... | collective-permute-start | bytes 1769480 | tf_op jit(solution)/shard_map/ppermute | solution.py:629
  69.1 14.9 %collective-permute-start.4 = (bf16[16,144,128]{2,1,0:T(8,128)(2,1)S(1)}, bf16[16,144,128]{2,1,0:T(8,128)(2,1)}, u32[]{:S(2)}, u32[]{:S(2)}) collective-permute-start(bf16[16,144,128]{2,1,0:T(8,128)(2,1)S(1)} %collective-permute-done.2.refs_2_), channel_id=1, source_target_pairs={{0,1},{1,0},{2,3},{3,2},{4,5},{5,4},{6,7},{7,6},{8,9},{9,8},{10,11... | collective-permute-start | bytes 1769480 | tf_op jit(solution)/shard_map/ppermute | solution.py:636
  69.2 19.1 %all-to-all-start.2 = ((bf16[16,128,128]{2,1,0:T(8,128)(2,1)}), bf16[16,128,128]{2,1,0:T(8,128)(2,1)S(1)}, u32[]{:S(2)}, u32[]{:S(2)}) async-start(bf16[16,128,128]{2,1,0:T(8,128)(2,1)} %get-tuple-element.48), calls=%async_computation.2 | async-start | bytes 1048576 | tf_op jit(solution)/shard_map/all_to_all | solution.py:597
  75.4 7.2 %collective-permute-start.6 = (bf16[128,768]{1,0:T(8,128)(2,1)}, bf16[128,768]{1,0:T(8,128)(2,1)S(1)}, u32[]{:S(2)}, u32[]{:S(2)}) collective-permute-start(bf16[128,768]{1,0:T(8,128)(2,1)} %get-tuple-element.54), channel_id=1, source_target_pairs={{0,32},{16,48},{32,0},{48,16},{64,96},{80,112},{96,64},{112,80},{1... | collective-permute-start | bytes 589832 | tf_op jit(solution)/shard_map/ppermute | solution.py:638
  77.1 5.4 %collective-permute-start.5 = (bf16[128,768]{1,0:T(8,128)(2,1)}, bf16[128,768]{1,0:T(8,128)(2,1)S(1)}, u32[]{:S(2)}, u32[]{:S(2)}) collective-permute-start(bf16[128,768]{1,0:T(8,128)(2,1)} %get-tuple-element.53.refs_4_), channel_id=1, source_target_pairs={{0,1},{1,0},{2,3},{3,2},{4,5},{5,4},{6,7},{7,6},{8,9},{9,8},{10,11... | collective-permute-start | bytes 589832 | tf_op jit(solution)/shard_map/ppermute | solution.py:639
  82.6 1.4 collective-permute-start.7
  84.0 0.9 copy-start
  89.1 25.0 %all-to-all-start.3 = ((bf16[16,320,128]{2,1,0:T(8,128)(2,1)}), bf16[16,320,128]{2,1,0:T(8,128)(2,1)S(1)}, u32[]{:S(2)}, u32[]{:S(2)}) async-start(bf16[16,320,128]{2,1,0:T(8,128)(2,1)} %tail.1), calls=%async_computation.3 | async-start | bytes 2621440 | tf_op jit(solution)/shard_map/all_to_all | solution.py:597
  114.2 38.2 %all-to-all-start.4 = ((bf16[16,288,128]{2,1,0:T(8,128)(2,1)}), bf16[16,288,128]{2,1,0:T(8,128)(2,1)S(1)}, u32[]{:S(2)}, u32[]{:S(2)}) async-start(bf16[16,288,128]{2,1,0:T(8,128)(2,1)} %attend_back.1), calls=%async_computation.4 | async-start | bytes 2359296 | tf_op jit(solution)/shard_map/all_to_all | solution.py:597
  122.2 14.6 %collective-permute-start.8 = (bf16[128,128]{1,0:T(8,128)(2,1)}, bf16[128,128]{1,0:T(8,128)(2,1)S(1)}, u32[]{:S(2)}, u32[]{:S(2)}) collective-permute-start(bf16[128,128]{1,0:T(8,128)(2,1)} %get-tuple-element.57), channel_id=1, source_target_pairs={{0,16},{16,0},{32,48},{48,32},{64,80},{80,64},{96,112},{112,96},{1... | collective-permute-start | bytes 98312 | tf_op jit(solution)/shard_map/ppermute | solution.py:649
  122.9 20.7 %collective-permute-start.9 = (bf16[128,128]{1,0:T(8,128)(2,1)}, bf16[128,128]{1,0:T(8,128)(2,1)S(1)}, u32[]{:S(2)}, u32[]{:S(2)}) collective-permute-start(bf16[128,128]{1,0:T(8,128)(2,1)} %get-tuple-element.58), channel_id=1, source_target_pairs={{0,64},{16,80},{32,96},{48,112},{64,0},{80,16},{96,32},{112,48},{1... | collective-permute-start | bytes 98312 | tf_op jit(solution)/shard_map/ppermute | solution.py:649
  126.1 18.2 %collective-permute-start.10 = (bf16[128,128]{1,0:T(8,128)(2,1)}, bf16[128,128]{1,0:T(8,128)(2,1)S(1)}, u32[]{:S(2)}, u32[]{:S(2)}) collective-permute-start(bf16[128,128]{1,0:T(8,128)(2,1)} %get-tuple-element.59), channel_id=1, source_target_pairs={{0,80},{16,64},{32,112},{48,96},{64,16},{80,0},{96,48},{112,32},{1... | collective-permute-start | bytes 98312 | tf_op jit(solution)/shard_map/ppermute | solution.py:649
  126.9 17.4 %collective-permute-start.11 = (bf16[128,128]{1,0:T(8,128)(2,1)}, bf16[128,128]{1,0:T(8,128)(2,1)S(1)}, u32[]{:S(2)}, u32[]{:S(2)}) collective-permute-start(bf16[128,128]{1,0:T(8,128)(2,1)} %get-tuple-element.60), channel_id=1, source_target_pairs={{0,128},{16,144},{32,160},{48,176},{64,192},{80,208},{96,224},{112... | collective-permute-start | bytes 98312 | tf_op jit(solution)/shard_map/ppermute | solution.py:649
  133.6 10.8 %collective-permute-start.12 = (bf16[128,128]{1,0:T(8,128)(2,1)}, bf16[128,128]{1,0:T(8,128)(2,1)S(1)}, u32[]{:S(2)}, u32[]{:S(2)}) collective-permute-start(bf16[128,128]{1,0:T(8,128)(2,1)} %get-tuple-element.61), channel_id=1, source_target_pairs={{0,144},{16,128},{32,176},{48,160},{64,208},{80,192},{96,240},{112... | collective-permute-start | bytes 98312 | tf_op jit(solution)/shard_map/ppermute | solution.py:649
  136.8 8.9 %collective-permute-start.13 = (bf16[128,128]{1,0:T(8,128)(2,1)}, bf16[128,128]{1,0:T(8,128)(2,1)S(1)}, u32[]{:S(2)}, u32[]{:S(2)}) collective-permute-start(bf16[128,128]{1,0:T(8,128)(2,1)} %get-tuple-element.62), channel_id=1, source_target_pairs={{0,192},{16,208},{32,224},{48,240},{64,128},{80,144},{96,160},{112... | collective-permute-start | bytes 98312 | tf_op jit(solution)/shard_map/ppermute | solution.py:649
  143.6 7.1 %collective-permute-start.14 = (bf16[128,128]{1,0:T(8,128)(2,1)}, bf16[128,128]{1,0:T(8,128)(2,1)S(1)}, u32[]{:S(2)}, u32[]{:S(2)}) collective-permute-start(bf16[128,128]{1,0:T(8,128)(2,1)} %get-tuple-element.63), channel_id=1, source_target_pairs={{0,208},{16,192},{32,240},{48,224},{64,144},{80,128},{96,176},{112... | collective-permute-start | bytes 98312 | tf_op jit(solution)/shard_map/ppermute | solution.py:649
  150.7 0.8 copy-start.1
  152.3 19.7 %all-to-all-start.5 = ((bf16[16,128,128]{2,1,0:T(8,128)(2,1)}), bf16[16,128,128]{2,1,0:T(8,128)(2,1)S(1)}, u32[]{:S(2)}, u32[]{:S(2)}) async-start(bf16[16,128,128]{2,1,0:T(8,128)(2,1)} %total.1), calls=%async_computation.5 | async-start | bytes 1048576 | tf_op jit(solution)/shard_map/all_to_all | solution.py:597

commit v4 on v3

--- a/solution.py
+++ b/solution.py
@@ -79,65 +79,84 @@
     )(q, k, v, res, cot)
 
 
-def fwd_kernel(len_ref, x_ref, e_ref, o_ref, inv_ref, pay_ref, kaug, vaug, sbuf):
-    step = pl.program_id(0)
+def fwd_kernel(len_ref, x_ref, e_hbm, o_ref, inv_ref, pay_ref, kaug, vaug, even, odd, ebuf, sems):
     blocks = x_ref.shape[0]
+    frames = blocks * LANES
     scale = math.log2(math.e) / math.sqrt(HEAD)
-
-    @pl.when(step == 0)
-    def _():
-        length = len_ref[0]
-        for j in range(blocks):
-            rows = pl.ds(j * LANES, LANES)
-            bias = jnp.where(j * LANES + lane_iota((32, LANES)) < length, 0.0, -1e30)
-            bias = jnp.where(row_iota((32, LANES)) == 0, bias, 0.0)
-            turned = jnp.concatenate([x_ref[j, HEAD : 2 * HEAD, :], bias.astype(BF)], axis=0).T
-            kaug[rows, 0:LANES] = turned
-            kaug[rows, LANES : 2 * LANES] = turned
-            vaug[0:HEAD, rows] = x_ref[j, 2 * HEAD : 3 * HEAD, :]
-            vaug[HEAD : HEAD + 16, rows] = jnp.where(row_iota((16, LANES)) == 0, 1.0, 0.0).astype(BF)
-
+    length = len_ref[0]
+    for j in range(blocks):
+        rows = slice(j * LANES, (j + 1) * LANES)
+        bias = jnp.where(j * LANES + lane_iota((32, LANES)) < length, 0.0, -1e30)
+        bias = jnp.where(row_iota((32, LANES)) == 0, bias, 0.0)
+        turned = jnp.concatenate([x_ref[j, HEAD : 2 * HEAD, :], bias.astype(BF)], axis=0).T
+        kaug[rows, 0:LANES] = turned
+        kaug[rows, LANES : 2 * LANES] = turned
+        vaug[0:HEAD, rows] = x_ref[j, 2 * HEAD : 3 * HEAD, :]
+        vaug[HEAD : HEAD + 16, rows] = jnp.where(row_iota((16, LANES)) == 0, 1.0, 0.0).astype(BF)
     per = QT // LANES
-    qt = jnp.concatenate([x_ref[step * per + p, 0:HEAD, :] for p in range(per)], axis=1)
-    qs = qt.astype(F32) * scale
-    hi = qs.astype(BF)
-    lo = (qs - hi.astype(F32)).astype(BF)
+    count = frames // QT
+    tiles = frames // KT
     one = jnp.where(row_iota((32, QT)) == 0, 1.0, 0.0).astype(BF)
-    qaug = jnp.concatenate([hi, one, lo, jnp.zeros((32, QT), BF)], axis=0)
-    tiles = kaug.shape[0] // KT
+
+    def queries(i):
+        qt = jnp.concatenate([x_ref[i * per + p, 0:HEAD, :] for p in range(per)], axis=1)
+        qs = qt.astype(F32) * scale
+        hi = qs.astype(BF)
+        lo = (qs - hi.astype(F32)).astype(BF)
+        return jnp.concatenate([hi, one, lo, jnp.zeros((32, QT), BF)], axis=0)
+
+    def score(buf, t, qaug, top):
+        s = dot(kaug[t * KT : (t + 1) * KT, :], qaug)
+        buf[t * KT : (t + 1) * KT, :] = s
+        part = jnp.max(s.reshape(KT // 8, 8, QT), axis=0)
+        return part if top is None else jnp.maximum(top, part)
+
+    def out_copy(i, t):
+        at = pl.ds(t * KT, 2 * KT)
+        return pltpu.make_async_copy(ebuf.at[i, at], e_hbm.at[i, at], sems.at[i, t // 2])
+
+    bufs = (even, odd)
     top = None
+    qaug = queries(0)
     for t in range(tiles):
-        s = dot(kaug[t * KT : (t + 1) * KT, :], qaug)
-        sbuf[t * KT : (t + 1) * KT, :] = s
-        part = jnp.max(s.reshape(KT // 8, 8, QT), axis=0)
-        top = part if top is None else jnp.maximum(top, part)
-    top = jnp.max(top, axis=0, keepdims=True)
-    acc = jnp.zeros((HEAD + 16, QT), F32)
-    for t in range(tiles):
-        e = jnp.exp2(sbuf[t * KT : (t + 1) * KT, :] - top).astype(BF)
-        e_ref[0, t * KT : (t + 1) * KT, :] = e
-        acc = acc + dot(vaug[:, t * KT : (t + 1) * KT], e)
-    inv = 1.0 / acc[HEAD : HEAD + 1, :]
-    out = acc[0:HEAD, :] * inv
-    o_ref[...] = out
-    inv_ref[...] = jnp.broadcast_to(inv, (8, QT))
-    rounded = out.astype(BF)
-    for p in range(per):
-        pay_ref[step * per + p, 0:HEAD, :] = rounded[:, p * LANES : (p + 1) * LANES]
-
-    @pl.when(step == pl.num_programs(0) - 1)
-    def _():
-        low = HEAD // 2
-        lane = lane_iota((low, LANES))
-        left = lane < LANES // 2
-        outer_lanes = jnp.logical_or(lane < HALO, lane >= LANES - HALO)
-        for j in range(blocks):
-            after = pay_ref[min(j + 1, blocks - 1), 0:HEAD, :].astype(F32)
-            before = pay_ref[max(j - 1, 0), 0:HEAD, :].astype(F32)
-            first = jnp.where(left, after[0:low], before[0:low])
-            second = jnp.where(left, after[low:HEAD], before[low:HEAD])
-            second = pltpu.roll(second, LANES // 2, 1)
-            pay_ref[j, HEAD : HEAD + low, :] = jnp.where(outer_lanes, first, second).astype(BF)
+        top = score(bufs[0], t, qaug, top)
+    for i in range(count):
+        peak = jnp.max(top, axis=0, keepdims=True)
+        top = None
+        if i + 1 < count:
+            qaug = queries(i + 1)
+        acc = jnp.zeros((HEAD + 16, QT), F32)
+        for t in range(tiles):
+            rows = slice(t * KT, (t + 1) * KT)
+            if i + 1 < count:
+                top = score(bufs[(i + 1) % 2], t, qaug, top)
+            e = jnp.exp2(bufs[i % 2][rows, :] - peak).astype(BF)
+            ebuf[i, rows, :] = e
+            acc = acc + dot(vaug[:, rows], e)
+            if t % 2 == 1:
+                out_copy(i, t - 1).start()
+        inv = 1.0 / acc[HEAD : HEAD + 1, :]
+        out = acc[0:HEAD, :] * inv
+        at = slice(i * QT, (i + 1) * QT)
+        o_ref[:, at] = out
+        inv_ref[:, at] = jnp.broadcast_to(inv, (8, QT))
+        rounded = out.astype(BF)
+        for p in range(per):
+            pay_ref[i * per + p, 0:HEAD, :] = rounded[:, p * LANES : (p + 1) * LANES]
+    low = HEAD // 2
+    lane = lane_iota((low, LANES))
+    left = lane < LANES // 2
+    outer_lanes = jnp.logical_or(lane < HALO, lane >= LANES - HALO)
+    for j in range(blocks):
+        after = pay_ref[min(j + 1, blocks - 1), 0:HEAD, :].astype(F32)
+        before = pay_ref[max(j - 1, 0), 0:HEAD, :].astype(F32)
+        first = jnp.where(left, after[0:low], before[0:low])
+        second = jnp.where(left, after[low:HEAD], before[low:HEAD])
+        second = pltpu.roll(second, LANES // 2, 1)
+        pay_ref[j, HEAD : HEAD + low, :] = jnp.where(outer_lanes, first, second).astype(BF)
+    for i in range(count):
+        for t in range(0, tiles, 2):
+            out_copy(i, t).wait()
 
 
 def fwd(length, x):
@@ -146,29 +165,28 @@
     steps = frames // QT
     return pl.pallas_call(
         fwd_kernel,
-        grid=(steps,),
         out_shape=(
             pltpu.HBM((steps, frames, QT), BF),
             pltpu.HBM((HEAD, frames), F32),
             jax.ShapeDtypeStruct((8, frames), F32),
             jax.ShapeDtypeStruct((blocks, HEAD + HEAD // 2, LANES), BF),
         ),
-        in_specs=[
-            pl.BlockSpec(memory_space=pltpu.SMEM),
-            pl.BlockSpec((blocks, 3 * HEAD, LANES), lambda i: (0, 0, 0)),
-        ],
+        in_specs=[pl.BlockSpec(memory_space=pltpu.SMEM), pl.BlockSpec()],
         out_specs=(
-            pl.BlockSpec((1, frames, QT), lambda i: (i, 0, 0)),
-            pl.BlockSpec((HEAD, QT), lambda i: (0, i)),
-            pl.BlockSpec((8, QT), lambda i: (0, i)),
-            pl.BlockSpec((blocks, HEAD + HEAD // 2, LANES), lambda i: (0, 0, 0)),
+            pl.BlockSpec(memory_space=pl.ANY),
+            pl.BlockSpec(),
+            pl.BlockSpec(),
+            pl.BlockSpec(),
         ),
         scratch_shapes=[
             pltpu.VMEM((frames, 2 * LANES), BF),
             pltpu.VMEM((HEAD + 16, frames), BF),
             pltpu.VMEM((frames, QT), F32),
+            pltpu.VMEM((frames, QT), F32),
+            pltpu.VMEM((steps, frames, QT), BF),
+            pltpu.SemaphoreType.DMA((steps, frames // KT // 2)),
         ],
-        compiler_params=params(20),
+        compiler_params=params(30),
         cost_estimate=cost(9e9, 1e7),
         name="attend",
     )(length, x)
@@ -176,9 +194,9 @@
 
 def conv_kernel_body(
     info_ref, att_ref, res_hbm, cot_hbm, left_hbm, right_hbm, w_hbm, taps_hbm,
-    out_ref, pay_ref, keep_ref, send_ref,
+    out_hbm, pay_ref, keep_hbm, send_hbm,
     lhs, block_in, masked, cot, grad, taps_sum, bg_ref,
-    res_ref, cot_ref, left_ref, right_ref, weight, taps_ref, proj, sems,
+    res_ref, cot_ref, left_ref, right_ref, weight, taps_ref, proj, out_ref, sems,
 ):
     rows, width = res_ref.shape
     cols = width // LANES
@@ -284,8 +302,20 @@
     taps_sum[HEADS - 1, pl.ds(cols, cols), :] = jnp.zeros((cols, LANES), F32)
     taps_sum[:, pl.ds(2 * cols, 8), :] = jnp.zeros((HEADS, 8, LANES), F32)
     half = width // 2
-    keep_ref[...] = bg_ref[:, pl.ds(pl.multiple_of(zbit * half, LANES), half)]
-    send_ref[...] = bg_ref[:, pl.ds(pl.multiple_of((1 - zbit) * half, LANES), half)]
+    mine = pl.ds(pl.multiple_of(zbit * half, LANES), half)
+    other = pl.ds(pl.multiple_of((1 - zbit) * half, LANES), half)
+    stores = [
+        pltpu.make_async_copy(src, dst, sems.at[pieces + 5 + n])
+        for n, (src, dst) in enumerate(
+            (
+                (bg_ref.at[:, other], send_hbm),
+                (bg_ref.at[:, mine], keep_hbm),
+                (out_ref, out_hbm),
+            )
+        )
+    ]
+    for store in stores:
+        store.start()
     bg = bg_ref[...]
     for h in range(0, HEADS, 2):
         mixed = lax.dot_general(
@@ -295,6 +325,8 @@
         pay_ref[h, 0:HEAD, :] = mixed[0:HEAD]
         pay_ref[h + 1, 0:HEAD, :] = mixed[HEAD : 2 * HEAD]
     pay_ref[:, HEAD:LANES, :] = taps_sum[...].astype(BF)
+    for store in stores:
+        store.wait()
 
 
 def conv(info, att, res, cot, left, right, w, taps):
@@ -305,7 +337,7 @@
     return pl.pallas_call(
         conv_kernel_body,
         out_shape=(
-            jax.ShapeDtypeStruct((rows, width), BF),
+            pltpu.HBM((rows, width), BF),
             pltpu.HBM((HEADS, LANES, LANES), BF),
             pltpu.HBM((rows, width // 2), BF),
             pltpu.HBM((rows, width // 2), BF),
@@ -313,7 +345,12 @@
         in_specs=[pl.BlockSpec(memory_space=pltpu.SMEM)]
         + [vm]
         + [pl.BlockSpec(memory_space=pl.ANY)] * 6,
-        out_specs=(vm,) * 4,
+        out_specs=(
+            pl.BlockSpec(memory_space=pl.ANY),
+            vm,
+            pl.BlockSpec(memory_space=pl.ANY),
+            pl.BlockSpec(memory_space=pl.ANY),
+        ),
         scratch_shapes=[
             pltpu.VMEM((span, width), BF),
             pltpu.VMEM((cols, span, LANES), F32),
@@ -329,7 +366,8 @@
             pltpu.VMEM((width, width), BF),
             pltpu.VMEM((TAPS, width), F32),
             pltpu.VMEM((span, 2 * LANES), F32),
-            pltpu.SemaphoreType.DMA((cols // 2 + 5,)),
+            pltpu.VMEM((rows, width), BF),
+            pltpu.SemaphoreType.DMA((cols // 2 + 8,)),
         ],
         compiler_params=params(20),
         cost_estimate=cost(9e9, 1e7),
@@ -505,7 +543,7 @@
 
 
 def pack_kernel(info_ref, x_ref, *refs):
-    outs, buf = refs[:GROUP], refs[GROUP]
+    keep_ref, send_ref, buf = refs
     cols = x_ref.shape[1] // HEAD
     below = cols * HEAD
     for r in range(HEAD // 16):
@@ -520,8 +558,9 @@
     for k in range(GROUP):
         j = jnp.bitwise_xor(info_ref[4], k)
         taps = [x_ref[2 * j + e, below : below + 32, :].astype(F32)[0:24] for e in range(2)]
-        rest = jnp.zeros((outs[k].shape[0] - share - 48, LANES), F32)
-        outs[k][...] = jnp.concatenate(
+        rest = jnp.zeros((LANES - share - 48, LANES), F32)
+        out = send_ref if k % 2 else keep_ref
+        out[k // 2] = jnp.concatenate(
             [buf[pl.ds(pl.multiple_of(share * j, 8), share), :]] + taps + [rest], axis=0
         ).astype(BF)
 
@@ -530,13 +569,28 @@
     units = x.shape[1] // HEAD * HEAD * 2
     return pl.pallas_call(
         pack_kernel,
-        out_shape=(pltpu.HBM((LANES, LANES), BF),) * GROUP,
+        out_shape=(pltpu.HBM((GROUP // 2, LANES, LANES), BF),) * 2,
         in_specs=[pl.BlockSpec(memory_space=pltpu.SMEM), pl.BlockSpec()],
         scratch_shapes=[pltpu.VMEM((units, LANES), F32)],
         compiler_params=params(12),
         cost_estimate=cost(1e6, 3e6),
         name="pack",
     )(info, x)
+
+
+def merge_kernel(a_ref, b_ref, *outs):
+    for k, out in enumerate(outs):
+        out[...] = (a_ref[k].astype(F32) + b_ref[k].astype(F32)).astype(BF)
+
+
+def merge(a, b):
+    return pl.pallas_call(
+        merge_kernel,
+        out_shape=(pltpu.HBM(a.shape[1:], BF),) * a.shape[0],
+        compiler_params=params(8),
+        cost_estimate=cost(1e6, 1e6),
+        name="merge",
+    )(a, b)
 
 
 def total_kernel(*refs):
@@ -646,7 +700,10 @@
     payload, partial = lax.optimization_barrier((payload, partial))
     back = exchange(payload, "seq")
     packed = pack(info, partial)
-    packed = [packed[0]] + [lax.ppermute(packed[k], "dp", hop(k)) for k in range(1, GROUP)]
+    packed = merge(in_hbm(packed[0]), lax.ppermute(packed[1], "dp", hop(1)))
+    packed = [in_hbm(packed[0])] + [
+        lax.ppermute(packed[k], "dp", hop(2 * k)) for k in range(1, GROUP // 2)
+    ]
     summed, back = lax.optimization_barrier((total(packed, batch), back))
     final = exchange(summed, "dp")
     query_grad, key_grad, value_grad = post(back)

time: 174 us -> 177 us (1.017)
  waiting for transfers between devices: 58.1 us -> 70.1 us
  starting transfers between devices: 67.4 us -> 57.5 us
    ppermute x7 -> x4, waiting for transfers between devices: 9.37 us -> 21.5 us  [the longest x1 15.2 us: shards(): packed = merge(in_hbm(packed[0]), lax.ppermute(packed[1], 'dp', hop(1)))]
    ppermute x7 -> x4, starting transfers between devices: 19.1 us -> 9.23 us  [the longest x3 8.55 us: shards(): lax.ppermute(packed[k], 'dp', hop(2 * k))]
    pallas_call x3 -> x4, Pallas kernels: 22.9 us -> 23.6 us  [the longest x1 12.1 us: conv(): pl.pallas_call(conv_kernel_body, out_shape=(pltpu.HBM((rows, width), BF),...]
  transfers between devices with their start and end apart: 21 -> 18, of which waited for: 10 -> 10; matrix products, arithmetic and copies ran while one was open for 0% -> 0% of each run, Pallas kernels for 18% -> 19%
where the time goes in v4:
time: 177 us; the launch traced here: 176 us
  waiting for transfers between devices  70.1 us (40%)
  starting transfers between devices  57.5 us (32%)
  Pallas kernels  45.8 us (26%)
    all_to_all x6, starting transfers between devices, exchange(): lax.all_to_all(x, axis, split_axis=0, concat_axis=0, tiled=True, axis_ind...  38.2 us
    all_to_all x6, waiting for transfers between devices, exchange(): lax.all_to_all(x, axis, split_axis=0, concat_axis=0, tiled=True, axis_ind...  29.5 us
    ppermute x1, waiting for transfers between devices, shards(): packed = merge(in_hbm(packed[0]), lax.ppermute(packed[1], 'dp', hop(1)))  15.2 us
    pallas_call x1, Pallas kernels, conv(): pl.pallas_call(conv_kernel_body, out_shape=(pltpu.HBM((rows, width), BF),...  12.1 us
    pallas_call x1, Pallas kernels, bwd(): pl.pallas_call(bwd_kernel, grid=(steps,), out_shape=pltpu.HBM((blocks, 3...  11.8 us
    ppermute x1, waiting for transfers between devices, shards(): left = lax.ppermute(edge_up, 'seq', up)  11.2 us
    pallas_call x1, Pallas kernels, fwd(): pl.pallas_call(fwd_kernel, out_shape=(pltpu.HBM((steps, frames, QT), BF),...  8.57 us
    ppermute x3, starting transfers between devices, shards(): lax.ppermute(packed[k], 'dp', hop(2 * k))  8.55 us
  transfers between devices with their start and end apart: 18, of which 10 were waited for; matrix products, arithmetic and copies ran while one was open for 0% of the time, Pallas kernels for 19%

profile of v4, /device:TPU:2, one launch (start us, length us, event | category | flops | bytes accessed | tf_op | source)
XLA Modules:
  0.0 175.9 jit_solution(12273391620751296978)
XLA Ops:
  0.6 2.6 %pre.1 = (bf16[16,288,128]{2,1,0:T(8,128)(2,1)}, bf16[64,1536]{1,0:T(8,128)(2,1)S(1)}, bf16[64,1536]{1,0:T(8,128)(2,1)S(1)}) custom-call(bf16[128,1536]{1,0:T(8,128)(2,1)} %bitcast.13, bf16[128,1536]{1,0:T(8,128)(2,1)} %bitcast.14, bf16[128,1536]{1,0:T(8,128)(2,1)} %bitcast.15, bf16[128,1536]{1,0:T(8,128)(2,1)} %bitcast.16, bf16[128,1536]{1,0:T(8,128)(2,1)} %bitcast.18), custom_call_target="tpu_custom_call" | custom-call | flops 1000000 | bytes 3000000 | tf_op jit(solution)/shard_map/pre/pallas_call | solution.py:71
  3.2 7.5 %all-to-all-start = ((bf16[16,288,128]{2,1,0:T(8,128)(2,1)}), bf16[16,288,128]{2,1,0:T(8,128)(2,1)S(1)}, u32[]{:S(2)}, u32[]{:S(2)}) async-start(bf16[16,288,128]{2,1,0:T(8,128)(2,1)} %get-tuple-element.37), calls=%async_computation | async-start | bytes 2359296 | tf_op jit(solution)/shard_map/all_to_all | solution.py:651
  10.7 2.0 %collective-permute-start = (bf16[64,1536]{1,0:T(8,128)(2,1)S(1)}, bf16[64,1536]{1,0:T(8,128)(2,1)S(1)}, u32[]{:S(2)}, u32[]{:S(2)}) collective-permute-start(bf16[64,1536]{1,0:T(8,128)(2,1)S(1)} %get-tuple-element.38), channel_id=1, source_target_pairs={{0,1},{1,2},{2,3},{3,4},{4,5},{5,6},{6,7},{7,8},{8,9},{9,10},{10,1... | collective-permute-start | bytes 589832 | tf_op jit(solution)/shard_map/ppermute | solution.py:677
  12.7 3.5 %collective-permute-start.1 = (bf16[64,1536]{1,0:T(8,128)(2,1)S(1)}, bf16[64,1536]{1,0:T(8,128)(2,1)S(1)}, u32[]{:S(2)}, u32[]{:S(2)}) collective-permute-start(bf16[64,1536]{1,0:T(8,128)(2,1)S(1)} %get-tuple-element.39), channel_id=1, source_target_pairs={{1,0},{2,1},{3,2},{4,3},{5,4},{6,5},{7,6},{8,7},{9,8},{10,9},{11,1... | collective-permute-start | bytes 589832 | tf_op jit(solution)/shard_map/ppermute | solution.py:678
  16.9 11.2 %collective-permute-done.left_hbm = bf16[64,1536]{1,0:T(8,128)(2,1)S(1)} collective-permute-done((bf16[64,1536]{1,0:T(8,128)(2,1)S(1)}, bf16[64,1536]{1,0:T(8,128)(2,1)S(1)}, u32[]{:S(2)}, u32[]{:S(2)}) %collective-permute-start) | collective-permute-done | bytes 196640 | tf_op jit(solution)/shard_map/ppermute | solution.py:677
  28.1 8.6 %attend.1 = (bf16[4,2048,512]{2,1,0:T(8,128)(2,1)}, f32[96,2048]{1,0:T(8,128)}, f32[8,2048]{1,0:T(8,128)S(1)}, bf16[16,144,128]{2,1,0:T(8,128)(2,1)}) custom-call(s32[1]{0:T(128)S(6)} %copy.16.len_ref, bf16[16,288,128]{2,1,0:T(8,128)(2,1)S(1)} %all-to-all-done.x_ref), custom_call_target="tpu_custom_call" | custom-call | flops 8999999488 | bytes 10000000 | tf_op jit(solution)/shard_map/attend/pallas_call | solution.py:166
  36.7 6.4 %all-to-all-start.1 = ((bf16[16,144,128]{2,1,0:T(8,128)(2,1)}), bf16[16,144,128]{2,1,0:T(8,128)(2,1)S(1)}, u32[]{:S(2)}, u32[]{:S(2)}) async-start(bf16[16,144,128]{2,1,0:T(8,128)(2,1)} %get-tuple-element.41), calls=%async_computation.1 | async-start | bytes 1179648 | tf_op jit(solution)/shard_map/all_to_all | solution.py:651
  43.3 9.1 %all-to-all-done.1.att_ref.refs_0_ = bf16[16,144,128]{2,1,0:T(8,128)(2,1)S(1)} async-done(((bf16[16,144,128]{2,1,0:T(8,128)(2,1)}), bf16[16,144,128]{2,1,0:T(8,128)(2,1)S(1)}, u32[]{:S(2)}, u32[]{:S(2)}) %all-to-all-start.1) | async-done | bytes 589856 | tf_op jit(solution)/shard_map/all_to_all | solution.py:651
  52.4 1.9 %collective-permute-start.2 = (bf16[16,144,128]{2,1,0:T(8,128)(2,1)S(1)}, bf16[16,144,128]{2,1,0:T(8,128)(2,1)S(1)}, u32[]{:S(2)}, u32[]{:S(2)}) collective-permute-start(bf16[16,144,128]{2,1,0:T(8,128)(2,1)S(1)} %all-to-all-done.1.att_ref.refs_0_), channel_id=1, source_target_pairs={{0,32},{16,48},{32,0},{48,16},{64,96},{80,112},{96,64},{112,80},{1... | collective-permute-start | bytes 1769480 | tf_op jit(solution)/shard_map/ppermute | solution.py:682
  55.1 12.1 %convolve.1 = (bf16[128,1536]{1,0:T(8,128)(2,1)}, bf16[16,128,128]{2,1,0:T(8,128)(2,1)}, bf16[128,768]{1,0:T(8,128)(2,1)}, bf16[128,768]{1,0:T(8,128)(2,1)}) custom-call(s32[5]{0:T(128)S(1)} %stack.19.info_ref, bf16[16,144,128]{2,1,0:T(8,128)(2,1)S(1)} %all-to-all-done.1.att_ref.refs_0_, bf16[128,1536]{1,0:T(8,128)(2,1)} %bitcast.17, ...), custom_call_target="tpu_custom_call" | custom-call | flops 8999999488 | bytes 10000000 | tf_op jit(solution)/shard_map/convolve/pallas_call | solution.py:337
  67.2 1.1 collective-permute-done.2.refs_2_
  68.4 6.2 %all-to-all-start.2 = ((bf16[16,128,128]{2,1,0:T(8,128)(2,1)}), bf16[16,128,128]{2,1,0:T(8,128)(2,1)S(1)}, u32[]{:S(2)}, u32[]{:S(2)}) async-start(bf16[16,128,128]{2,1,0:T(8,128)(2,1)} %get-tuple-element.46), calls=%async_computation.2 | async-start | bytes 1048576 | tf_op jit(solution)/shard_map/all_to_all | solution.py:651
  74.6 1.7 collective-permute-start.6
  76.3 5.4 %collective-permute-done.6.refs_6_ = bf16[128,768]{1,0:T(8,128)(2,1)S(1)} collective-permute-done((bf16[128,768]{1,0:T(8,128)(2,1)}, bf16[128,768]{1,0:T(8,128)(2,1)S(1)}, u32[]{:S(2)}, u32[]{:S(2)}) %collective-permute-start.6) | collective-permute-done | bytes 196640 | tf_op jit(solution)/shard_map/ppermute | solution.py:692
  81.8 1.4 collective-permute-done.7.refs_7_
  83.2 0.9 copy-done
  84.1 3.4 %outer.1.w_ref = bf16[16,320,128]{2,1,0:T(8,128)(2,1)} custom-call(s32[5]{0:T(128)S(1)} %stack.19.info_ref, bf16[16,144,128]{2,1,0:T(8,128)(2,1)S(1)} %all-to-all-done.1.att_ref.refs_0_, bf16[16,144,128]{2,1,0:T(8,128)(2,1)} %collective-permute-done.3.refs_1_, bf16[16,144,128]{2,1,0:T(8,128)(2,1)S(1)} %collective-permute-done.2.refs_2_, ...), custom_call_target="tpu_custom_call" | custom-call | flops 1000000000 | bytes 4000000 | tf_op jit(solution)/shard_map/outer/pallas_call | solution.py:403
  88.3 7.3 %all-to-all-start.3 = ((bf16[16,320,128]{2,1,0:T(8,128)(2,1)}), bf16[16,320,128]{2,1,0:T(8,128)(2,1)S(1)}, u32[]{:S(2)}, u32[]{:S(2)}) async-start(bf16[16,320,128]{2,1,0:T(8,128)(2,1)} %tail.1), calls=%async_computation.3 | async-start | bytes 2621440 | tf_op jit(solution)/shard_map/all_to_all | solution.py:651
  95.6 11.8 %attend_back.1 = bf16[16,288,128]{2,1,0:T(8,128)(2,1)} custom-call(bf16[16,288,128]{2,1,0:T(8,128)(2,1)S(1)} %all-to-all-done.x_ref, bf16[16,128,128]{2,1,0:T(8,128)(2,1)S(1)} %all-to-all-done.2.g_ref, bf16[4,2048,512]{2,1,0:T(8,128)(2,1)} %get-tuple-element.47.e_ref, f32[96,2048]{1,0:T(8,128)} %get-tuple-element.48.o_ref, ...), custom_call_target="tpu_custom_call" | custom-call | flops 20000000000 | bytes 10000000 | tf_op jit(solution)/shard_map/attend_back/pallas_call | solution.py:501
  107.4 6.0 %all-to-all-done.3.x_ref = bf16[16,320,128]{2,1,0:T(8,128)(2,1)S(1)} async-done(((bf16[16,320,128]{2,1,0:T(8,128)(2,1)}), bf16[16,320,128]{2,1,0:T(8,128)(2,1)S(1)}, u32[]{:S(2)}, u32[]{:S(2)}) %all-to-all-start.3) | async-done | bytes 1310752 | tf_op jit(solution)/shard_map/all_to_all | solution.py:651
  113.4 6.6 %all-to-all-start.4 = ((bf16[16,288,128]{2,1,0:T(8,128)(2,1)}), bf16[16,288,128]{2,1,0:T(8,128)(2,1)S(1)}, u32[]{:S(2)}, u32[]{:S(2)}) async-start(bf16[16,288,128]{2,1,0:T(8,128)(2,1)} %attend_back.1), calls=%async_computation.4 | async-start | bytes 2359296 | tf_op jit(solution)/shard_map/all_to_all | solution.py:651
  120.0 1.4 pack.1
  122.1 15.2 %collective-permute-done.8.b_ref = bf16[4,128,128]{2,1,0:T(8,128)(2,1)S(1)} collective-permute-done((bf16[4,128,128]{2,1,0:T(8,128)(2,1)}, bf16[4,128,128]{2,1,0:T(8,128)(2,1)S(1)}, u32[]{:S(2)}, u32[]{:S(2)}) %collective-permute-start.8) | collective-permute-done | bytes 131104 | tf_op jit(solution)/shard_map/ppermute | solution.py:703
  137.4 1.6 merge.1
  138.9 3.3 %collective-permute-start.9 = (bf16[128,128]{1,0:T(8,128)(2,1)}, bf16[128,128]{1,0:T(8,128)(2,1)S(1)}, u32[]{:S(2)}, u32[]{:S(2)}) collective-permute-start(bf16[128,128]{1,0:T(8,128)(2,1)} %get-tuple-element.57), channel_id=1, source_target_pairs={{0,64},{16,80},{32,96},{48,112},{64,0},{80,16},{96,32},{112,48},{1... | collective-permute-start | bytes 98312 | tf_op jit(solution)/shard_map/ppermute | solution.py:705
  142.2 5.3 %collective-permute-start.10 = (bf16[128,128]{1,0:T(8,128)(2,1)}, bf16[128,128]{1,0:T(8,128)(2,1)S(1)}, u32[]{:S(2)}, u32[]{:S(2)}) collective-permute-start(bf16[128,128]{1,0:T(8,128)(2,1)} %get-tuple-element.58), channel_id=1, source_target_pairs={{0,128},{16,144},{32,160},{48,176},{64,192},{80,208},{96,224},{112... | collective-permute-start | bytes 98312 | tf_op jit(solution)/shard_map/ppermute | solution.py:705
  147.5 2.7 %collective-permute-done.10.refs_2_ = bf16[128,128]{1,0:T(8,128)(2,1)S(1)} collective-permute-done((bf16[128,128]{1,0:T(8,128)(2,1)}, bf16[128,128]{1,0:T(8,128)(2,1)S(1)}, u32[]{:S(2)}, u32[]{:S(2)}) %collective-permute-start.10) | collective-permute-done | bytes 32800 | tf_op jit(solution)/shard_map/ppermute | solution.py:705
  150.2 3.5 %collective-permute-done.11.refs_3_ = bf16[128,128]{1,0:T(8,128)(2,1)S(1)} collective-permute-done((bf16[128,128]{1,0:T(8,128)(2,1)}, bf16[128,128]{1,0:T(8,128)(2,1)S(1)}, u32[]{:S(2)}, u32[]{:S(2)}) %collective-permute-start.11) | collective-permute-done | bytes 32800 | tf_op jit(solution)/shard_map/ppermute | solution.py:705
  153.7 1.6 total.1
  155.3 4.1 %all-to-all-start.5 = ((bf16[16,128,128]{2,1,0:T(8,128)(2,1)}), bf16[16,128,128]{2,1,0:T(8,128)(2,1)S(1)}, u32[]{:S(2)}, u32[]{:S(2)}) async-start(bf16[16,128,128]{2,1,0:T(8,128)(2,1)} %total.1), calls=%async_computation.5 | async-start | bytes 1048576 | tf_op jit(solution)/shard_map/all_to_all | solution.py:651
  159.4 1.2 post.1
  160.6 14.4 %all-to-all-done.5.x_ref = bf16[16,128,128]{2,1,0:T(8,128)(2,1)S(1)} async-done(((bf16[16,128,128]{2,1,0:T(8,128)(2,1)}), bf16[16,128,128]{2,1,0:T(8,128)(2,1)S(1)}, u32[]{:S(2)}, u32[]{:S(2)}) %all-to-all-start.5) | async-done | bytes 524320 | tf_op jit(solution)/shard_map/all_to_all | solution.py:651
  (22 shorter events, 3.5 us)
Async XLA Ops:
  3.2 24.9 %all-to-all-start = ((bf16[16,288,128]{2,1,0:T(8,128)(2,1)}), bf16[16,288,128]{2,1,0:T(8,128)(2,1)S(1)}, u32[]{:S(2)}, u32[]{:S(2)}) async-start(bf16[16,288,128]{2,1,0:T(8,128)(2,1)} %get-tuple-element.37), calls=%async_computation | async-start | bytes 2359296 | tf_op jit(solution)/shard_map/all_to_all | solution.py:651
  10.7 17.4 %collective-permute-start = (bf16[64,1536]{1,0:T(8,128)(2,1)S(1)}, bf16[64,1536]{1,0:T(8,128)(2,1)S(1)}, u32[]{:S(2)}, u32[]{:S(2)}) collective-permute-start(bf16[64,1536]{1,0:T(8,128)(2,1)S(1)} %get-tuple-element.38), channel_id=1, source_target_pairs={{0,1},{1,2},{2,3},{3,4},{4,5},{5,6},{6,7},{7,8},{8,9},{9,10},{10,1... | collective-permute-start | bytes 589832 | tf_op jit(solution)/shard_map/ppermute | solution.py:677
  12.7 15.4 %collective-permute-start.1 = (bf16[64,1536]{1,0:T(8,128)(2,1)S(1)}, bf16[64,1536]{1,0:T(8,128)(2,1)S(1)}, u32[]{:S(2)}, u32[]{:S(2)}) collective-permute-start(bf16[64,1536]{1,0:T(8,128)(2,1)S(1)} %get-tuple-element.39), channel_id=1, source_target_pairs={{1,0},{2,1},{3,2},{4,3},{5,4},{6,5},{7,6},{8,7},{9,8},{10,9},{11,1... | collective-permute-start | bytes 589832 | tf_op jit(solution)/shard_map/ppermute | solution.py:678
  28.1 8.6 %copy-start.1 = (bf16[64,1536]{1,0:T(8,128)(2,1)}, bf16[64,1536]{1,0:T(8,128)(2,1)S(1)}, u32[]{:S(2)}) copy-start(bf16[64,1536]{1,0:T(8,128)(2,1)S(1)} %collective-permute-done.left_hbm) | copy-start | bytes 589828
  28.1 8.6 %copy-start.2 = (bf16[64,1536]{1,0:T(8,128)(2,1)}, bf16[64,1536]{1,0:T(8,128)(2,1)S(1)}, u32[]{:S(2)}) copy-start(bf16[64,1536]{1,0:T(8,128)(2,1)S(1)} %collective-permute-done.1.right_hbm) | copy-start | bytes 589828
  36.7 15.7 %all-to-all-start.1 = ((bf16[16,144,128]{2,1,0:T(8,128)(2,1)}), bf16[16,144,128]{2,1,0:T(8,128)(2,1)S(1)}, u32[]{:S(2)}, u32[]{:S(2)}) async-start(bf16[16,144,128]{2,1,0:T(8,128)(2,1)} %get-tuple-element.41), calls=%async_computation.1 | async-start | bytes 1179648 | tf_op jit(solution)/shard_map/all_to_all | solution.py:651
  52.4 15.9 %collective-permute-start.2 = (bf16[16,144,128]{2,1,0:T(8,128)(2,1)S(1)}, bf16[16,144,128]{2,1,0:T(8,128)(2,1)S(1)}, u32[]{:S(2)}, u32[]{:S(2)}) collective-permute-start(bf16[16,144,128]{2,1,0:T(8,128)(2,1)S(1)} %all-to-all-done.1.att_ref.refs_0_), channel_id=1, source_target_pairs={{0,32},{16,48},{32,0},{48,16},{64,96},{80,112},{96,64},{112,80},{1... | collective-permute-start | bytes 1769480 | tf_op jit(solution)/shard_map/ppermute | solution.py:682
  54.3 28.9 %collective-permute-start.3 = (bf16[16,144,128]{2,1,0:T(8,128)(2,1)S(1)}, bf16[16,144,128]{2,1,0:T(8,128)(2,1)}, u32[]{:S(2)}, u32[]{:S(2)}) collective-permute-start(bf16[16,144,128]{2,1,0:T(8,128)(2,1)S(1)} %all-to-all-done.1.att_ref.refs_0_), channel_id=1, source_target_pairs={{0,1},{1,0},{2,3},{3,2},{4,5},{5,4},{6,7},{7,6},{8,9},{9,8},{10,11... | collective-permute-start | bytes 1769480 | tf_op jit(solution)/shard_map/ppermute | solution.py:683
  68.3 14.9 %collective-permute-start.4 = (bf16[16,144,128]{2,1,0:T(8,128)(2,1)S(1)}, bf16[16,144,128]{2,1,0:T(8,128)(2,1)}, u32[]{:S(2)}, u32[]{:S(2)}) collective-permute-start(bf16[16,144,128]{2,1,0:T(8,128)(2,1)S(1)} %collective-permute-done.2.refs_2_), channel_id=1, source_target_pairs={{0,1},{1,0},{2,3},{3,2},{4,5},{5,4},{6,7},{7,6},{8,9},{9,8},{10,11... | collective-permute-start | bytes 1769480 | tf_op jit(solution)/shard_map/ppermute | solution.py:690
  68.4 19.1 %all-to-all-start.2 = ((bf16[16,128,128]{2,1,0:T(8,128)(2,1)}), bf16[16,128,128]{2,1,0:T(8,128)(2,1)S(1)}, u32[]{:S(2)}, u32[]{:S(2)}) async-start(bf16[16,128,128]{2,1,0:T(8,128)(2,1)} %get-tuple-element.46), calls=%async_computation.2 | async-start | bytes 1048576 | tf_op jit(solution)/shard_map/all_to_all | solution.py:651
  74.6 7.2 %collective-permute-start.6 = (bf16[128,768]{1,0:T(8,128)(2,1)}, bf16[128,768]{1,0:T(8,128)(2,1)S(1)}, u32[]{:S(2)}, u32[]{:S(2)}) collective-permute-start(bf16[128,768]{1,0:T(8,128)(2,1)} %get-tuple-element.52), channel_id=1, source_target_pairs={{0,32},{16,48},{32,0},{48,16},{64,96},{80,112},{96,64},{112,80},{1... | collective-permute-start | bytes 589832 | tf_op jit(solution)/shard_map/ppermute | solution.py:692
  76.3 5.4 %collective-permute-start.5 = (bf16[128,768]{1,0:T(8,128)(2,1)}, bf16[128,768]{1,0:T(8,128)(2,1)S(1)}, u32[]{:S(2)}, u32[]{:S(2)}) collective-permute-start(bf16[128,768]{1,0:T(8,128)(2,1)} %get-tuple-element.51.refs_4_), channel_id=1, source_target_pairs={{0,1},{1,0},{2,3},{3,2},{4,5},{5,4},{6,7},{7,6},{8,9},{9,8},{10,11... | collective-permute-start | bytes 589832 | tf_op jit(solution)/shard_map/ppermute | solution.py:693
  81.8 1.4 collective-permute-start.7
  83.2 0.9 copy-start
  88.3 25.0 %all-to-all-start.3 = ((bf16[16,320,128]{2,1,0:T(8,128)(2,1)}), bf16[16,320,128]{2,1,0:T(8,128)(2,1)S(1)}, u32[]{:S(2)}, u32[]{:S(2)}) async-start(bf16[16,320,128]{2,1,0:T(8,128)(2,1)} %tail.1), calls=%async_computation.3 | async-start | bytes 2621440 | tf_op jit(solution)/shard_map/all_to_all | solution.py:651
  113.4 41.9 %all-to-all-start.4 = ((bf16[16,288,128]{2,1,0:T(8,128)(2,1)}), bf16[16,288,128]{2,1,0:T(8,128)(2,1)S(1)}, u32[]{:S(2)}, u32[]{:S(2)}) async-start(bf16[16,288,128]{2,1,0:T(8,128)(2,1)} %attend_back.1), calls=%async_computation.4 | async-start | bytes 2359296 | tf_op jit(solution)/shard_map/all_to_all | solution.py:651
  121.4 15.9 %collective-permute-start.8 = (bf16[4,128,128]{2,1,0:T(8,128)(2,1)}, bf16[4,128,128]{2,1,0:T(8,128)(2,1)S(1)}, u32[]{:S(2)}, u32[]{:S(2)}) collective-permute-start(bf16[4,128,128]{2,1,0:T(8,128)(2,1)} %get-tuple-element.55), channel_id=1, source_target_pairs={{0,16},{16,0},{32,48},{48,32},{64,80},{80,64},{96,112},{112,96},{1... | collective-permute-start | bytes 393224 | tf_op jit(solution)/shard_map/ppermute | solution.py:703
  138.9 8.6 %collective-permute-start.9 = (bf16[128,128]{1,0:T(8,128)(2,1)}, bf16[128,128]{1,0:T(8,128)(2,1)S(1)}, u32[]{:S(2)}, u32[]{:S(2)}) collective-permute-start(bf16[128,128]{1,0:T(8,128)(2,1)} %get-tuple-element.57), channel_id=1, source_target_pairs={{0,64},{16,80},{32,96},{48,112},{64,0},{80,16},{96,32},{112,48},{1... | collective-permute-start | bytes 98312 | tf_op jit(solution)/shard_map/ppermute | solution.py:705
  142.2 8.0 %collective-permute-start.10 = (bf16[128,128]{1,0:T(8,128)(2,1)}, bf16[128,128]{1,0:T(8,128)(2,1)S(1)}, u32[]{:S(2)}, u32[]{:S(2)}) collective-permute-start(bf16[128,128]{1,0:T(8,128)(2,1)} %get-tuple-element.58), channel_id=1, source_target_pairs={{0,128},{16,144},{32,160},{48,176},{64,192},{80,208},{96,224},{112... | collective-permute-start | bytes 98312 | tf_op jit(solution)/shard_map/ppermute | solution.py:705
  147.5 6.2 %collective-permute-start.11 = (bf16[128,128]{1,0:T(8,128)(2,1)}, bf16[128,128]{1,0:T(8,128)(2,1)S(1)}, u32[]{:S(2)}, u32[]{:S(2)}) collective-permute-start(bf16[128,128]{1,0:T(8,128)(2,1)} %get-tuple-element.59), channel_id=1, source_target_pairs={{0,192},{16,208},{32,224},{48,240},{64,128},{80,144},{96,160},{112... | collective-permute-start | bytes 98312 | tf_op jit(solution)/shard_map/ppermute | solution.py:705
  155.3 19.7 %all-to-all-start.5 = ((bf16[16,128,128]{2,1,0:T(8,128)(2,1)}), bf16[16,128,128]{2,1,0:T(8,128)(2,1)S(1)}, u32[]{:S(2)}, u32[]{:S(2)}) async-start(bf16[16,128,128]{2,1,0:T(8,128)(2,1)} %total.1), calls=%async_computation.5 | async-start | bytes 1048576 | tf_op jit(solution)/shard_map/all_to_all | solution.py:651

commit v5 on v4

--- a/solution.py
+++ b/solution.py
@@ -13,6 +13,7 @@
 TAPS = 31
 HALF = 15
 HALO = 32
+NEAR = 16
 QT = 512
 KT = 256
 BF = jnp.bfloat16
@@ -47,12 +48,12 @@
         for i, ref in enumerate((q_hbm, k_hbm, v_hbm))
     ]
     edges = [
-        pltpu.make_async_copy(ref.at[pl.ds(lo, HALO)], out.at[pl.ds(at, HALO)], sems.at[n])
-        for n, ref, lo, out, at in (
-            (3, res_hbm, rows - HALO, up_ref, 0),
-            (4, cot_hbm, rows - HALO, up_ref, HALO),
-            (5, res_hbm, 0, down_ref, 0),
-            (6, cot_hbm, 0, down_ref, HALO),
+        pltpu.make_async_copy(ref.at[pl.ds(lo, size)], out.at[pl.ds(at, size)], sems.at[n])
+        for n, ref, lo, size, out, at in (
+            (3, res_hbm, rows - HALO, HALO, up_ref, 0),
+            (4, cot_hbm, rows - NEAR, NEAR, up_ref, HALO),
+            (5, res_hbm, 0, HALO, down_ref, 0),
+            (6, cot_hbm, 0, NEAR, down_ref, HALO),
         )
     ]
     for copy in loads + edges:
@@ -67,7 +68,7 @@
 
 
 def pre(q, k, v, res, cot):
-    edge = jax.ShapeDtypeStruct((2 * HALO, q.shape[1]), BF)
+    edge = jax.ShapeDtypeStruct((HALO + NEAR, q.shape[1]), BF)
     return pl.pallas_call(
         pre_kernel,
         out_shape=(jax.ShapeDtypeStruct((HEADS, 3 * HEAD, LANES), BF), edge, edge),
@@ -256,9 +257,13 @@
             block_in[c] = block
             masked[c] = jnp.where(valid, block, 0.0).astype(BF).astype(F32)
             cot[c] = jnp.concatenate(
-                [left_ref[HALO : 2 * HALO, at], cot_ref[:, at], right_ref[HALO : 2 * HALO, at]],
+                [
+                    left_ref[HALO : HALO + NEAR, at],
+                    cot_ref[:, at],
+                    right_ref[HALO : HALO + NEAR, at],
+                ],
                 axis=0,
-            ).astype(F32)[16 : 16 + mid, :]
+            ).astype(F32)
 
     for load in small:
         load.wait()
@@ -361,8 +366,8 @@
             pltpu.VMEM((rows, width), BF),
             pltpu.VMEM((rows, width), BF),
             pltpu.VMEM((rows, width), BF),
-            pltpu.VMEM((2 * HALO, width), BF),
-            pltpu.VMEM((2 * HALO, width), BF),
+            pltpu.VMEM((HALO + NEAR, width), BF),
+            pltpu.VMEM((HALO + NEAR, width), BF),
             pltpu.VMEM((width, width), BF),
             pltpu.VMEM((TAPS, width), F32),
             pltpu.VMEM((span, 2 * LANES), F32),
@@ -543,7 +548,7 @@
 
 
 def pack_kernel(info_ref, x_ref, *refs):
-    keep_ref, send_ref, buf = refs
+    outs, buf = refs[:-1], refs[-1]
     cols = x_ref.shape[1] // HEAD
     below = cols * HEAD
     for r in range(HEAD // 16):
@@ -559,8 +564,7 @@
         j = jnp.bitwise_xor(info_ref[4], k)
         taps = [x_ref[2 * j + e, below : below + 32, :].astype(F32)[0:24] for e in range(2)]
         rest = jnp.zeros((LANES - share - 48, LANES), F32)
-        out = send_ref if k % 2 else keep_ref
-        out[k // 2] = jnp.concatenate(
+        outs[k // 2][k % 2] = jnp.concatenate(
             [buf[pl.ds(pl.multiple_of(share * j, 8), share), :]] + taps + [rest], axis=0
         ).astype(BF)
 
@@ -569,7 +573,7 @@
     units = x.shape[1] // HEAD * HEAD * 2
     return pl.pallas_call(
         pack_kernel,
-        out_shape=(pltpu.HBM((GROUP // 2, LANES, LANES), BF),) * 2,
+        out_shape=(pltpu.HBM((2, LANES, LANES), BF),) * (GROUP // 2),
         in_specs=[pl.BlockSpec(memory_space=pltpu.SMEM), pl.BlockSpec()],
         scratch_shapes=[pltpu.VMEM((units, LANES), F32)],
         compiler_params=params(12),
@@ -578,19 +582,21 @@
     )(info, x)
 
 
-def merge_kernel(a_ref, b_ref, *outs):
-    for k, out in enumerate(outs):
-        out[...] = (a_ref[k].astype(F32) + b_ref[k].astype(F32)).astype(BF)
-
-
-def merge(a, b):
+def merge_kernel(*refs):
+    keep_ref, send_ref = refs[-2:]
+    both = sum([ref[...].astype(F32) for ref in refs[1:-2]], refs[0][...].astype(F32))
+    keep_ref[...] = both[0].astype(BF)
+    send_ref[...] = both[1].astype(BF)
+
+
+def merge(xs):
     return pl.pallas_call(
         merge_kernel,
-        out_shape=(pltpu.HBM(a.shape[1:], BF),) * a.shape[0],
+        out_shape=(pltpu.HBM(xs[0].shape[1:], BF),) * 2,
         compiler_params=params(8),
         cost_estimate=cost(1e6, 1e6),
         name="merge",
-    )(a, b)
+    )(*xs)
 
 
 def total_kernel(*refs):
@@ -693,17 +699,18 @@
     partner = lax.ppermute(keep, "seq", cores)
     both = lax.ppermute(level, "seq", cores)
     partial = outer(
-        info, (attended, att_core, att_level, att_both), (keep, partner, level, both)
+        info, (attended, att_core, att_level, att_both), (in_hbm(keep), partner, level, both)
     )
     partial = exchange(tail(grads, partial), "seq")
     payload = bwd(heads, grads, in_hbm(weights), in_hbm(mixed), inv)
     payload, partial = lax.optimization_barrier((payload, partial))
     back = exchange(payload, "seq")
     packed = pack(info, partial)
-    packed = merge(in_hbm(packed[0]), lax.ppermute(packed[1], "dp", hop(1)))
-    packed = [in_hbm(packed[0])] + [
+    level_parts = [in_hbm(packed[0])] + [
         lax.ppermute(packed[k], "dp", hop(2 * k)) for k in range(1, GROUP // 2)
     ]
+    keep, send = merge(level_parts)
+    packed = [in_hbm(keep), lax.ppermute(send, "dp", hop(1))]
     summed, back = lax.optimization_barrier((total(packed, batch), back))
     final = exchange(summed, "dp")
     query_grad, key_grad, value_grad = post(back)

time: 177 us -> 167 us (0.944)
  waiting for transfers between devices: 70.1 us -> 59.1 us
  starting transfers between devices: 57.5 us -> 59.4 us
    ppermute x1, waiting for transfers between devices: 15.2 us -> 3.45 us  [shards(): packed = [in_hbm(keep), lax.ppermute(send, 'dp', hop(1))]]
    all_to_all x6, starting transfers between devices: 38.2 us -> 40 us  [exchange(): lax.all_to_all(x, axis, split_axis=0, concat_axis=0, tiled=True, axis_ind...]
  transfers between devices with their start and end apart: 18 -> 18, of which waited for: 10 -> 10; matrix products, arithmetic and copies ran while one was open for 0% -> 0% of each run, Pallas kernels for 19% -> 20%
where the time goes in v5:
time: 167 us; the launch traced here: 166 us
  starting transfers between devices  59.4 us (36%)
  waiting for transfers between devices  59.1 us (35%)
  Pallas kernels  45.7 us (27%)
    all_to_all x6, starting transfers between devices, exchange(): lax.all_to_all(x, axis, split_axis=0, concat_axis=0, tiled=True, axis_ind...  40 us
    all_to_all x6, waiting for transfers between devices, exchange(): lax.all_to_all(x, axis, split_axis=0, concat_axis=0, tiled=True, axis_ind...  30.4 us
    pallas_call x1, Pallas kernels, conv(): pl.pallas_call(conv_kernel_body, out_shape=(pltpu.HBM((rows, width), BF),...  12 us
    pallas_call x1, Pallas kernels, bwd(): pl.pallas_call(bwd_kernel, grid=(steps,), out_shape=pltpu.HBM((blocks, 3...  11.8 us
    ppermute x1, waiting for transfers between devices, shards(): left = lax.ppermute(edge_up, 'seq', up)  10.7 us
    ppermute x3, starting transfers between devices, shards(): lax.ppermute(packed[k], 'dp', hop(2 * k))  8.56 us
    pallas_call x1, Pallas kernels, fwd(): pl.pallas_call(fwd_kernel, out_shape=(pltpu.HBM((steps, frames, QT), BF),...  8.55 us
    ppermute x3, waiting for transfers between devices, shards(): lax.ppermute(packed[k], 'dp', hop(2 * k))  6.58 us
  transfers between devices with their start and end apart: 18, of which 10 were waited for; matrix products, arithmetic and copies ran while one was open for 0% of the time, Pallas kernels for 20%

profile of v5, /device:TPU:2, one launch (start us, length us, event | category | flops | bytes accessed | tf_op | source)
XLA Modules:
  0.0 165.7 jit_solution(1927319391298543153)
XLA Ops:
  0.6 2.5 %pre.1 = (bf16[16,288,128]{2,1,0:T(8,128)(2,1)}, bf16[48,1536]{1,0:T(8,128)(2,1)S(1)}, bf16[48,1536]{1,0:T(8,128)(2,1)S(1)}) custom-call(bf16[128,1536]{1,0:T(8,128)(2,1)} %bitcast.13, bf16[128,1536]{1,0:T(8,128)(2,1)} %bitcast.14, bf16[128,1536]{1,0:T(8,128)(2,1)} %bitcast.15, bf16[128,1536]{1,0:T(8,128)(2,1)} %bitcast.16, bf16[128,1536]{1,0:T(8,128)(2,1)} %bitcast.18), custom_call_target="tpu_custom_call" | custom-call | flops 1000000 | bytes 3000000 | tf_op jit(solution)/shard_map/pre/pallas_call | solution.py:72
  3.2 7.5 %all-to-all-start = ((bf16[16,288,128]{2,1,0:T(8,128)(2,1)}), bf16[16,288,128]{2,1,0:T(8,128)(2,1)S(1)}, u32[]{:S(2)}, u32[]{:S(2)}) async-start(bf16[16,288,128]{2,1,0:T(8,128)(2,1)} %get-tuple-element.37), calls=%async_computation | async-start | bytes 2359296 | tf_op jit(solution)/shard_map/all_to_all | solution.py:657
  10.7 2.0 %collective-permute-start = (bf16[48,1536]{1,0:T(8,128)(2,1)S(1)}, bf16[48,1536]{1,0:T(8,128)(2,1)S(1)}, u32[]{:S(2)}, u32[]{:S(2)}) collective-permute-start(bf16[48,1536]{1,0:T(8,128)(2,1)S(1)} %get-tuple-element.38), channel_id=1, source_target_pairs={{0,1},{1,2},{2,3},{3,4},{4,5},{5,6},{6,7},{7,8},{8,9},{9,10},{10,1... | collective-permute-start | bytes 442376 | tf_op jit(solution)/shard_map/ppermute | solution.py:683
  12.7 3.5 %collective-permute-start.1 = (bf16[48,1536]{1,0:T(8,128)(2,1)S(1)}, bf16[48,1536]{1,0:T(8,128)(2,1)S(1)}, u32[]{:S(2)}, u32[]{:S(2)}) collective-permute-start(bf16[48,1536]{1,0:T(8,128)(2,1)S(1)} %get-tuple-element.39), channel_id=1, source_target_pairs={{1,0},{2,1},{3,2},{4,3},{5,4},{6,5},{7,6},{8,7},{9,8},{10,9},{11,1... | collective-permute-start | bytes 442376 | tf_op jit(solution)/shard_map/ppermute | solution.py:684
  16.9 10.7 %collective-permute-done.left_hbm = bf16[48,1536]{1,0:T(8,128)(2,1)S(1)} collective-permute-done((bf16[48,1536]{1,0:T(8,128)(2,1)S(1)}, bf16[48,1536]{1,0:T(8,128)(2,1)S(1)}, u32[]{:S(2)}, u32[]{:S(2)}) %collective-permute-start) | collective-permute-done | bytes 147488 | tf_op jit(solution)/shard_map/ppermute | solution.py:683
  27.6 8.6 %attend.1 = (bf16[4,2048,512]{2,1,0:T(8,128)(2,1)}, f32[96,2048]{1,0:T(8,128)}, f32[8,2048]{1,0:T(8,128)S(1)}, bf16[16,144,128]{2,1,0:T(8,128)(2,1)}) custom-call(s32[1]{0:T(128)S(6)} %copy.16.len_ref, bf16[16,288,128]{2,1,0:T(8,128)(2,1)S(1)} %all-to-all-done.x_ref), custom_call_target="tpu_custom_call" | custom-call | flops 8999999488 | bytes 10000000 | tf_op jit(solution)/shard_map/attend/pallas_call | solution.py:167
  36.2 6.4 %all-to-all-start.1 = ((bf16[16,144,128]{2,1,0:T(8,128)(2,1)}), bf16[16,144,128]{2,1,0:T(8,128)(2,1)S(1)}, u32[]{:S(2)}, u32[]{:S(2)}) async-start(bf16[16,144,128]{2,1,0:T(8,128)(2,1)} %get-tuple-element.41), calls=%async_computation.1 | async-start | bytes 1179648 | tf_op jit(solution)/shard_map/all_to_all | solution.py:657
  42.7 9.1 %all-to-all-done.1.att_ref.refs_0_ = bf16[16,144,128]{2,1,0:T(8,128)(2,1)S(1)} async-done(((bf16[16,144,128]{2,1,0:T(8,128)(2,1)}), bf16[16,144,128]{2,1,0:T(8,128)(2,1)S(1)}, u32[]{:S(2)}, u32[]{:S(2)}) %all-to-all-start.1) | async-done | bytes 589856 | tf_op jit(solution)/shard_map/all_to_all | solution.py:657
  51.8 1.9 %collective-permute-start.2 = (bf16[16,144,128]{2,1,0:T(8,128)(2,1)S(1)}, bf16[16,144,128]{2,1,0:T(8,128)(2,1)S(1)}, u32[]{:S(2)}, u32[]{:S(2)}) collective-permute-start(bf16[16,144,128]{2,1,0:T(8,128)(2,1)S(1)} %all-to-all-done.1.att_ref.refs_0_), channel_id=1, source_target_pairs={{0,32},{16,48},{32,0},{48,16},{64,96},{80,112},{96,64},{112,80},{1... | collective-permute-start | bytes 1769480 | tf_op jit(solution)/shard_map/ppermute | solution.py:688
  54.6 12.0 %convolve.1 = (bf16[128,1536]{1,0:T(8,128)(2,1)}, bf16[16,128,128]{2,1,0:T(8,128)(2,1)}, bf16[128,768]{1,0:T(8,128)(2,1)}, bf16[128,768]{1,0:T(8,128)(2,1)}) custom-call(s32[5]{0:T(128)S(1)} %stack.19.info_ref, bf16[16,144,128]{2,1,0:T(8,128)(2,1)S(1)} %all-to-all-done.1.att_ref.refs_0_, bf16[128,1536]{1,0:T(8,128)(2,1)} %bitcast.17, ...), custom_call_target="tpu_custom_call" | custom-call | flops 8999999488 | bytes 10000000 | tf_op jit(solution)/shard_map/convolve/pallas_call | solution.py:342
  66.6 1.1 collective-permute-done.2.refs_2_
  67.9 6.2 %all-to-all-start.2 = ((bf16[16,128,128]{2,1,0:T(8,128)(2,1)}), bf16[16,128,128]{2,1,0:T(8,128)(2,1)S(1)}, u32[]{:S(2)}, u32[]{:S(2)}) async-start(bf16[16,128,128]{2,1,0:T(8,128)(2,1)} %get-tuple-element.46), calls=%async_computation.2 | async-start | bytes 1048576 | tf_op jit(solution)/shard_map/all_to_all | solution.py:657
  74.0 1.7 %collective-permute-start.6 = (bf16[128,768]{1,0:T(8,128)(2,1)}, bf16[128,768]{1,0:T(8,128)(2,1)S(1)}, u32[]{:S(2)}, u32[]{:S(2)}) collective-permute-start(bf16[128,768]{1,0:T(8,128)(2,1)} %get-tuple-element.52), channel_id=1, source_target_pairs={{0,32},{16,48},{32,0},{48,16},{64,96},{80,112},{96,64},{112,80},{1... | collective-permute-start | bytes 589832 | tf_op jit(solution)/shard_map/ppermute | solution.py:698
  75.8 5.4 %collective-permute-done.6.refs_6_ = bf16[128,768]{1,0:T(8,128)(2,1)S(1)} collective-permute-done((bf16[128,768]{1,0:T(8,128)(2,1)}, bf16[128,768]{1,0:T(8,128)(2,1)S(1)}, u32[]{:S(2)}, u32[]{:S(2)}) %collective-permute-start.6) | collective-permute-done | bytes 196640 | tf_op jit(solution)/shard_map/ppermute | solution.py:698
  81.2 1.4 collective-permute-done.7.refs_7_
  82.7 3.4 %outer.1.w_ref = bf16[16,320,128]{2,1,0:T(8,128)(2,1)} custom-call(s32[5]{0:T(128)S(1)} %stack.19.info_ref, bf16[16,144,128]{2,1,0:T(8,128)(2,1)S(1)} %all-to-all-done.1.att_ref.refs_0_, bf16[16,144,128]{2,1,0:T(8,128)(2,1)} %collective-permute-done.3.refs_1_, bf16[16,144,128]{2,1,0:T(8,128)(2,1)S(1)} %collective-permute-done.2.refs_2_, ...), custom_call_target="tpu_custom_call" | custom-call | flops 1000000000 | bytes 4000000 | tf_op jit(solution)/shard_map/outer/pallas_call | solution.py:408
  86.9 7.3 %all-to-all-start.3 = ((bf16[16,320,128]{2,1,0:T(8,128)(2,1)}), bf16[16,320,128]{2,1,0:T(8,128)(2,1)S(1)}, u32[]{:S(2)}, u32[]{:S(2)}) async-start(bf16[16,320,128]{2,1,0:T(8,128)(2,1)} %tail.1), calls=%async_computation.3 | async-start | bytes 2621440 | tf_op jit(solution)/shard_map/all_to_all | solution.py:657
  94.2 11.8 %attend_back.1 = bf16[16,288,128]{2,1,0:T(8,128)(2,1)} custom-call(bf16[16,288,128]{2,1,0:T(8,128)(2,1)S(1)} %all-to-all-done.x_ref, bf16[16,128,128]{2,1,0:T(8,128)(2,1)S(1)} %all-to-all-done.2.g_ref, bf16[4,2048,512]{2,1,0:T(8,128)(2,1)} %get-tuple-element.47.e_ref, f32[96,2048]{1,0:T(8,128)} %get-tuple-element.48.o_ref, ...), custom_call_target="tpu_custom_call" | custom-call | flops 20000000000 | bytes 10000000 | tf_op jit(solution)/shard_map/attend_back/pallas_call | solution.py:506
  106.0 6.0 %all-to-all-done.3.x_ref = bf16[16,320,128]{2,1,0:T(8,128)(2,1)S(1)} async-done(((bf16[16,320,128]{2,1,0:T(8,128)(2,1)}), bf16[16,320,128]{2,1,0:T(8,128)(2,1)S(1)}, u32[]{:S(2)}, u32[]{:S(2)}) %all-to-all-start.3) | async-done | bytes 1310752 | tf_op jit(solution)/shard_map/all_to_all | solution.py:657
  111.9 6.6 %all-to-all-start.4 = ((bf16[16,288,128]{2,1,0:T(8,128)(2,1)}), bf16[16,288,128]{2,1,0:T(8,128)(2,1)S(1)}, u32[]{:S(2)}, u32[]{:S(2)}) async-start(bf16[16,288,128]{2,1,0:T(8,128)(2,1)} %attend_back.1), calls=%async_computation.4 | async-start | bytes 2359296 | tf_op jit(solution)/shard_map/all_to_all | solution.py:657
  118.6 1.4 pack.1
  120.0 3.3 %collective-permute-start.8 = (bf16[2,128,128]{2,1,0:T(8,128)(2,1)}, bf16[2,128,128]{2,1,0:T(8,128)(2,1)S(1)}, u32[]{:S(2)}, u32[]{:S(2)}) collective-permute-start(bf16[2,128,128]{2,1,0:T(8,128)(2,1)} %get-tuple-element.55), channel_id=1, source_target_pairs={{0,64},{16,80},{32,96},{48,112},{64,0},{80,16},{96,32},{112,48},{1... | collective-permute-start | bytes 196616 | tf_op jit(solution)/shard_map/ppermute | solution.py:710
  123.3 5.3 %collective-permute-start.9 = (bf16[2,128,128]{2,1,0:T(8,128)(2,1)}, bf16[2,128,128]{2,1,0:T(8,128)(2,1)S(1)}, u32[]{:S(2)}, u32[]{:S(2)}) collective-permute-start(bf16[2,128,128]{2,1,0:T(8,128)(2,1)} %get-tuple-element.56), channel_id=1, source_target_pairs={{0,128},{16,144},{32,160},{48,176},{64,192},{80,208},{96,224},{112... | collective-permute-start | bytes 196616 | tf_op jit(solution)/shard_map/ppermute | solution.py:710
  128.5 3.8 %collective-permute-done.9.refs_2_ = bf16[2,128,128]{2,1,0:T(8,128)(2,1)S(1)} collective-permute-done((bf16[2,128,128]{2,1,0:T(8,128)(2,1)}, bf16[2,128,128]{2,1,0:T(8,128)(2,1)S(1)}, u32[]{:S(2)}, u32[]{:S(2)}) %collective-permute-start.9) | collective-permute-done | bytes 65568 | tf_op jit(solution)/shard_map/ppermute | solution.py:710
  132.4 2.7 %collective-permute-done.10.refs_3_ = bf16[2,128,128]{2,1,0:T(8,128)(2,1)S(1)} collective-permute-done((bf16[2,128,128]{2,1,0:T(8,128)(2,1)}, bf16[2,128,128]{2,1,0:T(8,128)(2,1)S(1)}, u32[]{:S(2)}, u32[]{:S(2)}) %collective-permute-start.10) | collective-permute-done | bytes 65568 | tf_op jit(solution)/shard_map/ppermute | solution.py:710
  135.1 1.5 merge.1
  137.3 3.4 %collective-permute-done.11.refs_1_ = bf16[128,128]{1,0:T(8,128)(2,1)S(1)} collective-permute-done((bf16[128,128]{1,0:T(8,128)(2,1)}, bf16[128,128]{1,0:T(8,128)(2,1)S(1)}, u32[]{:S(2)}, u32[]{:S(2)}) %collective-permute-start.11) | collective-permute-done | bytes 32800 | tf_op jit(solution)/shard_map/ppermute | solution.py:713
  140.7 1.6 total.1
  142.4 6.0 %all-to-all-start.5 = ((bf16[16,128,128]{2,1,0:T(8,128)(2,1)}), bf16[16,128,128]{2,1,0:T(8,128)(2,1)S(1)}, u32[]{:S(2)}, u32[]{:S(2)}) async-start(bf16[16,128,128]{2,1,0:T(8,128)(2,1)} %total.1), calls=%async_computation.5 | async-start | bytes 1048576 | tf_op jit(solution)/shard_map/all_to_all | solution.py:657
  148.3 1.2 post.1
  149.5 15.3 %all-to-all-done.5.x_ref = bf16[16,128,128]{2,1,0:T(8,128)(2,1)S(1)} async-done(((bf16[16,128,128]{2,1,0:T(8,128)(2,1)}), bf16[16,128,128]{2,1,0:T(8,128)(2,1)S(1)}, u32[]{:S(2)}, u32[]{:S(2)}) %all-to-all-start.5) | async-done | bytes 524320 | tf_op jit(solution)/shard_map/all_to_all | solution.py:657
  164.7 0.9 unpack.1
  (20 shorter events, 2.6 us)
Async XLA Ops:
  3.2 24.4 %all-to-all-start = ((bf16[16,288,128]{2,1,0:T(8,128)(2,1)}), bf16[16,288,128]{2,1,0:T(8,128)(2,1)S(1)}, u32[]{:S(2)}, u32[]{:S(2)}) async-start(bf16[16,288,128]{2,1,0:T(8,128)(2,1)} %get-tuple-element.37), calls=%async_computation | async-start | bytes 2359296 | tf_op jit(solution)/shard_map/all_to_all | solution.py:657
  10.7 16.9 %collective-permute-start = (bf16[48,1536]{1,0:T(8,128)(2,1)S(1)}, bf16[48,1536]{1,0:T(8,128)(2,1)S(1)}, u32[]{:S(2)}, u32[]{:S(2)}) collective-permute-start(bf16[48,1536]{1,0:T(8,128)(2,1)S(1)} %get-tuple-element.38), channel_id=1, source_target_pairs={{0,1},{1,2},{2,3},{3,4},{4,5},{5,6},{6,7},{7,8},{8,9},{9,10},{10,1... | collective-permute-start | bytes 442376 | tf_op jit(solution)/shard_map/ppermute | solution.py:683
  12.7 14.9 %collective-permute-start.1 = (bf16[48,1536]{1,0:T(8,128)(2,1)S(1)}, bf16[48,1536]{1,0:T(8,128)(2,1)S(1)}, u32[]{:S(2)}, u32[]{:S(2)}) collective-permute-start(bf16[48,1536]{1,0:T(8,128)(2,1)S(1)} %get-tuple-element.39), channel_id=1, source_target_pairs={{1,0},{2,1},{3,2},{4,3},{5,4},{6,5},{7,6},{8,7},{9,8},{10,9},{11,1... | collective-permute-start | bytes 442376 | tf_op jit(solution)/shard_map/ppermute | solution.py:684
  27.6 8.6 %copy-start = (bf16[48,1536]{1,0:T(8,128)(2,1)}, bf16[48,1536]{1,0:T(8,128)(2,1)S(1)}, u32[]{:S(2)}) copy-start(bf16[48,1536]{1,0:T(8,128)(2,1)S(1)} %collective-permute-done.left_hbm) | copy-start | bytes 442372
  27.6 8.6 %copy-start.1 = (bf16[48,1536]{1,0:T(8,128)(2,1)}, bf16[48,1536]{1,0:T(8,128)(2,1)S(1)}, u32[]{:S(2)}) copy-start(bf16[48,1536]{1,0:T(8,128)(2,1)S(1)} %collective-permute-done.1.right_hbm) | copy-start | bytes 442372
  36.2 15.7 %all-to-all-start.1 = ((bf16[16,144,128]{2,1,0:T(8,128)(2,1)}), bf16[16,144,128]{2,1,0:T(8,128)(2,1)S(1)}, u32[]{:S(2)}, u32[]{:S(2)}) async-start(bf16[16,144,128]{2,1,0:T(8,128)(2,1)} %get-tuple-element.41), calls=%async_computation.1 | async-start | bytes 1179648 | tf_op jit(solution)/shard_map/all_to_all | solution.py:657
  51.8 15.9 %collective-permute-start.2 = (bf16[16,144,128]{2,1,0:T(8,128)(2,1)S(1)}, bf16[16,144,128]{2,1,0:T(8,128)(2,1)S(1)}, u32[]{:S(2)}, u32[]{:S(2)}) collective-permute-start(bf16[16,144,128]{2,1,0:T(8,128)(2,1)S(1)} %all-to-all-done.1.att_ref.refs_0_), channel_id=1, source_target_pairs={{0,32},{16,48},{32,0},{48,16},{64,96},{80,112},{96,64},{112,80},{1... | collective-permute-start | bytes 1769480 | tf_op jit(solution)/shard_map/ppermute | solution.py:688
  53.8 28.9 %collective-permute-start.3 = (bf16[16,144,128]{2,1,0:T(8,128)(2,1)S(1)}, bf16[16,144,128]{2,1,0:T(8,128)(2,1)}, u32[]{:S(2)}, u32[]{:S(2)}) collective-permute-start(bf16[16,144,128]{2,1,0:T(8,128)(2,1)S(1)} %all-to-all-done.1.att_ref.refs_0_), channel_id=1, source_target_pairs={{0,1},{1,0},{2,3},{3,2},{4,5},{5,4},{6,7},{7,6},{8,9},{9,8},{10,11... | collective-permute-start | bytes 1769480 | tf_op jit(solution)/shard_map/ppermute | solution.py:689
  67.7 14.9 %collective-permute-start.4 = (bf16[16,144,128]{2,1,0:T(8,128)(2,1)S(1)}, bf16[16,144,128]{2,1,0:T(8,128)(2,1)}, u32[]{:S(2)}, u32[]{:S(2)}) collective-permute-start(bf16[16,144,128]{2,1,0:T(8,128)(2,1)S(1)} %collective-permute-done.2.refs_2_), channel_id=1, source_target_pairs={{0,1},{1,0},{2,3},{3,2},{4,5},{5,4},{6,7},{7,6},{8,9},{9,8},{10,11... | collective-permute-start | bytes 1769480 | tf_op jit(solution)/shard_map/ppermute | solution.py:696
  67.9 18.2 %all-to-all-start.2 = ((bf16[16,128,128]{2,1,0:T(8,128)(2,1)}), bf16[16,128,128]{2,1,0:T(8,128)(2,1)S(1)}, u32[]{:S(2)}, u32[]{:S(2)}) async-start(bf16[16,128,128]{2,1,0:T(8,128)(2,1)} %get-tuple-element.46), calls=%async_computation.2 | async-start | bytes 1048576 | tf_op jit(solution)/shard_map/all_to_all | solution.py:657
  74.0 7.2 %collective-permute-start.6 = (bf16[128,768]{1,0:T(8,128)(2,1)}, bf16[128,768]{1,0:T(8,128)(2,1)S(1)}, u32[]{:S(2)}, u32[]{:S(2)}) collective-permute-start(bf16[128,768]{1,0:T(8,128)(2,1)} %get-tuple-element.52), channel_id=1, source_target_pairs={{0,32},{16,48},{32,0},{48,16},{64,96},{80,112},{96,64},{112,80},{1... | collective-permute-start | bytes 589832 | tf_op jit(solution)/shard_map/ppermute | solution.py:698
  75.8 5.4 %collective-permute-start.5 = (bf16[128,768]{1,0:T(8,128)(2,1)}, bf16[128,768]{1,0:T(8,128)(2,1)S(1)}, u32[]{:S(2)}, u32[]{:S(2)}) collective-permute-start(bf16[128,768]{1,0:T(8,128)(2,1)} %get-tuple-element.51.refs_4_), channel_id=1, source_target_pairs={{0,1},{1,0},{2,3},{3,2},{4,5},{5,4},{6,7},{7,6},{8,9},{9,8},{10,11... | collective-permute-start | bytes 589832 | tf_op jit(solution)/shard_map/ppermute | solution.py:699
  81.2 1.4 collective-permute-start.7
  86.9 25.0 %all-to-all-start.3 = ((bf16[16,320,128]{2,1,0:T(8,128)(2,1)}), bf16[16,320,128]{2,1,0:T(8,128)(2,1)S(1)}, u32[]{:S(2)}, u32[]{:S(2)}) async-start(bf16[16,320,128]{2,1,0:T(8,128)(2,1)} %tail.1), calls=%async_computation.3 | async-start | bytes 2621440 | tf_op jit(solution)/shard_map/all_to_all | solution.py:657
  111.9 30.4 %all-to-all-start.4 = ((bf16[16,288,128]{2,1,0:T(8,128)(2,1)}), bf16[16,288,128]{2,1,0:T(8,128)(2,1)S(1)}, u32[]{:S(2)}, u32[]{:S(2)}) async-start(bf16[16,288,128]{2,1,0:T(8,128)(2,1)} %attend_back.1), calls=%async_computation.4 | async-start | bytes 2359296 | tf_op jit(solution)/shard_map/all_to_all | solution.py:657
  120.0 8.6 %collective-permute-start.8 = (bf16[2,128,128]{2,1,0:T(8,128)(2,1)}, bf16[2,128,128]{2,1,0:T(8,128)(2,1)S(1)}, u32[]{:S(2)}, u32[]{:S(2)}) collective-permute-start(bf16[2,128,128]{2,1,0:T(8,128)(2,1)} %get-tuple-element.55), channel_id=1, source_target_pairs={{0,64},{16,80},{32,96},{48,112},{64,0},{80,16},{96,32},{112,48},{1... | collective-permute-start | bytes 196616 | tf_op jit(solution)/shard_map/ppermute | solution.py:710
  123.3 9.1 %collective-permute-start.9 = (bf16[2,128,128]{2,1,0:T(8,128)(2,1)}, bf16[2,128,128]{2,1,0:T(8,128)(2,1)S(1)}, u32[]{:S(2)}, u32[]{:S(2)}) collective-permute-start(bf16[2,128,128]{2,1,0:T(8,128)(2,1)} %get-tuple-element.56), channel_id=1, source_target_pairs={{0,128},{16,144},{32,160},{48,176},{64,192},{80,208},{96,224},{112... | collective-permute-start | bytes 196616 | tf_op jit(solution)/shard_map/ppermute | solution.py:710
  128.5 6.6 %collective-permute-start.10 = (bf16[2,128,128]{2,1,0:T(8,128)(2,1)}, bf16[2,128,128]{2,1,0:T(8,128)(2,1)S(1)}, u32[]{:S(2)}, u32[]{:S(2)}) collective-permute-start(bf16[2,128,128]{2,1,0:T(8,128)(2,1)} %get-tuple-element.57), channel_id=1, source_target_pairs={{0,192},{16,208},{32,224},{48,240},{64,128},{80,144},{96,160},{112... | collective-permute-start | bytes 196616 | tf_op jit(solution)/shard_map/ppermute | solution.py:710
  136.6 4.1 %collective-permute-start.11 = (bf16[128,128]{1,0:T(8,128)(2,1)}, bf16[128,128]{1,0:T(8,128)(2,1)S(1)}, u32[]{:S(2)}, u32[]{:S(2)}) collective-permute-start(bf16[128,128]{1,0:T(8,128)(2,1)} %get-tuple-element.59), channel_id=1, source_target_pairs={{0,16},{16,0},{32,48},{48,32},{64,80},{80,64},{96,112},{112,96},{1... | collective-permute-start | bytes 98312 | tf_op jit(solution)/shard_map/ppermute | solution.py:713
  142.4 22.4 %all-to-all-start.5 = ((bf16[16,128,128]{2,1,0:T(8,128)(2,1)}), bf16[16,128,128]{2,1,0:T(8,128)(2,1)S(1)}, u32[]{:S(2)}, u32[]{:S(2)}) async-start(bf16[16,128,128]{2,1,0:T(8,128)(2,1)} %total.1), calls=%async_computation.5 | async-start | bytes 1048576 | tf_op jit(solution)/shard_map/all_to_all | solution.py:657

commit v6 on v5

--- a/solution.py
+++ b/solution.py
@@ -195,9 +195,9 @@
 
 def conv_kernel_body(
     info_ref, att_ref, res_hbm, cot_hbm, left_hbm, right_hbm, w_hbm, taps_hbm,
-    out_hbm, pay_ref, keep_hbm, send_hbm,
+    out_hbm, pay_hbm, keep_hbm, send_hbm,
     lhs, block_in, masked, cot, grad, taps_sum, bg_ref,
-    res_ref, cot_ref, left_ref, right_ref, weight, taps_ref, proj, out_ref, sems,
+    res_ref, cot_ref, left_ref, right_ref, weight, taps_ref, proj, out_ref, pay_ref, sems,
 ):
     rows, width = res_ref.shape
     cols = width // LANES
@@ -321,6 +321,7 @@
     ]
     for store in stores:
         store.start()
+    pay_ref[:, HEAD:LANES, :] = taps_sum[...].astype(BF)
     bg = bg_ref[...]
     for h in range(0, HEADS, 2):
         mixed = lax.dot_general(
@@ -329,7 +330,13 @@
         ).astype(BF)
         pay_ref[h, 0:HEAD, :] = mixed[0:HEAD]
         pay_ref[h + 1, 0:HEAD, :] = mixed[HEAD : 2 * HEAD]
-    pay_ref[:, HEAD:LANES, :] = taps_sum[...].astype(BF)
+        if h % 4 == 2:
+            at = pl.ds(h - 2, 4)
+            store = pltpu.make_async_copy(
+                pay_ref.at[at], pay_hbm.at[at], sems.at[pieces + 8 + h // 4]
+            )
+            store.start()
+            stores.append(store)
     for store in stores:
         store.wait()
 
@@ -352,10 +359,8 @@
         + [pl.BlockSpec(memory_space=pl.ANY)] * 6,
         out_specs=(
             pl.BlockSpec(memory_space=pl.ANY),
-            vm,
-            pl.BlockSpec(memory_space=pl.ANY),
-            pl.BlockSpec(memory_space=pl.ANY),
-        ),
+        )
+        * 4,
         scratch_shapes=[
             pltpu.VMEM((span, width), BF),
             pltpu.VMEM((cols, span, LANES), F32),
@@ -372,7 +377,8 @@
             pltpu.VMEM((TAPS, width), F32),
             pltpu.VMEM((span, 2 * LANES), F32),
             pltpu.VMEM((rows, width), BF),
-            pltpu.SemaphoreType.DMA((cols // 2 + 8,)),
+            pltpu.VMEM((HEADS, LANES, LANES), BF),
+            pltpu.SemaphoreType.DMA((cols // 2 + 12,)),
         ],
         compiler_params=params(20),
         cost_estimate=cost(9e9, 1e7),
@@ -545,6 +551,7 @@
 
 
 GROUP = 8
+PIECE = 120
 
 
 def pack_kernel(info_ref, x_ref, *refs):
@@ -563,9 +570,8 @@
     for k in range(GROUP):
         j = jnp.bitwise_xor(info_ref[4], k)
         taps = [x_ref[2 * j + e, below : below + 32, :].astype(F32)[0:24] for e in range(2)]
-        rest = jnp.zeros((LANES - share - 48, LANES), F32)
         outs[k // 2][k % 2] = jnp.concatenate(
-            [buf[pl.ds(pl.multiple_of(share * j, 8), share), :]] + taps + [rest], axis=0
+            [buf[pl.ds(pl.multiple_of(share * j, 8), share), :]] + taps, axis=0
         ).astype(BF)
 
 
@@ -573,7 +579,7 @@
     units = x.shape[1] // HEAD * HEAD * 2
     return pl.pallas_call(
         pack_kernel,
-        out_shape=(pltpu.HBM((2, LANES, LANES), BF),) * (GROUP // 2),
+        out_shape=(pltpu.HBM((2, PIECE, LANES), BF),) * (GROUP // 2),
         in_specs=[pl.BlockSpec(memory_space=pltpu.SMEM), pl.BlockSpec()],
         scratch_shapes=[pltpu.VMEM((units, LANES), F32)],
         compiler_params=params(12),
@@ -692,7 +698,7 @@
     block_out, payload, keep, send = conv(
         info, attended, res, cot, in_hbm(left), in_hbm(right), out_weight, conv_kernel
     )
-    att_level, payload = lax.optimization_barrier((att_level, payload))
+    att_level, send = lax.optimization_barrier((att_level, send))
     att_both = lax.ppermute(att_level, "seq", cores)
     grads = exchange(payload, "seq")
     level = lax.ppermute(send, "dp", levels)

time: 167 us -> 167 us (level)
  no operation moved by 1% of the time
where the time goes in v6:
time: 167 us; the launch traced here: 165 us
  starting transfers between devices  59.8 us (36%)
  waiting for transfers between devices  58.5 us (35%)
  Pallas kernels  45.5 us (27%)
    all_to_all x6, starting transfers between devices, exchange(): lax.all_to_all(x, axis, split_axis=0, concat_axis=0, tiled=True, axis_ind...  40.3 us
    all_to_all x6, waiting for transfers between devices, exchange(): lax.all_to_all(x, axis, split_axis=0, concat_axis=0, tiled=True, axis_ind...  29.4 us
    pallas_call x1, Pallas kernels, conv(): pl.pallas_call(conv_kernel_body, out_shape=(pltpu.HBM((rows, width), BF),...  11.9 us
    pallas_call x1, Pallas kernels, bwd(): pl.pallas_call(bwd_kernel, grid=(steps,), out_shape=pltpu.HBM((blocks, 3...  11.8 us
    ppermute x1, waiting for transfers between devices, shards(): left = lax.ppermute(edge_up, 'seq', up)  10.7 us
    ppermute x3, starting transfers between devices, shards(): lax.ppermute(packed[k], 'dp', hop(2 * k))  8.56 us
    pallas_call x1, Pallas kernels, fwd(): pl.pallas_call(fwd_kernel, out_shape=(pltpu.HBM((steps, frames, QT), BF),...  8.55 us
    ppermute x3, waiting for transfers between devices, shards(): lax.ppermute(packed[k], 'dp', hop(2 * k))  6.54 us
  transfers between devices with their start and end apart: 18, of which 10 were waited for; matrix products, arithmetic and copies ran while one was open for 0% of the time, Pallas kernels for 20%

profile of v6, /device:TPU:2, one launch (start us, length us, event | category | flops | bytes accessed | tf_op | source)
XLA Modules:
  0.0 165.3 jit_solution(14444236632133968217)
XLA Ops:
  0.6 2.5 %pre.1 = (bf16[16,288,128]{2,1,0:T(8,128)(2,1)}, bf16[48,1536]{1,0:T(8,128)(2,1)S(1)}, bf16[48,1536]{1,0:T(8,128)(2,1)S(1)}) custom-call(bf16[128,1536]{1,0:T(8,128)(2,1)} %bitcast.13, bf16[128,1536]{1,0:T(8,128)(2,1)} %bitcast.14, bf16[128,1536]{1,0:T(8,128)(2,1)} %bitcast.15, bf16[128,1536]{1,0:T(8,128)(2,1)} %bitcast.16, bf16[128,1536]{1,0:T(8,128)(2,1)} %bitcast.18), custom_call_target="tpu_custom_call" | custom-call | flops 1000000 | bytes 3000000 | tf_op jit(solution)/shard_map/pre/pallas_call | solution.py:72
  3.2 7.5 %all-to-all-start = ((bf16[16,288,128]{2,1,0:T(8,128)(2,1)}), bf16[16,288,128]{2,1,0:T(8,128)(2,1)S(1)}, u32[]{:S(2)}, u32[]{:S(2)}) async-start(bf16[16,288,128]{2,1,0:T(8,128)(2,1)} %get-tuple-element.37), calls=%async_computation | async-start | bytes 2359296 | tf_op jit(solution)/shard_map/all_to_all | solution.py:663
  10.7 2.0 %collective-permute-start = (bf16[48,1536]{1,0:T(8,128)(2,1)S(1)}, bf16[48,1536]{1,0:T(8,128)(2,1)S(1)}, u32[]{:S(2)}, u32[]{:S(2)}) collective-permute-start(bf16[48,1536]{1,0:T(8,128)(2,1)S(1)} %get-tuple-element.38), channel_id=1, source_target_pairs={{0,1},{1,2},{2,3},{3,4},{4,5},{5,6},{6,7},{7,8},{8,9},{9,10},{10,1... | collective-permute-start | bytes 442376 | tf_op jit(solution)/shard_map/ppermute | solution.py:689
  12.7 3.5 %collective-permute-start.1 = (bf16[48,1536]{1,0:T(8,128)(2,1)S(1)}, bf16[48,1536]{1,0:T(8,128)(2,1)S(1)}, u32[]{:S(2)}, u32[]{:S(2)}) collective-permute-start(bf16[48,1536]{1,0:T(8,128)(2,1)S(1)} %get-tuple-element.39), channel_id=1, source_target_pairs={{1,0},{2,1},{3,2},{4,3},{5,4},{6,5},{7,6},{8,7},{9,8},{10,9},{11,1... | collective-permute-start | bytes 442376 | tf_op jit(solution)/shard_map/ppermute | solution.py:690
  16.9 10.7 %collective-permute-done.left_hbm = bf16[48,1536]{1,0:T(8,128)(2,1)S(1)} collective-permute-done((bf16[48,1536]{1,0:T(8,128)(2,1)S(1)}, bf16[48,1536]{1,0:T(8,128)(2,1)S(1)}, u32[]{:S(2)}, u32[]{:S(2)}) %collective-permute-start) | collective-permute-done | bytes 147488 | tf_op jit(solution)/shard_map/ppermute | solution.py:689
  27.6 8.6 %attend.1 = (bf16[4,2048,512]{2,1,0:T(8,128)(2,1)}, f32[96,2048]{1,0:T(8,128)}, f32[8,2048]{1,0:T(8,128)S(1)}, bf16[16,144,128]{2,1,0:T(8,128)(2,1)}) custom-call(s32[1]{0:T(128)S(6)} %copy.16.len_ref, bf16[16,288,128]{2,1,0:T(8,128)(2,1)S(1)} %all-to-all-done.x_ref), custom_call_target="tpu_custom_call" | custom-call | flops 8999999488 | bytes 10000000 | tf_op jit(solution)/shard_map/attend/pallas_call | solution.py:167
  36.2 6.4 %all-to-all-start.1 = ((bf16[16,144,128]{2,1,0:T(8,128)(2,1)}), bf16[16,144,128]{2,1,0:T(8,128)(2,1)S(1)}, u32[]{:S(2)}, u32[]{:S(2)}) async-start(bf16[16,144,128]{2,1,0:T(8,128)(2,1)} %get-tuple-element.41), calls=%async_computation.1 | async-start | bytes 1179648 | tf_op jit(solution)/shard_map/all_to_all | solution.py:663
  42.7 9.1 %all-to-all-done.1.att_ref.refs_0_ = bf16[16,144,128]{2,1,0:T(8,128)(2,1)S(1)} async-done(((bf16[16,144,128]{2,1,0:T(8,128)(2,1)}), bf16[16,144,128]{2,1,0:T(8,128)(2,1)S(1)}, u32[]{:S(2)}, u32[]{:S(2)}) %all-to-all-start.1) | async-done | bytes 589856 | tf_op jit(solution)/shard_map/all_to_all | solution.py:663
  51.8 1.1 collective-permute-start.2
  52.9 1.9 %collective-permute-start.3 = (bf16[16,144,128]{2,1,0:T(8,128)(2,1)S(1)}, bf16[16,144,128]{2,1,0:T(8,128)(2,1)}, u32[]{:S(2)}, u32[]{:S(2)}) collective-permute-start(bf16[16,144,128]{2,1,0:T(8,128)(2,1)S(1)} %all-to-all-done.1.att_ref.refs_0_), channel_id=1, source_target_pairs={{0,32},{16,48},{32,0},{48,16},{64,96},{80,112},{96,64},{112,80},{1... | collective-permute-start | bytes 1769480 | tf_op jit(solution)/shard_map/ppermute | solution.py:694
  54.8 11.9 %convolve.1 = (bf16[128,1536]{1,0:T(8,128)(2,1)}, bf16[16,128,128]{2,1,0:T(8,128)(2,1)}, bf16[128,768]{1,0:T(8,128)(2,1)}, bf16[128,768]{1,0:T(8,128)(2,1)}) custom-call(s32[5]{0:T(128)S(1)} %stack.19.info_ref, bf16[16,144,128]{2,1,0:T(8,128)(2,1)S(1)} %all-to-all-done.1.att_ref.refs_0_, bf16[128,1536]{1,0:T(8,128)(2,1)} %bitcast.17, ...), custom_call_target="tpu_custom_call" | custom-call | flops 8999999488 | bytes 10000000 | tf_op jit(solution)/shard_map/convolve/pallas_call | solution.py:349
  66.8 1.6 collective-permute-done.3.refs_2_
  68.4 6.7 %all-to-all-start.2 = ((bf16[16,128,128]{2,1,0:T(8,128)(2,1)}), bf16[16,128,128]{2,1,0:T(8,128)(2,1)S(1)}, u32[]{:S(2)}, u32[]{:S(2)}) async-start(bf16[16,128,128]{2,1,0:T(8,128)(2,1)} %get-tuple-element.45), calls=%async_computation.2 | async-start | bytes 1048576 | tf_op jit(solution)/shard_map/all_to_all | solution.py:663
  75.2 1.7 %collective-permute-start.6 = (bf16[128,768]{1,0:T(8,128)(2,1)}, bf16[128,768]{1,0:T(8,128)(2,1)S(1)}, u32[]{:S(2)}, u32[]{:S(2)}) collective-permute-start(bf16[128,768]{1,0:T(8,128)(2,1)} %get-tuple-element.52), channel_id=1, source_target_pairs={{0,32},{16,48},{32,0},{48,16},{64,96},{80,112},{96,64},{112,80},{1... | collective-permute-start | bytes 589832 | tf_op jit(solution)/shard_map/ppermute | solution.py:704
  76.9 5.4 %collective-permute-done.6.refs_6_ = bf16[128,768]{1,0:T(8,128)(2,1)S(1)} collective-permute-done((bf16[128,768]{1,0:T(8,128)(2,1)}, bf16[128,768]{1,0:T(8,128)(2,1)S(1)}, u32[]{:S(2)}, u32[]{:S(2)}) %collective-permute-start.6) | collective-permute-done | bytes 196640 | tf_op jit(solution)/shard_map/ppermute | solution.py:704
  82.4 1.4 collective-permute-done.7.refs_7_
  83.8 3.4 %outer.1.w_ref = bf16[16,320,128]{2,1,0:T(8,128)(2,1)} custom-call(s32[5]{0:T(128)S(1)} %stack.19.info_ref, bf16[16,144,128]{2,1,0:T(8,128)(2,1)S(1)} %all-to-all-done.1.att_ref.refs_0_, bf16[16,144,128]{2,1,0:T(8,128)(2,1)S(1)} %collective-permute-done.2.refs_1_, bf16[16,144,128]{2,1,0:T(8,128)(2,1)} %collective-permute-done.3.refs_2_, ...), custom_call_target="tpu_custom_call" | custom-call | flops 1000000000 | bytes 4000000 | tf_op jit(solution)/shard_map/outer/pallas_call | solution.py:414
  88.0 7.3 %all-to-all-start.3 = ((bf16[16,320,128]{2,1,0:T(8,128)(2,1)}), bf16[16,320,128]{2,1,0:T(8,128)(2,1)S(1)}, u32[]{:S(2)}, u32[]{:S(2)}) async-start(bf16[16,320,128]{2,1,0:T(8,128)(2,1)} %tail.1), calls=%async_computation.3 | async-start | bytes 2621440 | tf_op jit(solution)/shard_map/all_to_all | solution.py:663
  95.3 11.8 %attend_back.1 = bf16[16,288,128]{2,1,0:T(8,128)(2,1)} custom-call(bf16[16,288,128]{2,1,0:T(8,128)(2,1)S(1)} %all-to-all-done.x_ref, bf16[16,128,128]{2,1,0:T(8,128)(2,1)S(1)} %all-to-all-done.2.g_ref, bf16[4,2048,512]{2,1,0:T(8,128)(2,1)} %get-tuple-element.46.e_ref, f32[96,2048]{1,0:T(8,128)} %get-tuple-element.47.o_ref, ...), custom_call_target="tpu_custom_call" | custom-call | flops 20000000000 | bytes 10000000 | tf_op jit(solution)/shard_map/attend_back/pallas_call | solution.py:512
  107.1 6.0 %all-to-all-done.3.x_ref = bf16[16,320,128]{2,1,0:T(8,128)(2,1)S(1)} async-done(((bf16[16,320,128]{2,1,0:T(8,128)(2,1)}), bf16[16,320,128]{2,1,0:T(8,128)(2,1)S(1)}, u32[]{:S(2)}, u32[]{:S(2)}) %all-to-all-start.3) | async-done | bytes 1310752 | tf_op jit(solution)/shard_map/all_to_all | solution.py:663
  113.1 6.6 %all-to-all-start.4 = ((bf16[16,288,128]{2,1,0:T(8,128)(2,1)}), bf16[16,288,128]{2,1,0:T(8,128)(2,1)S(1)}, u32[]{:S(2)}, u32[]{:S(2)}) async-start(bf16[16,288,128]{2,1,0:T(8,128)(2,1)} %attend_back.1), calls=%async_computation.4 | async-start | bytes 2359296 | tf_op jit(solution)/shard_map/all_to_all | solution.py:663
  119.7 1.4 pack.1
  121.1 3.3 %collective-permute-start.8 = (bf16[2,120,128]{2,1,0:T(8,128)(2,1)}, bf16[2,120,128]{2,1,0:T(8,128)(2,1)S(1)}, u32[]{:S(2)}, u32[]{:S(2)}) collective-permute-start(bf16[2,120,128]{2,1,0:T(8,128)(2,1)} %get-tuple-element.55), channel_id=1, source_target_pairs={{0,64},{16,80},{32,96},{48,112},{64,0},{80,16},{96,32},{112,48},{1... | collective-permute-start | bytes 184328 | tf_op jit(solution)/shard_map/ppermute | solution.py:716
  124.4 5.3 %collective-permute-start.9 = (bf16[2,120,128]{2,1,0:T(8,128)(2,1)}, bf16[2,120,128]{2,1,0:T(8,128)(2,1)S(1)}, u32[]{:S(2)}, u32[]{:S(2)}) collective-permute-start(bf16[2,120,128]{2,1,0:T(8,128)(2,1)} %get-tuple-element.56), channel_id=1, source_target_pairs={{0,128},{16,144},{32,160},{48,176},{64,192},{80,208},{96,224},{112... | collective-permute-start | bytes 184328 | tf_op jit(solution)/shard_map/ppermute | solution.py:716
  129.7 3.7 %collective-permute-done.9.refs_2_ = bf16[2,120,128]{2,1,0:T(8,128)(2,1)S(1)} collective-permute-done((bf16[2,120,128]{2,1,0:T(8,128)(2,1)}, bf16[2,120,128]{2,1,0:T(8,128)(2,1)S(1)}, u32[]{:S(2)}, u32[]{:S(2)}) %collective-permute-start.9) | collective-permute-done | bytes 61472 | tf_op jit(solution)/shard_map/ppermute | solution.py:716
  133.3 2.9 %collective-permute-done.10.refs_3_ = bf16[2,120,128]{2,1,0:T(8,128)(2,1)S(1)} collective-permute-done((bf16[2,120,128]{2,1,0:T(8,128)(2,1)}, bf16[2,120,128]{2,1,0:T(8,128)(2,1)S(1)}, u32[]{:S(2)}, u32[]{:S(2)}) %collective-permute-start.10) | collective-permute-done | bytes 61472 | tf_op jit(solution)/shard_map/ppermute | solution.py:716
  136.2 1.5 merge.1
  138.4 3.4 %collective-permute-done.11.refs_1_ = bf16[120,128]{1,0:T(8,128)(2,1)S(1)} collective-permute-done((bf16[120,128]{1,0:T(8,128)(2,1)}, bf16[120,128]{1,0:T(8,128)(2,1)S(1)}, u32[]{:S(2)}, u32[]{:S(2)}) %collective-permute-start.11) | collective-permute-done | bytes 30752 | tf_op jit(solution)/shard_map/ppermute | solution.py:719
  141.8 1.6 total.1
  143.4 5.6 %all-to-all-start.5 = ((bf16[16,120,128]{2,1,0:T(8,128)(2,1)}), bf16[16,120,128]{2,1,0:T(8,128)(2,1)S(1)}, u32[]{:S(2)}, u32[]{:S(2)}) async-start(bf16[16,120,128]{2,1,0:T(8,128)(2,1)} %total.1), calls=%async_computation.5 | async-start | bytes 983040 | tf_op jit(solution)/shard_map/all_to_all | solution.py:663
  149.0 1.2 post.1
  150.2 14.2 %all-to-all-done.5.x_ref = bf16[16,120,128]{2,1,0:T(8,128)(2,1)S(1)} async-done(((bf16[16,120,128]{2,1,0:T(8,128)(2,1)}), bf16[16,120,128]{2,1,0:T(8,128)(2,1)S(1)}, u32[]{:S(2)}, u32[]{:S(2)}) %all-to-all-start.5) | async-done | bytes 491552 | tf_op jit(solution)/shard_map/all_to_all | solution.py:663
  (20 shorter events, 2.5 us)
Async XLA Ops:
  3.2 24.4 %all-to-all-start = ((bf16[16,288,128]{2,1,0:T(8,128)(2,1)}), bf16[16,288,128]{2,1,0:T(8,128)(2,1)S(1)}, u32[]{:S(2)}, u32[]{:S(2)}) async-start(bf16[16,288,128]{2,1,0:T(8,128)(2,1)} %get-tuple-element.37), calls=%async_computation | async-start | bytes 2359296 | tf_op jit(solution)/shard_map/all_to_all | solution.py:663
  10.7 16.9 %collective-permute-start = (bf16[48,1536]{1,0:T(8,128)(2,1)S(1)}, bf16[48,1536]{1,0:T(8,128)(2,1)S(1)}, u32[]{:S(2)}, u32[]{:S(2)}) collective-permute-start(bf16[48,1536]{1,0:T(8,128)(2,1)S(1)} %get-tuple-element.38), channel_id=1, source_target_pairs={{0,1},{1,2},{2,3},{3,4},{4,5},{5,6},{6,7},{7,8},{8,9},{9,10},{10,1... | collective-permute-start | bytes 442376 | tf_op jit(solution)/shard_map/ppermute | solution.py:689
  12.7 14.9 %collective-permute-start.1 = (bf16[48,1536]{1,0:T(8,128)(2,1)S(1)}, bf16[48,1536]{1,0:T(8,128)(2,1)S(1)}, u32[]{:S(2)}, u32[]{:S(2)}) collective-permute-start(bf16[48,1536]{1,0:T(8,128)(2,1)S(1)} %get-tuple-element.39), channel_id=1, source_target_pairs={{1,0},{2,1},{3,2},{4,3},{5,4},{6,5},{7,6},{8,7},{9,8},{10,9},{11,1... | collective-permute-start | bytes 442376 | tf_op jit(solution)/shard_map/ppermute | solution.py:690
  27.6 8.6 %copy-start = (bf16[48,1536]{1,0:T(8,128)(2,1)}, bf16[48,1536]{1,0:T(8,128)(2,1)S(1)}, u32[]{:S(2)}) copy-start(bf16[48,1536]{1,0:T(8,128)(2,1)S(1)} %collective-permute-done.left_hbm) | copy-start | bytes 442372
  27.6 8.6 %copy-start.1 = (bf16[48,1536]{1,0:T(8,128)(2,1)}, bf16[48,1536]{1,0:T(8,128)(2,1)S(1)}, u32[]{:S(2)}) copy-start(bf16[48,1536]{1,0:T(8,128)(2,1)S(1)} %collective-permute-done.1.right_hbm) | copy-start | bytes 442372
  36.2 15.7 %all-to-all-start.1 = ((bf16[16,144,128]{2,1,0:T(8,128)(2,1)}), bf16[16,144,128]{2,1,0:T(8,128)(2,1)S(1)}, u32[]{:S(2)}, u32[]{:S(2)}) async-start(bf16[16,144,128]{2,1,0:T(8,128)(2,1)} %get-tuple-element.41), calls=%async_computation.1 | async-start | bytes 1179648 | tf_op jit(solution)/shard_map/all_to_all | solution.py:663
  51.8 30.5 %collective-permute-start.2 = (bf16[16,144,128]{2,1,0:T(8,128)(2,1)S(1)}, bf16[16,144,128]{2,1,0:T(8,128)(2,1)S(1)}, u32[]{:S(2)}, u32[]{:S(2)}) collective-permute-start(bf16[16,144,128]{2,1,0:T(8,128)(2,1)S(1)} %all-to-all-done.1.att_ref.refs_0_), channel_id=1, source_target_pairs={{0,1},{1,0},{2,3},{3,2},{4,5},{5,4},{6,7},{7,6},{8,9},{9,8},{10,11... | collective-permute-start | bytes 1769480 | tf_op jit(solution)/shard_map/ppermute | solution.py:695
  52.9 15.5 %collective-permute-start.3 = (bf16[16,144,128]{2,1,0:T(8,128)(2,1)S(1)}, bf16[16,144,128]{2,1,0:T(8,128)(2,1)}, u32[]{:S(2)}, u32[]{:S(2)}) collective-permute-start(bf16[16,144,128]{2,1,0:T(8,128)(2,1)S(1)} %all-to-all-done.1.att_ref.refs_0_), channel_id=1, source_target_pairs={{0,32},{16,48},{32,0},{48,16},{64,96},{80,112},{96,64},{112,80},{1... | collective-permute-start | bytes 1769480 | tf_op jit(solution)/shard_map/ppermute | solution.py:694
  68.4 15.4 %collective-permute-start.4 = (bf16[16,144,128]{2,1,0:T(8,128)(2,1)}, bf16[16,144,128]{2,1,0:T(8,128)(2,1)}, u32[]{:S(2)}, u32[]{:S(2)}) collective-permute-start(bf16[16,144,128]{2,1,0:T(8,128)(2,1)} %collective-permute-done.3.refs_2_), channel_id=1, source_target_pairs={{0,1},{1,0},{2,3},{3,2},{4,5},{5,4},{6,7},{7,6},{8,9},{9,8},{10,11... | collective-permute-start | bytes 1769480 | tf_op jit(solution)/shard_map/ppermute | solution.py:702
  68.4 18.7 %all-to-all-start.2 = ((bf16[16,128,128]{2,1,0:T(8,128)(2,1)}), bf16[16,128,128]{2,1,0:T(8,128)(2,1)S(1)}, u32[]{:S(2)}, u32[]{:S(2)}) async-start(bf16[16,128,128]{2,1,0:T(8,128)(2,1)} %get-tuple-element.45), calls=%async_computation.2 | async-start | bytes 1048576 | tf_op jit(solution)/shard_map/all_to_all | solution.py:663
  75.2 7.2 %collective-permute-start.6 = (bf16[128,768]{1,0:T(8,128)(2,1)}, bf16[128,768]{1,0:T(8,128)(2,1)S(1)}, u32[]{:S(2)}, u32[]{:S(2)}) collective-permute-start(bf16[128,768]{1,0:T(8,128)(2,1)} %get-tuple-element.52), channel_id=1, source_target_pairs={{0,32},{16,48},{32,0},{48,16},{64,96},{80,112},{96,64},{112,80},{1... | collective-permute-start | bytes 589832 | tf_op jit(solution)/shard_map/ppermute | solution.py:704
  76.9 5.4 %collective-permute-start.5 = (bf16[128,768]{1,0:T(8,128)(2,1)}, bf16[128,768]{1,0:T(8,128)(2,1)S(1)}, u32[]{:S(2)}, u32[]{:S(2)}) collective-permute-start(bf16[128,768]{1,0:T(8,128)(2,1)} %get-tuple-element.51.refs_4_), channel_id=1, source_target_pairs={{0,1},{1,0},{2,3},{3,2},{4,5},{5,4},{6,7},{7,6},{8,9},{9,8},{10,11... | collective-permute-start | bytes 589832 | tf_op jit(solution)/shard_map/ppermute | solution.py:705
  82.4 1.4 collective-permute-start.7
  88.0 25.0 %all-to-all-start.3 = ((bf16[16,320,128]{2,1,0:T(8,128)(2,1)}), bf16[16,320,128]{2,1,0:T(8,128)(2,1)S(1)}, u32[]{:S(2)}, u32[]{:S(2)}) async-start(bf16[16,320,128]{2,1,0:T(8,128)(2,1)} %tail.1), calls=%async_computation.3 | async-start | bytes 2621440 | tf_op jit(solution)/shard_map/all_to_all | solution.py:663
  113.1 30.3 %all-to-all-start.4 = ((bf16[16,288,128]{2,1,0:T(8,128)(2,1)}), bf16[16,288,128]{2,1,0:T(8,128)(2,1)S(1)}, u32[]{:S(2)}, u32[]{:S(2)}) async-start(bf16[16,288,128]{2,1,0:T(8,128)(2,1)} %attend_back.1), calls=%async_computation.4 | async-start | bytes 2359296 | tf_op jit(solution)/shard_map/all_to_all | solution.py:663
  121.1 8.6 %collective-permute-start.8 = (bf16[2,120,128]{2,1,0:T(8,128)(2,1)}, bf16[2,120,128]{2,1,0:T(8,128)(2,1)S(1)}, u32[]{:S(2)}, u32[]{:S(2)}) collective-permute-start(bf16[2,120,128]{2,1,0:T(8,128)(2,1)} %get-tuple-element.55), channel_id=1, source_target_pairs={{0,64},{16,80},{32,96},{48,112},{64,0},{80,16},{96,32},{112,48},{1... | collective-permute-start | bytes 184328 | tf_op jit(solution)/shard_map/ppermute | solution.py:716
  124.4 8.9 %collective-permute-start.9 = (bf16[2,120,128]{2,1,0:T(8,128)(2,1)}, bf16[2,120,128]{2,1,0:T(8,128)(2,1)S(1)}, u32[]{:S(2)}, u32[]{:S(2)}) collective-permute-start(bf16[2,120,128]{2,1,0:T(8,128)(2,1)} %get-tuple-element.56), channel_id=1, source_target_pairs={{0,128},{16,144},{32,160},{48,176},{64,192},{80,208},{96,224},{112... | collective-permute-start | bytes 184328 | tf_op jit(solution)/shard_map/ppermute | solution.py:716
  129.7 6.5 %collective-permute-start.10 = (bf16[2,120,128]{2,1,0:T(8,128)(2,1)}, bf16[2,120,128]{2,1,0:T(8,128)(2,1)S(1)}, u32[]{:S(2)}, u32[]{:S(2)}) collective-permute-start(bf16[2,120,128]{2,1,0:T(8,128)(2,1)} %get-tuple-element.57), channel_id=1, source_target_pairs={{0,192},{16,208},{32,224},{48,240},{64,128},{80,144},{96,160},{112... | collective-permute-start | bytes 184328 | tf_op jit(solution)/shard_map/ppermute | solution.py:716
  137.7 4.1 %collective-permute-start.11 = (bf16[120,128]{1,0:T(8,128)(2,1)}, bf16[120,128]{1,0:T(8,128)(2,1)S(1)}, u32[]{:S(2)}, u32[]{:S(2)}) collective-permute-start(bf16[120,128]{1,0:T(8,128)(2,1)} %get-tuple-element.59), channel_id=1, source_target_pairs={{0,16},{16,0},{32,48},{48,32},{64,80},{80,64},{96,112},{112,96},{1... | collective-permute-start | bytes 92168 | tf_op jit(solution)/shard_map/ppermute | solution.py:719
  143.4 21.0 %all-to-all-start.5 = ((bf16[16,120,128]{2,1,0:T(8,128)(2,1)}), bf16[16,120,128]{2,1,0:T(8,128)(2,1)S(1)}, u32[]{:S(2)}, u32[]{:S(2)}) async-start(bf16[16,120,128]{2,1,0:T(8,128)(2,1)} %total.1), calls=%async_computation.5 | async-start | bytes 983040 | tf_op jit(solution)/shard_map/all_to_all | solution.py:663

commit v7 on v6

--- a/solution.py
+++ b/solution.py
@@ -691,21 +691,22 @@
     heads, left, right = lax.optimization_barrier((heads, left, right))
     weights, mixed, inv, payload = fwd(lengths, heads)
     attended = exchange(payload, "seq")
-    att_level = lax.ppermute(attended, "dp", levels)
-    att_core = lax.ppermute(attended, "seq", cores)
+    own = attended[:, 0:HEAD]
+    att_level = lax.ppermute(own, "dp", levels)
+    att_core = lax.ppermute(own, "seq", cores)
     member = depth // 4 * 2 + depth % 2
     info = jnp.stack([lengths[0], me * rows, me % 2, depth // 2 % 2, member]).astype(jnp.int32)
     block_out, payload, keep, send = conv(
         info, attended, res, cot, in_hbm(left), in_hbm(right), out_weight, conv_kernel
     )
-    att_level, send = lax.optimization_barrier((att_level, send))
+    att_level, payload = lax.optimization_barrier((att_level, payload))
     att_both = lax.ppermute(att_level, "seq", cores)
     grads = exchange(payload, "seq")
     level = lax.ppermute(send, "dp", levels)
     partner = lax.ppermute(keep, "seq", cores)
     both = lax.ppermute(level, "seq", cores)
     partial = outer(
-        info, (attended, att_core, att_level, att_both), (in_hbm(keep), partner, level, both)
+        info, (own, att_core, att_level, att_both), (in_hbm(keep), partner, level, both)
     )
     partial = exchange(tail(grads, partial), "seq")
     payload = bwd(heads, grads, in_hbm(weights), in_hbm(mixed), inv)

time: 167 us -> 163 us (0.976)
  starting transfers between devices: 59.8 us -> 57.5 us
  transfers between devices with their start and end apart: 18 -> 18, of which waited for: 10 -> 9; matrix products, arithmetic and copies ran while one was open for 0% -> 0% of each run, Pallas kernels for 20% -> 20%
where the time goes in v7:
time: 163 us; the launch traced here: 162 us
  waiting for transfers between devices  57.9 us (36%)
  starting transfers between devices  57.5 us (35%)
  Pallas kernels  45.2 us (28%)
    all_to_all x6, starting transfers between devices, exchange(): lax.all_to_all(x, axis, split_axis=0, concat_axis=0, tiled=True, axis_ind...  40.6 us
    all_to_all x6, waiting for transfers between devices, exchange(): lax.all_to_all(x, axis, split_axis=0, concat_axis=0, tiled=True, axis_ind...  29.1 us
    pallas_call x1, Pallas kernels, conv(): pl.pallas_call(conv_kernel_body, out_shape=(pltpu.HBM((rows, width), BF),...  11.9 us
    pallas_call x1, Pallas kernels, bwd(): pl.pallas_call(bwd_kernel, grid=(steps,), out_shape=pltpu.HBM((blocks, 3...  11.8 us
    ppermute x1, waiting for transfers between devices, shards(): left = lax.ppermute(edge_up, 'seq', up)  10.7 us
    pallas_call x1, Pallas kernels, fwd(): pl.pallas_call(fwd_kernel, out_shape=(pltpu.HBM((steps, frames, QT), BF),...  8.55 us
    ppermute x3, starting transfers between devices, shards(): lax.ppermute(packed[k], 'dp', hop(2 * k))  7.77 us
    ppermute x1, waiting for transfers between devices, shards(): level = lax.ppermute(send, 'dp', levels)  6.64 us
  transfers between devices with their start and end apart: 18, of which 9 were waited for; matrix products, arithmetic and copies ran while one was open for 0% of the time, Pallas kernels for 20%

profile of v7, /device:TPU:2, one launch (start us, length us, event | category | flops | bytes accessed | tf_op | source)
XLA Modules:
  0.0 162.1 jit_solution(16512242291506346827)
XLA Ops:
  0.6 2.5 %pre.1 = (bf16[16,288,128]{2,1,0:T(8,128)(2,1)}, bf16[48,1536]{1,0:T(8,128)(2,1)S(1)}, bf16[48,1536]{1,0:T(8,128)(2,1)S(1)}) custom-call(bf16[128,1536]{1,0:T(8,128)(2,1)} %bitcast.13, bf16[128,1536]{1,0:T(8,128)(2,1)} %bitcast.14, bf16[128,1536]{1,0:T(8,128)(2,1)} %bitcast.15, bf16[128,1536]{1,0:T(8,128)(2,1)} %bitcast.16, bf16[128,1536]{1,0:T(8,128)(2,1)} %bitcast.18), custom_call_target="tpu_custom_call" | custom-call | flops 1000000 | bytes 3000000 | tf_op jit(solution)/shard_map/pre/pallas_call | solution.py:72
  3.2 7.5 %all-to-all-start = ((bf16[16,288,128]{2,1,0:T(8,128)(2,1)}), bf16[16,288,128]{2,1,0:T(8,128)(2,1)S(1)}, u32[]{:S(2)}, u32[]{:S(2)}) async-start(bf16[16,288,128]{2,1,0:T(8,128)(2,1)} %get-tuple-element.37), calls=%async_computation | async-start | bytes 2359296 | tf_op jit(solution)/shard_map/all_to_all | solution.py:663
  10.7 2.0 %collective-permute-start = (bf16[48,1536]{1,0:T(8,128)(2,1)S(1)}, bf16[48,1536]{1,0:T(8,128)(2,1)S(1)}, u32[]{:S(2)}, u32[]{:S(2)}) collective-permute-start(bf16[48,1536]{1,0:T(8,128)(2,1)S(1)} %get-tuple-element.38), channel_id=1, source_target_pairs={{0,1},{1,2},{2,3},{3,4},{4,5},{5,6},{6,7},{7,8},{8,9},{9,10},{10,1... | collective-permute-start | bytes 442376 | tf_op jit(solution)/shard_map/ppermute | solution.py:689
  12.7 3.5 %collective-permute-start.1 = (bf16[48,1536]{1,0:T(8,128)(2,1)S(1)}, bf16[48,1536]{1,0:T(8,128)(2,1)S(1)}, u32[]{:S(2)}, u32[]{:S(2)}) collective-permute-start(bf16[48,1536]{1,0:T(8,128)(2,1)S(1)} %get-tuple-element.39), channel_id=1, source_target_pairs={{1,0},{2,1},{3,2},{4,3},{5,4},{6,5},{7,6},{8,7},{9,8},{10,9},{11,1... | collective-permute-start | bytes 442376 | tf_op jit(solution)/shard_map/ppermute | solution.py:690
  16.9 10.7 %collective-permute-done.left_hbm = bf16[48,1536]{1,0:T(8,128)(2,1)S(1)} collective-permute-done((bf16[48,1536]{1,0:T(8,128)(2,1)S(1)}, bf16[48,1536]{1,0:T(8,128)(2,1)S(1)}, u32[]{:S(2)}, u32[]{:S(2)}) %collective-permute-start) | collective-permute-done | bytes 147488 | tf_op jit(solution)/shard_map/ppermute | solution.py:689
  27.6 8.5 %attend.1 = (bf16[4,2048,512]{2,1,0:T(8,128)(2,1)}, f32[96,2048]{1,0:T(8,128)}, f32[8,2048]{1,0:T(8,128)S(1)}, bf16[16,144,128]{2,1,0:T(8,128)(2,1)}) custom-call(s32[1]{0:T(128)S(6)} %copy.16.len_ref, bf16[16,288,128]{2,1,0:T(8,128)(2,1)S(1)} %all-to-all-done.x_ref), custom_call_target="tpu_custom_call" | custom-call | flops 8999999488 | bytes 10000000 | tf_op jit(solution)/shard_map/attend/pallas_call | solution.py:167
  36.2 6.4 %all-to-all-start.1 = ((bf16[16,144,128]{2,1,0:T(8,128)(2,1)}), bf16[16,144,128]{2,1,0:T(8,128)(2,1)S(1)}, u32[]{:S(2)}, u32[]{:S(2)}) async-start(bf16[16,144,128]{2,1,0:T(8,128)(2,1)} %get-tuple-element.41), calls=%async_computation.1 | async-start | bytes 1179648 | tf_op jit(solution)/shard_map/all_to_all | solution.py:663
  42.7 9.1 %all-to-all-done.1.att_ref = bf16[16,144,128]{2,1,0:T(8,128)(2,1)S(1)} async-done(((bf16[16,144,128]{2,1,0:T(8,128)(2,1)}), bf16[16,144,128]{2,1,0:T(8,128)(2,1)S(1)}, u32[]{:S(2)}, u32[]{:S(2)}) %all-to-all-start.1) | async-done | bytes 589856 | tf_op jit(solution)/shard_map/all_to_all | solution.py:663
  51.9 2.0 %collective-permute-start.2 = (bf16[16,96,128]{2,1,0:T(8,128)(2,1)S(1)}, bf16[16,96,128]{2,1,0:T(8,128)(2,1)S(1)}, u32[]{:S(2)}, u32[]{:S(2)}) collective-permute-start(bf16[16,96,128]{2,1,0:T(8,128)(2,1)S(1)} %slice.4.refs_0_), channel_id=1, source_target_pairs={{0,32},{16,48},{32,0},{48,16},{64,96},{80,112},{96,64},{112,80},{1... | collective-permute-start | bytes 1179656 | tf_op jit(solution)/shard_map/ppermute | solution.py:695
  53.9 11.9 %convolve.1 = (bf16[128,1536]{1,0:T(8,128)(2,1)}, bf16[16,128,128]{2,1,0:T(8,128)(2,1)}, bf16[128,768]{1,0:T(8,128)(2,1)}, bf16[128,768]{1,0:T(8,128)(2,1)}) custom-call(s32[5]{0:T(128)S(1)} %stack.19.info_ref, bf16[16,144,128]{2,1,0:T(8,128)(2,1)S(1)} %all-to-all-done.1.att_ref, bf16[128,1536]{1,0:T(8,128)(2,1)} %bitcast.17, bf16[128,1536]{1,0:T(8,128)(2,1)} %bitcast.19, ...), custom_call_target="tpu_custom_call" | custom-call | flops 8999999488 | bytes 10000000 | tf_op jit(solution)/shard_map/convolve/pallas_call | solution.py:349
  65.8 7.3 %all-to-all-start.2 = ((bf16[16,128,128]{2,1,0:T(8,128)(2,1)}), bf16[16,128,128]{2,1,0:T(8,128)(2,1)S(1)}, u32[]{:S(2)}, u32[]{:S(2)}) async-start(bf16[16,128,128]{2,1,0:T(8,128)(2,1)} %get-tuple-element.46), calls=%async_computation.2 | async-start | bytes 1048576 | tf_op jit(solution)/shard_map/all_to_all | solution.py:663
  74.1 6.6 %collective-permute-done.6.refs_6_ = bf16[128,768]{1,0:T(8,128)(2,1)S(1)} collective-permute-done((bf16[128,768]{1,0:T(8,128)(2,1)}, bf16[128,768]{1,0:T(8,128)(2,1)S(1)}, u32[]{:S(2)}, u32[]{:S(2)}) %collective-permute-start.6) | collective-permute-done | bytes 196640 | tf_op jit(solution)/shard_map/ppermute | solution.py:705
  80.7 1.4 collective-permute-done.7.refs_7_
  82.1 3.0 %outer.1.w_ref = bf16[16,320,128]{2,1,0:T(8,128)(2,1)} custom-call(s32[5]{0:T(128)S(1)} %stack.19.info_ref, bf16[16,96,128]{2,1,0:T(8,128)(2,1)S(1)} %slice.4.refs_0_, bf16[16,96,128]{2,1,0:T(8,128)(2,1)S(1)} %collective-permute-done.3.refs_1_, bf16[16,96,128]{2,1,0:T(8,128)(2,1)S(1)} %collective-permute-done.2.refs_2_, ...), custom_call_target="tpu_custom_call" | custom-call | flops 1000000000 | bytes 4000000 | tf_op jit(solution)/shard_map/outer/pallas_call | solution.py:414
  85.2 0.8 tail.1
  86.0 7.3 %all-to-all-start.3 = ((bf16[16,320,128]{2,1,0:T(8,128)(2,1)}), bf16[16,320,128]{2,1,0:T(8,128)(2,1)S(1)}, u32[]{:S(2)}, u32[]{:S(2)}) async-start(bf16[16,320,128]{2,1,0:T(8,128)(2,1)} %tail.1), calls=%async_computation.3 | async-start | bytes 2621440 | tf_op jit(solution)/shard_map/all_to_all | solution.py:663
  93.3 11.8 %attend_back.1 = bf16[16,288,128]{2,1,0:T(8,128)(2,1)} custom-call(bf16[16,288,128]{2,1,0:T(8,128)(2,1)S(1)} %all-to-all-done.x_ref, bf16[16,128,128]{2,1,0:T(8,128)(2,1)S(1)} %all-to-all-done.2.g_ref, bf16[4,2048,512]{2,1,0:T(8,128)(2,1)} %get-tuple-element.47.e_ref, f32[96,2048]{1,0:T(8,128)} %get-tuple-element.48.o_ref, ...), custom_call_target="tpu_custom_call" | custom-call | flops 20000000000 | bytes 10000000 | tf_op jit(solution)/shard_map/attend_back/pallas_call | solution.py:512
  105.1 6.0 %all-to-all-done.3.x_ref = bf16[16,320,128]{2,1,0:T(8,128)(2,1)S(1)} async-done(((bf16[16,320,128]{2,1,0:T(8,128)(2,1)}), bf16[16,320,128]{2,1,0:T(8,128)(2,1)S(1)}, u32[]{:S(2)}, u32[]{:S(2)}) %all-to-all-start.3) | async-done | bytes 1310752 | tf_op jit(solution)/shard_map/all_to_all | solution.py:663
  111.1 6.6 %all-to-all-start.4 = ((bf16[16,288,128]{2,1,0:T(8,128)(2,1)}), bf16[16,288,128]{2,1,0:T(8,128)(2,1)S(1)}, u32[]{:S(2)}, u32[]{:S(2)}) async-start(bf16[16,288,128]{2,1,0:T(8,128)(2,1)} %attend_back.1), calls=%async_computation.4 | async-start | bytes 2359296 | tf_op jit(solution)/shard_map/all_to_all | solution.py:663
  117.7 1.4 pack.1
  119.1 3.3 %collective-permute-start.8 = (bf16[2,120,128]{2,1,0:T(8,128)(2,1)}, bf16[2,120,128]{2,1,0:T(8,128)(2,1)S(1)}, u32[]{:S(2)}, u32[]{:S(2)}) collective-permute-start(bf16[2,120,128]{2,1,0:T(8,128)(2,1)} %get-tuple-element.55), channel_id=1, source_target_pairs={{0,64},{16,80},{32,96},{48,112},{64,0},{80,16},{96,32},{112,48},{1... | collective-permute-start | bytes 184328 | tf_op jit(solution)/shard_map/ppermute | solution.py:717
  122.4 4.5 %collective-permute-start.9 = (bf16[2,120,128]{2,1,0:T(8,128)(2,1)}, bf16[2,120,128]{2,1,0:T(8,128)(2,1)S(1)}, u32[]{:S(2)}, u32[]{:S(2)}) collective-permute-start(bf16[2,120,128]{2,1,0:T(8,128)(2,1)} %get-tuple-element.56), channel_id=1, source_target_pairs={{0,128},{16,144},{32,160},{48,176},{64,192},{80,208},{96,224},{112... | collective-permute-start | bytes 184328 | tf_op jit(solution)/shard_map/ppermute | solution.py:717
  126.9 3.8 %collective-permute-done.9.refs_2_ = bf16[2,120,128]{2,1,0:T(8,128)(2,1)S(1)} collective-permute-done((bf16[2,120,128]{2,1,0:T(8,128)(2,1)}, bf16[2,120,128]{2,1,0:T(8,128)(2,1)S(1)}, u32[]{:S(2)}, u32[]{:S(2)}) %collective-permute-start.9) | collective-permute-done | bytes 61472 | tf_op jit(solution)/shard_map/ppermute | solution.py:717
  130.7 2.7 %collective-permute-done.10.refs_3_ = bf16[2,120,128]{2,1,0:T(8,128)(2,1)S(1)} collective-permute-done((bf16[2,120,128]{2,1,0:T(8,128)(2,1)}, bf16[2,120,128]{2,1,0:T(8,128)(2,1)S(1)}, u32[]{:S(2)}, u32[]{:S(2)}) %collective-permute-start.10) | collective-permute-done | bytes 61472 | tf_op jit(solution)/shard_map/ppermute | solution.py:717
  133.4 1.5 merge.1
  134.9 0.7 collective-permute-start.11
  135.6 3.4 %collective-permute-done.11.refs_1_ = bf16[120,128]{1,0:T(8,128)(2,1)S(1)} collective-permute-done((bf16[120,128]{1,0:T(8,128)(2,1)}, bf16[120,128]{1,0:T(8,128)(2,1)S(1)}, u32[]{:S(2)}, u32[]{:S(2)}) %collective-permute-start.11) | collective-permute-done | bytes 30752 | tf_op jit(solution)/shard_map/ppermute | solution.py:720
  139.0 1.6 total.1
  140.6 5.4 %all-to-all-start.5 = ((bf16[16,120,128]{2,1,0:T(8,128)(2,1)}), bf16[16,120,128]{2,1,0:T(8,128)(2,1)S(1)}, u32[]{:S(2)}, u32[]{:S(2)}) async-start(bf16[16,120,128]{2,1,0:T(8,128)(2,1)} %total.1), calls=%async_computation.5 | async-start | bytes 983040 | tf_op jit(solution)/shard_map/all_to_all | solution.py:663
  146.0 1.2 post.1
  147.2 14.0 %all-to-all-done.5.x_ref = bf16[16,120,128]{2,1,0:T(8,128)(2,1)S(1)} async-done(((bf16[16,120,128]{2,1,0:T(8,128)(2,1)}), bf16[16,120,128]{2,1,0:T(8,128)(2,1)S(1)}, u32[]{:S(2)}, u32[]{:S(2)}) %all-to-all-start.5) | async-done | bytes 491552 | tf_op jit(solution)/shard_map/all_to_all | solution.py:663
  161.2 0.9 unpack.1
  (21 shorter events, 1.0 us)
Async XLA Ops:
  3.2 24.4 %all-to-all-start = ((bf16[16,288,128]{2,1,0:T(8,128)(2,1)}), bf16[16,288,128]{2,1,0:T(8,128)(2,1)S(1)}, u32[]{:S(2)}, u32[]{:S(2)}) async-start(bf16[16,288,128]{2,1,0:T(8,128)(2,1)} %get-tuple-element.37), calls=%async_computation | async-start | bytes 2359296 | tf_op jit(solution)/shard_map/all_to_all | solution.py:663
  10.7 16.9 %collective-permute-start = (bf16[48,1536]{1,0:T(8,128)(2,1)S(1)}, bf16[48,1536]{1,0:T(8,128)(2,1)S(1)}, u32[]{:S(2)}, u32[]{:S(2)}) collective-permute-start(bf16[48,1536]{1,0:T(8,128)(2,1)S(1)} %get-tuple-element.38), channel_id=1, source_target_pairs={{0,1},{1,2},{2,3},{3,4},{4,5},{5,6},{6,7},{7,8},{8,9},{9,10},{10,1... | collective-permute-start | bytes 442376 | tf_op jit(solution)/shard_map/ppermute | solution.py:689
  12.7 14.9 %collective-permute-start.1 = (bf16[48,1536]{1,0:T(8,128)(2,1)S(1)}, bf16[48,1536]{1,0:T(8,128)(2,1)S(1)}, u32[]{:S(2)}, u32[]{:S(2)}) collective-permute-start(bf16[48,1536]{1,0:T(8,128)(2,1)S(1)} %get-tuple-element.39), channel_id=1, source_target_pairs={{1,0},{2,1},{3,2},{4,3},{5,4},{6,5},{7,6},{8,7},{9,8},{10,9},{11,1... | collective-permute-start | bytes 442376 | tf_op jit(solution)/shard_map/ppermute | solution.py:690
  27.6 8.6 %copy-start = (bf16[48,1536]{1,0:T(8,128)(2,1)}, bf16[48,1536]{1,0:T(8,128)(2,1)S(1)}, u32[]{:S(2)}) copy-start(bf16[48,1536]{1,0:T(8,128)(2,1)S(1)} %collective-permute-done.left_hbm) | copy-start | bytes 442372
  27.6 8.6 %copy-start.1 = (bf16[48,1536]{1,0:T(8,128)(2,1)}, bf16[48,1536]{1,0:T(8,128)(2,1)S(1)}, u32[]{:S(2)}) copy-start(bf16[48,1536]{1,0:T(8,128)(2,1)S(1)} %collective-permute-done.1.right_hbm) | copy-start | bytes 442372
  36.2 15.7 %all-to-all-start.1 = ((bf16[16,144,128]{2,1,0:T(8,128)(2,1)}), bf16[16,144,128]{2,1,0:T(8,128)(2,1)S(1)}, u32[]{:S(2)}, u32[]{:S(2)}) async-start(bf16[16,144,128]{2,1,0:T(8,128)(2,1)} %get-tuple-element.41), calls=%async_computation.1 | async-start | bytes 1179648 | tf_op jit(solution)/shard_map/all_to_all | solution.py:663
  51.9 14.0 %collective-permute-start.2 = (bf16[16,96,128]{2,1,0:T(8,128)(2,1)S(1)}, bf16[16,96,128]{2,1,0:T(8,128)(2,1)S(1)}, u32[]{:S(2)}, u32[]{:S(2)}) collective-permute-start(bf16[16,96,128]{2,1,0:T(8,128)(2,1)S(1)} %slice.4.refs_0_), channel_id=1, source_target_pairs={{0,32},{16,48},{32,0},{48,16},{64,96},{80,112},{96,64},{112,80},{1... | collective-permute-start | bytes 1179656 | tf_op jit(solution)/shard_map/ppermute | solution.py:695
  65.8 19.4 %all-to-all-start.2 = ((bf16[16,128,128]{2,1,0:T(8,128)(2,1)}), bf16[16,128,128]{2,1,0:T(8,128)(2,1)S(1)}, u32[]{:S(2)}, u32[]{:S(2)}) async-start(bf16[16,128,128]{2,1,0:T(8,128)(2,1)} %get-tuple-element.46), calls=%async_computation.2 | async-start | bytes 1048576 | tf_op jit(solution)/shard_map/all_to_all | solution.py:663
  73.2 7.5 %collective-permute-start.3 = (bf16[16,96,128]{2,1,0:T(8,128)(2,1)S(1)}, bf16[16,96,128]{2,1,0:T(8,128)(2,1)S(1)}, u32[]{:S(2)}, u32[]{:S(2)}) collective-permute-start(bf16[16,96,128]{2,1,0:T(8,128)(2,1)S(1)} %slice.4.refs_0_), channel_id=1, source_target_pairs={{0,1},{1,0},{2,3},{3,2},{4,5},{5,4},{6,7},{7,6},{8,9},{9,8},{10,11... | collective-permute-start | bytes 1179656 | tf_op jit(solution)/shard_map/ppermute | solution.py:696
  73.3 7.4 %collective-permute-start.6 = (bf16[128,768]{1,0:T(8,128)(2,1)}, bf16[128,768]{1,0:T(8,128)(2,1)S(1)}, u32[]{:S(2)}, u32[]{:S(2)}) collective-permute-start(bf16[128,768]{1,0:T(8,128)(2,1)} %get-tuple-element.52), channel_id=1, source_target_pairs={{0,32},{16,48},{32,0},{48,16},{64,96},{80,112},{96,64},{112,80},{1... | collective-permute-start | bytes 589832 | tf_op jit(solution)/shard_map/ppermute | solution.py:705
  73.4 8.7 %collective-permute-start.4 = (bf16[16,96,128]{2,1,0:T(8,128)(2,1)S(1)}, bf16[16,96,128]{2,1,0:T(8,128)(2,1)S(1)}, u32[]{:S(2)}, u32[]{:S(2)}) collective-permute-start(bf16[16,96,128]{2,1,0:T(8,128)(2,1)S(1)} %collective-permute-done.2.refs_2_), channel_id=1, source_target_pairs={{0,1},{1,0},{2,3},{3,2},{4,5},{5,4},{6,7},{7,6},{8,9},{9,8},{10,11... | collective-permute-start | bytes 1179656 | tf_op jit(solution)/shard_map/ppermute | solution.py:703
  73.7 7.0 %collective-permute-start.5 = (bf16[128,768]{1,0:T(8,128)(2,1)}, bf16[128,768]{1,0:T(8,128)(2,1)S(1)}, u32[]{:S(2)}, u32[]{:S(2)}) collective-permute-start(bf16[128,768]{1,0:T(8,128)(2,1)} %get-tuple-element.51.refs_4_), channel_id=1, source_target_pairs={{0,1},{1,0},{2,3},{3,2},{4,5},{5,4},{6,7},{7,6},{8,9},{9,8},{10,11... | collective-permute-start | bytes 589832 | tf_op jit(solution)/shard_map/ppermute | solution.py:706
  80.7 1.4 collective-permute-start.7
  86.0 25.0 %all-to-all-start.3 = ((bf16[16,320,128]{2,1,0:T(8,128)(2,1)}), bf16[16,320,128]{2,1,0:T(8,128)(2,1)S(1)}, u32[]{:S(2)}, u32[]{:S(2)}) async-start(bf16[16,320,128]{2,1,0:T(8,128)(2,1)} %tail.1), calls=%async_computation.3 | async-start | bytes 2621440 | tf_op jit(solution)/shard_map/all_to_all | solution.py:663
  111.1 29.5 %all-to-all-start.4 = ((bf16[16,288,128]{2,1,0:T(8,128)(2,1)}), bf16[16,288,128]{2,1,0:T(8,128)(2,1)S(1)}, u32[]{:S(2)}, u32[]{:S(2)}) async-start(bf16[16,288,128]{2,1,0:T(8,128)(2,1)} %attend_back.1), calls=%async_computation.4 | async-start | bytes 2359296 | tf_op jit(solution)/shard_map/all_to_all | solution.py:663
  119.1 7.8 %collective-permute-start.8 = (bf16[2,120,128]{2,1,0:T(8,128)(2,1)}, bf16[2,120,128]{2,1,0:T(8,128)(2,1)S(1)}, u32[]{:S(2)}, u32[]{:S(2)}) collective-permute-start(bf16[2,120,128]{2,1,0:T(8,128)(2,1)} %get-tuple-element.55), channel_id=1, source_target_pairs={{0,64},{16,80},{32,96},{48,112},{64,0},{80,16},{96,32},{112,48},{1... | collective-permute-start | bytes 184328 | tf_op jit(solution)/shard_map/ppermute | solution.py:717
  122.4 8.3 %collective-permute-start.9 = (bf16[2,120,128]{2,1,0:T(8,128)(2,1)}, bf16[2,120,128]{2,1,0:T(8,128)(2,1)S(1)}, u32[]{:S(2)}, u32[]{:S(2)}) collective-permute-start(bf16[2,120,128]{2,1,0:T(8,128)(2,1)} %get-tuple-element.56), channel_id=1, source_target_pairs={{0,128},{16,144},{32,160},{48,176},{64,192},{80,208},{96,224},{112... | collective-permute-start | bytes 184328 | tf_op jit(solution)/shard_map/ppermute | solution.py:717
  126.9 6.5 %collective-permute-start.10 = (bf16[2,120,128]{2,1,0:T(8,128)(2,1)}, bf16[2,120,128]{2,1,0:T(8,128)(2,1)S(1)}, u32[]{:S(2)}, u32[]{:S(2)}) collective-permute-start(bf16[2,120,128]{2,1,0:T(8,128)(2,1)} %get-tuple-element.57), channel_id=1, source_target_pairs={{0,192},{16,208},{32,224},{48,240},{64,128},{80,144},{96,160},{112... | collective-permute-start | bytes 184328 | tf_op jit(solution)/shard_map/ppermute | solution.py:717
  134.9 4.1 %collective-permute-start.11 = (bf16[120,128]{1,0:T(8,128)(2,1)}, bf16[120,128]{1,0:T(8,128)(2,1)S(1)}, u32[]{:S(2)}, u32[]{:S(2)}) collective-permute-start(bf16[120,128]{1,0:T(8,128)(2,1)} %get-tuple-element.59), channel_id=1, source_target_pairs={{0,16},{16,0},{32,48},{48,32},{64,80},{80,64},{96,112},{112,96},{1... | collective-permute-start | bytes 92168 | tf_op jit(solution)/shard_map/ppermute | solution.py:720
  140.6 20.6 %all-to-all-start.5 = ((bf16[16,120,128]{2,1,0:T(8,128)(2,1)}), bf16[16,120,128]{2,1,0:T(8,128)(2,1)S(1)}, u32[]{:S(2)}, u32[]{:S(2)}) async-start(bf16[16,120,128]{2,1,0:T(8,128)(2,1)} %total.1), calls=%async_computation.5 | async-start | bytes 983040 | tf_op jit(solution)/shard_map/all_to_all | solution.py:663

commit v8 on v7

--- a/solution.py
+++ b/solution.py
@@ -568,7 +568,7 @@
                 buf[8 * n : 8 * n + 8, :] = both[8 * e : 8 * e + 8, :]
     share = buf.shape[0] // GROUP
     for k in range(GROUP):
-        j = jnp.bitwise_xor(info_ref[4], k)
+        j = 2 * jnp.bitwise_xor(info_ref[4], k // 2) + k % 2
         taps = [x_ref[2 * j + e, below : below + 32, :].astype(F32)[0:24] for e in range(2)]
         outs[k // 2][k % 2] = jnp.concatenate(
             [buf[pl.ds(pl.multiple_of(share * j, 8), share), :]] + taps, axis=0
@@ -589,37 +589,34 @@
 
 
 def merge_kernel(*refs):
-    keep_ref, send_ref = refs[-2:]
-    both = sum([ref[...].astype(F32) for ref in refs[1:-2]], refs[0][...].astype(F32))
-    keep_ref[...] = both[0].astype(BF)
-    send_ref[...] = both[1].astype(BF)
+    o_ref = refs[-1]
+    both = sum([ref[...].astype(F32) for ref in refs[1:-1]], refs[0][...].astype(F32))
+    o_ref[...] = both.astype(BF)
 
 
 def merge(xs):
     return pl.pallas_call(
         merge_kernel,
-        out_shape=(pltpu.HBM(xs[0].shape[1:], BF),) * 2,
+        out_shape=pltpu.HBM(xs[0].shape, BF),
         compiler_params=params(8),
         cost_estimate=cost(1e6, 1e6),
         name="merge",
     )(*xs)
 
 
-def total_kernel(*refs):
-    o_ref = refs[-1]
-    total = sum([ref[...].astype(F32) for ref in refs[1:-1]], refs[0][...].astype(F32))
-    total = total * (1.0 / o_ref.shape[0])
-    o_ref[...] = jnp.broadcast_to(total.astype(BF)[None], o_ref.shape)
-
-
-def total(xs, batch):
+def total_kernel(a_ref, b_ref, o_ref):
+    both = (a_ref[...].astype(F32) + b_ref[...].astype(F32)) * (0.5 / o_ref.shape[0])
+    o_ref[...] = jnp.broadcast_to(both.astype(BF)[None], o_ref.shape)
+
+
+def total(a, b):
     return pl.pallas_call(
         total_kernel,
-        out_shape=pltpu.HBM((batch,) + xs[0].shape, BF),
+        out_shape=pltpu.HBM((GROUP,) + a.shape, BF),
         compiler_params=params(12),
         cost_estimate=cost(1e6, 1e6),
         name="total",
-    )(*xs)
+    )(a, b)
 
 
 def unpack_kernel(x_ref, w_ref, k_ref):
@@ -628,13 +625,13 @@
     share = HEAD // 8 * cols // 2 // GROUP
     for z in range(2):
         for j in range(GROUP):
-            x = x_ref[4 * (j // 2) + 2 * z + j % 2].astype(F32)
+            x = x_ref[j // 2 * 2 + z, j % 2].astype(F32)
             for i in range(share):
                 n = j * share + i
                 r, c = 8 * (n // (cols // 2)), width // 2 * z + LANES * (n % (cols // 2))
                 w_ref[r : r + 8, c : c + LANES] = x[8 * i : 8 * i + 8, :]
     for j in range(GROUP):
-        x = x_ref[4 * (j // 2) + j % 2].astype(F32) + x_ref[4 * (j // 2) + 2 + j % 2].astype(F32)
+        x = x_ref[j // 2 * 2, j % 2].astype(F32) + x_ref[j // 2 * 2 + 1, j % 2].astype(F32)
         for i in range(4):
             if 4 * j + i < TAPS:
                 for c in range(cols):
@@ -686,15 +683,16 @@
     )
     payload, edge_up, edge_down = pre(query, key, value, res, cot)
     heads = exchange(payload, "seq")
+    heads, edge_up, edge_down = lax.optimization_barrier((heads, edge_up, edge_down))
     left = lax.ppermute(edge_up, "seq", up)
     right = lax.ppermute(edge_down, "seq", down)
-    heads, left, right = lax.optimization_barrier((heads, left, right))
     weights, mixed, inv, payload = fwd(lengths, heads)
+    payload, left, right = lax.optimization_barrier((payload, left, right))
     attended = exchange(payload, "seq")
     own = attended[:, 0:HEAD]
     att_level = lax.ppermute(own, "dp", levels)
     att_core = lax.ppermute(own, "seq", cores)
-    member = depth // 4 * 2 + depth % 2
+    member = depth // 4
     info = jnp.stack([lengths[0], me * rows, me % 2, depth // 2 % 2, member]).astype(jnp.int32)
     block_out, payload, keep, send = conv(
         info, attended, res, cot, in_hbm(left), in_hbm(right), out_weight, conv_kernel
@@ -716,10 +714,11 @@
     level_parts = [in_hbm(packed[0])] + [
         lax.ppermute(packed[k], "dp", hop(2 * k)) for k in range(1, GROUP // 2)
     ]
-    keep, send = merge(level_parts)
-    packed = [in_hbm(keep), lax.ppermute(send, "dp", hop(1))]
-    summed, back = lax.optimization_barrier((total(packed, batch), back))
-    final = exchange(summed, "dp")
+    merged = merge(level_parts)
+    summed = total(in_hbm(merged), lax.ppermute(merged, "dp", hop(1)))
+    summed, back = lax.optimization_barrier((summed, back))
+    column = [[i for i in range(batch) if i % 2 == y] for y in range(2)]
+    final = exchange(summed, "dp", column)
     query_grad, key_grad, value_grad = post(back)
     weight_grad, kernel_grad = unpack(final, width)
     return (

time: 163 us -> 170 us (1.043)
  waiting for transfers between devices: 57.9 us -> 63.4 us
  starting transfers between devices: 57.5 us -> 59.5 us
    all_to_all x6, waiting for transfers between devices: 29.1 us -> 45 us  [exchange(): lax.all_to_all(x, axis, split_axis=0, concat_axis=0, tiled=True, axis_ind...]
    ppermute x1, waiting for transfers between devices: 10.7 us -> 0.01 us  [shards(): left = lax.ppermute(edge_up, 'seq', up)]
  transfers between devices with their start and end apart: 18 -> 18, of which waited for: 9 -> 9; matrix products, arithmetic and copies ran while one was open for 0% -> 0% of each run, Pallas kernels for 20% -> 24%
where the time goes in v8:
time: 170 us
  waiting for transfers between devices  63.4 us (37%)
  starting transfers between devices  59.5 us (35%)
  Pallas kernels  45.3 us (27%)
    all_to_all x6, waiting for transfers between devices, exchange(): lax.all_to_all(x, axis, split_axis=0, concat_axis=0, tiled=True, axis_ind...  45 us
    all_to_all x6, starting transfers between devices, exchange(): lax.all_to_all(x, axis, split_axis=0, concat_axis=0, tiled=True, axis_ind...  41.8 us
    pallas_call x1, Pallas kernels, conv(): pl.pallas_call(conv_kernel_body, out_shape=(pltpu.HBM((rows, width), BF),...  11.9 us
    pallas_call x1, Pallas kernels, bwd(): pl.pallas_call(bwd_kernel, grid=(steps,), out_shape=pltpu.HBM((blocks, 3...  11.7 us
    pallas_call x1, Pallas kernels, fwd(): pl.pallas_call(fwd_kernel, out_shape=(pltpu.HBM((steps, frames, QT), BF),...  8.57 us
    ppermute x3, starting transfers between devices, shards(): lax.ppermute(packed[k], 'dp', hop(2 * k))  7.78 us
    ppermute x1, waiting for transfers between devices, shards(): level = lax.ppermute(send, 'dp', levels)  6.64 us
    ppermute x3, waiting for transfers between devices, shards(): lax.ppermute(packed[k], 'dp', hop(2 * k))  6.54 us
  transfers between devices with their start and end apart: 18, of which 9 were waited for; matrix products, arithmetic and copies ran while one was open for 0% of the time, Pallas kernels for 24%

profile of v8, /device:TPU:2, one launch (start us, length us, event | category | flops | bytes accessed | tf_op | source)
XLA Modules:
  0.0 169.7 jit_solution(8666894079890531546)
XLA Ops:
  0.6 2.6 %pre.1 = (bf16[16,288,128]{2,1,0:T(8,128)(2,1)}, bf16[48,1536]{1,0:T(8,128)(2,1)S(1)}, bf16[48,1536]{1,0:T(8,128)(2,1)S(1)}) custom-call(bf16[128,1536]{1,0:T(8,128)(2,1)} %bitcast.13, bf16[128,1536]{1,0:T(8,128)(2,1)} %bitcast.14, bf16[128,1536]{1,0:T(8,128)(2,1)} %bitcast.15, bf16[128,1536]{1,0:T(8,128)(2,1)} %bitcast.16, bf16[128,1536]{1,0:T(8,128)(2,1)} %bitcast.18), custom_call_target="tpu_custom_call" | custom-call | flops 1000000 | bytes 3000000 | tf_op jit(solution)/shard_map/pre/pallas_call | solution.py:72
  3.2 7.5 %all-to-all-start = ((bf16[16,288,128]{2,1,0:T(8,128)(2,1)}), bf16[16,288,128]{2,1,0:T(8,128)(2,1)S(1)}, u32[]{:S(2)}, u32[]{:S(2)}) async-start(bf16[16,288,128]{2,1,0:T(8,128)(2,1)} %get-tuple-element.38), calls=%async_computation | async-start | bytes 2359296 | tf_op jit(solution)/shard_map/all_to_all | solution.py:660
  11.3 15.7 %all-to-all-done.x_ref = bf16[16,288,128]{2,1,0:T(8,128)(2,1)S(1)} async-done(((bf16[16,288,128]{2,1,0:T(8,128)(2,1)}), bf16[16,288,128]{2,1,0:T(8,128)(2,1)S(1)}, u32[]{:S(2)}, u32[]{:S(2)}) %all-to-all-start) | async-done | bytes 1179680 | tf_op jit(solution)/shard_map/all_to_all | solution.py:660
  27.0 2.2 %collective-permute-start = (bf16[48,1536]{1,0:T(8,128)(2,1)S(1)}, bf16[48,1536]{1,0:T(8,128)(2,1)S(1)}, u32[]{:S(2)}, u32[]{:S(2)}) collective-permute-start(bf16[48,1536]{1,0:T(8,128)(2,1)S(1)} %get-tuple-element.43), channel_id=1, source_target_pairs={{0,1},{1,2},{2,3},{3,4},{4,5},{5,6},{6,7},{7,8},{8,9},{9,10},{10,1... | collective-permute-start | bytes 442376 | tf_op jit(solution)/shard_map/ppermute | solution.py:687
  29.2 4.2 %collective-permute-start.1 = (bf16[48,1536]{1,0:T(8,128)(2,1)S(1)}, bf16[48,1536]{1,0:T(8,128)(2,1)S(1)}, u32[]{:S(2)}, u32[]{:S(2)}) collective-permute-start(bf16[48,1536]{1,0:T(8,128)(2,1)S(1)} %get-tuple-element.44), channel_id=1, source_target_pairs={{1,0},{2,1},{3,2},{4,3},{5,4},{6,5},{7,6},{8,7},{9,8},{10,9},{11,1... | collective-permute-start | bytes 442376 | tf_op jit(solution)/shard_map/ppermute | solution.py:688
  33.4 8.6 %attend.1 = (bf16[4,2048,512]{2,1,0:T(8,128)(2,1)}, f32[96,2048]{1,0:T(8,128)}, f32[8,2048]{1,0:T(8,128)S(1)}, bf16[16,144,128]{2,1,0:T(8,128)(2,1)}) custom-call(s32[1]{0:T(128)S(6)} %copy.16.len_ref, bf16[16,288,128]{2,1,0:T(8,128)(2,1)S(1)} %all-to-all-done.x_ref), custom_call_target="tpu_custom_call" | custom-call | flops 8999999488 | bytes 10000000 | tf_op jit(solution)/shard_map/attend/pallas_call | solution.py:167
  42.0 7.8 %all-to-all-start.1 = ((bf16[16,144,128]{2,1,0:T(8,128)(2,1)}), bf16[16,144,128]{2,1,0:T(8,128)(2,1)S(1)}, u32[]{:S(2)}, u32[]{:S(2)}) async-start(bf16[16,144,128]{2,1,0:T(8,128)(2,1)} %get-tuple-element.45), calls=%async_computation.1 | async-start | bytes 1179648 | tf_op jit(solution)/shard_map/all_to_all | solution.py:660
  49.9 9.1 %all-to-all-done.1.att_ref = bf16[16,144,128]{2,1,0:T(8,128)(2,1)S(1)} async-done(((bf16[16,144,128]{2,1,0:T(8,128)(2,1)}), bf16[16,144,128]{2,1,0:T(8,128)(2,1)S(1)}, u32[]{:S(2)}, u32[]{:S(2)}) %all-to-all-start.1) | async-done | bytes 589856 | tf_op jit(solution)/shard_map/all_to_all | solution.py:660
  59.1 2.0 %collective-permute-start.2 = (bf16[16,96,128]{2,1,0:T(8,128)(2,1)S(1)}, bf16[16,96,128]{2,1,0:T(8,128)(2,1)S(1)}, u32[]{:S(2)}, u32[]{:S(2)}) collective-permute-start(bf16[16,96,128]{2,1,0:T(8,128)(2,1)S(1)} %slice.4.refs_0_), channel_id=1, source_target_pairs={{0,32},{16,48},{32,0},{48,16},{64,96},{80,112},{96,64},{112,80},{1... | collective-permute-start | bytes 1179656 | tf_op jit(solution)/shard_map/ppermute | solution.py:693
  61.1 11.9 %convolve.1 = (bf16[128,1536]{1,0:T(8,128)(2,1)}, bf16[16,128,128]{2,1,0:T(8,128)(2,1)}, bf16[128,768]{1,0:T(8,128)(2,1)}, bf16[128,768]{1,0:T(8,128)(2,1)}) custom-call(s32[5]{0:T(128)S(1)} %stack.19.info_ref, bf16[16,144,128]{2,1,0:T(8,128)(2,1)S(1)} %all-to-all-done.1.att_ref, bf16[128,1536]{1,0:T(8,128)(2,1)} %bitcast.17, bf16[128,1536]{1,0:T(8,128)(2,1)} %bitcast.19, ...), custom_call_target="tpu_custom_call" | custom-call | flops 8999999488 | bytes 10000000 | tf_op jit(solution)/shard_map/convolve/pallas_call | solution.py:349
  73.0 7.3 %all-to-all-start.2 = ((bf16[16,128,128]{2,1,0:T(8,128)(2,1)}), bf16[16,128,128]{2,1,0:T(8,128)(2,1)S(1)}, u32[]{:S(2)}, u32[]{:S(2)}) async-start(bf16[16,128,128]{2,1,0:T(8,128)(2,1)} %get-tuple-element.50), calls=%async_computation.2 | async-start | bytes 1048576 | tf_op jit(solution)/shard_map/all_to_all | solution.py:660
  81.3 6.6 %collective-permute-done.6.refs_6_ = bf16[128,768]{1,0:T(8,128)(2,1)S(1)} collective-permute-done((bf16[128,768]{1,0:T(8,128)(2,1)}, bf16[128,768]{1,0:T(8,128)(2,1)S(1)}, u32[]{:S(2)}, u32[]{:S(2)}) %collective-permute-start.6) | collective-permute-done | bytes 196640 | tf_op jit(solution)/shard_map/ppermute | solution.py:703
  87.9 1.4 collective-permute-done.7.refs_7_
  89.3 3.0 %outer.1.w_ref = bf16[16,320,128]{2,1,0:T(8,128)(2,1)} custom-call(s32[5]{0:T(128)S(1)} %stack.19.info_ref, bf16[16,96,128]{2,1,0:T(8,128)(2,1)S(1)} %slice.4.refs_0_, bf16[16,96,128]{2,1,0:T(8,128)(2,1)S(1)} %collective-permute-done.3.refs_1_, bf16[16,96,128]{2,1,0:T(8,128)(2,1)S(1)} %collective-permute-done.2.refs_2_, ...), custom_call_target="tpu_custom_call" | custom-call | flops 1000000000 | bytes 4000000 | tf_op jit(solution)/shard_map/outer/pallas_call | solution.py:414
  92.4 0.8 tail.1
  93.2 7.3 %all-to-all-start.3 = ((bf16[16,320,128]{2,1,0:T(8,128)(2,1)}), bf16[16,320,128]{2,1,0:T(8,128)(2,1)S(1)}, u32[]{:S(2)}, u32[]{:S(2)}) async-start(bf16[16,320,128]{2,1,0:T(8,128)(2,1)} %tail.1), calls=%async_computation.3 | async-start | bytes 2621440 | tf_op jit(solution)/shard_map/all_to_all | solution.py:660
  100.6 11.7 %attend_back.1 = bf16[16,288,128]{2,1,0:T(8,128)(2,1)} custom-call(bf16[16,288,128]{2,1,0:T(8,128)(2,1)S(1)} %all-to-all-done.x_ref, bf16[16,128,128]{2,1,0:T(8,128)(2,1)S(1)} %all-to-all-done.2.g_ref, bf16[4,2048,512]{2,1,0:T(8,128)(2,1)} %get-tuple-element.51.e_ref, f32[96,2048]{1,0:T(8,128)} %get-tuple-element.52.o_ref, ...), custom_call_target="tpu_custom_call" | custom-call | flops 20000000000 | bytes 10000000 | tf_op jit(solution)/shard_map/attend_back/pallas_call | solution.py:512
  112.3 6.0 %all-to-all-done.3.x_ref = bf16[16,320,128]{2,1,0:T(8,128)(2,1)S(1)} async-done(((bf16[16,320,128]{2,1,0:T(8,128)(2,1)}), bf16[16,320,128]{2,1,0:T(8,128)(2,1)S(1)}, u32[]{:S(2)}, u32[]{:S(2)}) %all-to-all-start.3) | async-done | bytes 1310752 | tf_op jit(solution)/shard_map/all_to_all | solution.py:660
  118.3 6.6 %all-to-all-start.4 = ((bf16[16,288,128]{2,1,0:T(8,128)(2,1)}), bf16[16,288,128]{2,1,0:T(8,128)(2,1)S(1)}, u32[]{:S(2)}, u32[]{:S(2)}) async-start(bf16[16,288,128]{2,1,0:T(8,128)(2,1)} %attend_back.1), calls=%async_computation.4 | async-start | bytes 2359296 | tf_op jit(solution)/shard_map/all_to_all | solution.py:660
  124.9 1.4 pack.1
  126.3 3.3 %collective-permute-start.8 = (bf16[2,120,128]{2,1,0:T(8,128)(2,1)}, bf16[2,120,128]{2,1,0:T(8,128)(2,1)S(1)}, u32[]{:S(2)}, u32[]{:S(2)}) collective-permute-start(bf16[2,120,128]{2,1,0:T(8,128)(2,1)} %get-tuple-element.59), channel_id=1, source_target_pairs={{0,64},{16,80},{32,96},{48,112},{64,0},{80,16},{96,32},{112,48},{1... | collective-permute-start | bytes 184328 | tf_op jit(solution)/shard_map/ppermute | solution.py:715
  129.6 4.5 %collective-permute-start.9 = (bf16[2,120,128]{2,1,0:T(8,128)(2,1)}, bf16[2,120,128]{2,1,0:T(8,128)(2,1)S(1)}, u32[]{:S(2)}, u32[]{:S(2)}) collective-permute-start(bf16[2,120,128]{2,1,0:T(8,128)(2,1)} %get-tuple-element.60), channel_id=1, source_target_pairs={{0,128},{16,144},{32,160},{48,176},{64,192},{80,208},{96,224},{112... | collective-permute-start | bytes 184328 | tf_op jit(solution)/shard_map/ppermute | solution.py:715
  134.1 3.8 %collective-permute-done.9.refs_2_ = bf16[2,120,128]{2,1,0:T(8,128)(2,1)S(1)} collective-permute-done((bf16[2,120,128]{2,1,0:T(8,128)(2,1)}, bf16[2,120,128]{2,1,0:T(8,128)(2,1)S(1)}, u32[]{:S(2)}, u32[]{:S(2)}) %collective-permute-start.9) | collective-permute-done | bytes 61472 | tf_op jit(solution)/shard_map/ppermute | solution.py:715
  137.9 2.7 %collective-permute-done.10.refs_3_ = bf16[2,120,128]{2,1,0:T(8,128)(2,1)S(1)} collective-permute-done((bf16[2,120,128]{2,1,0:T(8,128)(2,1)}, bf16[2,120,128]{2,1,0:T(8,128)(2,1)S(1)}, u32[]{:S(2)}, u32[]{:S(2)}) %collective-permute-start.10) | collective-permute-done | bytes 61472 | tf_op jit(solution)/shard_map/ppermute | solution.py:715
  140.6 1.5 merge.1.a_ref
  142.1 0.7 collective-permute-start.11
  142.8 3.8 %collective-permute-done.11.b_ref = bf16[2,120,128]{2,1,0:T(8,128)(2,1)S(1)} collective-permute-done((bf16[2,120,128]{2,1,0:T(8,128)(2,1)}, bf16[2,120,128]{2,1,0:T(8,128)(2,1)S(1)}, u32[]{:S(2)}, u32[]{:S(2)}) %collective-permute-start.11) | collective-permute-done | bytes 61472 | tf_op jit(solution)/shard_map/ppermute | solution.py:718
  146.6 1.6 total.1
  148.2 5.2 %all-to-all-start.5 = ((bf16[8,2,120,128]{3,2,1,0:T(8,128)(2,1)}), bf16[8,2,120,128]{3,2,1,0:T(8,128)(2,1)S(1)}, u32[]{:S(2)}, u32[]{:S(2)}) async-start(bf16[8,2,120,128]{3,2,1,0:T(8,128)(2,1)} %total.1), calls=%async_computation.5 | async-start | bytes 983040 | tf_op jit(solution)/shard_map/all_to_all | solution.py:660
  153.4 1.2 post.1
  154.6 14.2 %all-to-all-done.5.x_ref = bf16[8,2,120,128]{3,2,1,0:T(8,128)(2,1)S(1)} async-done(((bf16[8,2,120,128]{3,2,1,0:T(8,128)(2,1)}), bf16[8,2,120,128]{3,2,1,0:T(8,128)(2,1)S(1)}, u32[]{:S(2)}, u32[]{:S(2)}) %all-to-all-start.5) | async-done | bytes 491552 | tf_op jit(solution)/shard_map/all_to_all | solution.py:660
  168.8 0.9 unpack.1
  (21 shorter events, 1.0 us)
Async XLA Ops:
  3.2 23.8 %all-to-all-start = ((bf16[16,288,128]{2,1,0:T(8,128)(2,1)}), bf16[16,288,128]{2,1,0:T(8,128)(2,1)S(1)}, u32[]{:S(2)}, u32[]{:S(2)}) async-start(bf16[16,288,128]{2,1,0:T(8,128)(2,1)} %get-tuple-element.38), calls=%async_computation | async-start | bytes 2359296 | tf_op jit(solution)/shard_map/all_to_all | solution.py:660
  27.0 15.0 %collective-permute-start = (bf16[48,1536]{1,0:T(8,128)(2,1)S(1)}, bf16[48,1536]{1,0:T(8,128)(2,1)S(1)}, u32[]{:S(2)}, u32[]{:S(2)}) collective-permute-start(bf16[48,1536]{1,0:T(8,128)(2,1)S(1)} %get-tuple-element.43), channel_id=1, source_target_pairs={{0,1},{1,2},{2,3},{3,4},{4,5},{5,6},{6,7},{7,8},{8,9},{9,10},{10,1... | collective-permute-start | bytes 442376 | tf_op jit(solution)/shard_map/ppermute | solution.py:687
  29.2 12.8 %collective-permute-start.1 = (bf16[48,1536]{1,0:T(8,128)(2,1)S(1)}, bf16[48,1536]{1,0:T(8,128)(2,1)S(1)}, u32[]{:S(2)}, u32[]{:S(2)}) collective-permute-start(bf16[48,1536]{1,0:T(8,128)(2,1)S(1)} %get-tuple-element.44), channel_id=1, source_target_pairs={{1,0},{2,1},{3,2},{4,3},{5,4},{6,5},{7,6},{8,7},{9,8},{10,9},{11,1... | collective-permute-start | bytes 442376 | tf_op jit(solution)/shard_map/ppermute | solution.py:688
  42.0 19.1 %copy-start = (bf16[48,1536]{1,0:T(8,128)(2,1)}, bf16[48,1536]{1,0:T(8,128)(2,1)S(1)}, u32[]{:S(2)}) copy-start(bf16[48,1536]{1,0:T(8,128)(2,1)S(1)} %collective-permute-done.left_hbm) | copy-start | bytes 442372
  42.0 19.1 %copy-start.1 = (bf16[48,1536]{1,0:T(8,128)(2,1)}, bf16[48,1536]{1,0:T(8,128)(2,1)S(1)}, u32[]{:S(2)}) copy-start(bf16[48,1536]{1,0:T(8,128)(2,1)S(1)} %collective-permute-done.1.right_hbm) | copy-start | bytes 442372
  42.0 17.0 %all-to-all-start.1 = ((bf16[16,144,128]{2,1,0:T(8,128)(2,1)}), bf16[16,144,128]{2,1,0:T(8,128)(2,1)S(1)}, u32[]{:S(2)}, u32[]{:S(2)}) async-start(bf16[16,144,128]{2,1,0:T(8,128)(2,1)} %get-tuple-element.45), calls=%async_computation.1 | async-start | bytes 1179648 | tf_op jit(solution)/shard_map/all_to_all | solution.py:660
  59.1 14.0 %collective-permute-start.2 = (bf16[16,96,128]{2,1,0:T(8,128)(2,1)S(1)}, bf16[16,96,128]{2,1,0:T(8,128)(2,1)S(1)}, u32[]{:S(2)}, u32[]{:S(2)}) collective-permute-start(bf16[16,96,128]{2,1,0:T(8,128)(2,1)S(1)} %slice.4.refs_0_), channel_id=1, source_target_pairs={{0,32},{16,48},{32,0},{48,16},{64,96},{80,112},{96,64},{112,80},{1... | collective-permute-start | bytes 1179656 | tf_op jit(solution)/shard_map/ppermute | solution.py:693
  73.0 19.4 %all-to-all-start.2 = ((bf16[16,128,128]{2,1,0:T(8,128)(2,1)}), bf16[16,128,128]{2,1,0:T(8,128)(2,1)S(1)}, u32[]{:S(2)}, u32[]{:S(2)}) async-start(bf16[16,128,128]{2,1,0:T(8,128)(2,1)} %get-tuple-element.50), calls=%async_computation.2 | async-start | bytes 1048576 | tf_op jit(solution)/shard_map/all_to_all | solution.py:660
  80.4 7.5 %collective-permute-start.3 = (bf16[16,96,128]{2,1,0:T(8,128)(2,1)S(1)}, bf16[16,96,128]{2,1,0:T(8,128)(2,1)S(1)}, u32[]{:S(2)}, u32[]{:S(2)}) collective-permute-start(bf16[16,96,128]{2,1,0:T(8,128)(2,1)S(1)} %slice.4.refs_0_), channel_id=1, source_target_pairs={{0,1},{1,0},{2,3},{3,2},{4,5},{5,4},{6,7},{7,6},{8,9},{9,8},{10,11... | collective-permute-start | bytes 1179656 | tf_op jit(solution)/shard_map/ppermute | solution.py:694
  80.5 7.4 %collective-permute-start.6 = (bf16[128,768]{1,0:T(8,128)(2,1)}, bf16[128,768]{1,0:T(8,128)(2,1)S(1)}, u32[]{:S(2)}, u32[]{:S(2)}) collective-permute-start(bf16[128,768]{1,0:T(8,128)(2,1)} %get-tuple-element.56), channel_id=1, source_target_pairs={{0,32},{16,48},{32,0},{48,16},{64,96},{80,112},{96,64},{112,80},{1... | collective-permute-start | bytes 589832 | tf_op jit(solution)/shard_map/ppermute | solution.py:703
  80.7 8.7 %collective-permute-start.4 = (bf16[16,96,128]{2,1,0:T(8,128)(2,1)S(1)}, bf16[16,96,128]{2,1,0:T(8,128)(2,1)S(1)}, u32[]{:S(2)}, u32[]{:S(2)}) collective-permute-start(bf16[16,96,128]{2,1,0:T(8,128)(2,1)S(1)} %collective-permute-done.2.refs_2_), channel_id=1, source_target_pairs={{0,1},{1,0},{2,3},{3,2},{4,5},{5,4},{6,7},{7,6},{8,9},{9,8},{10,11... | collective-permute-start | bytes 1179656 | tf_op jit(solution)/shard_map/ppermute | solution.py:701
  80.9 7.0 %collective-permute-start.5 = (bf16[128,768]{1,0:T(8,128)(2,1)}, bf16[128,768]{1,0:T(8,128)(2,1)S(1)}, u32[]{:S(2)}, u32[]{:S(2)}) collective-permute-start(bf16[128,768]{1,0:T(8,128)(2,1)} %get-tuple-element.55.refs_4_), channel_id=1, source_target_pairs={{0,1},{1,0},{2,3},{3,2},{4,5},{5,4},{6,7},{7,6},{8,9},{9,8},{10,11... | collective-permute-start | bytes 589832 | tf_op jit(solution)/shard_map/ppermute | solution.py:704
  87.9 1.4 collective-permute-start.7
  93.2 25.0 %all-to-all-start.3 = ((bf16[16,320,128]{2,1,0:T(8,128)(2,1)}), bf16[16,320,128]{2,1,0:T(8,128)(2,1)S(1)}, u32[]{:S(2)}, u32[]{:S(2)}) async-start(bf16[16,320,128]{2,1,0:T(8,128)(2,1)} %tail.1), calls=%async_computation.3 | async-start | bytes 2621440 | tf_op jit(solution)/shard_map/all_to_all | solution.py:660
  118.3 29.9 %all-to-all-start.4 = ((bf16[16,288,128]{2,1,0:T(8,128)(2,1)}), bf16[16,288,128]{2,1,0:T(8,128)(2,1)S(1)}, u32[]{:S(2)}, u32[]{:S(2)}) async-start(bf16[16,288,128]{2,1,0:T(8,128)(2,1)} %attend_back.1), calls=%async_computation.4 | async-start | bytes 2359296 | tf_op jit(solution)/shard_map/all_to_all | solution.py:660
  126.3 7.8 %collective-permute-start.8 = (bf16[2,120,128]{2,1,0:T(8,128)(2,1)}, bf16[2,120,128]{2,1,0:T(8,128)(2,1)S(1)}, u32[]{:S(2)}, u32[]{:S(2)}) collective-permute-start(bf16[2,120,128]{2,1,0:T(8,128)(2,1)} %get-tuple-element.59), channel_id=1, source_target_pairs={{0,64},{16,80},{32,96},{48,112},{64,0},{80,16},{96,32},{112,48},{1... | collective-permute-start | bytes 184328 | tf_op jit(solution)/shard_map/ppermute | solution.py:715
  129.6 8.3 %collective-permute-start.9 = (bf16[2,120,128]{2,1,0:T(8,128)(2,1)}, bf16[2,120,128]{2,1,0:T(8,128)(2,1)S(1)}, u32[]{:S(2)}, u32[]{:S(2)}) collective-permute-start(bf16[2,120,128]{2,1,0:T(8,128)(2,1)} %get-tuple-element.60), channel_id=1, source_target_pairs={{0,128},{16,144},{32,160},{48,176},{64,192},{80,208},{96,224},{112... | collective-permute-start | bytes 184328 | tf_op jit(solution)/shard_map/ppermute | solution.py:715
  134.1 6.5 %collective-permute-start.10 = (bf16[2,120,128]{2,1,0:T(8,128)(2,1)}, bf16[2,120,128]{2,1,0:T(8,128)(2,1)S(1)}, u32[]{:S(2)}, u32[]{:S(2)}) collective-permute-start(bf16[2,120,128]{2,1,0:T(8,128)(2,1)} %get-tuple-element.61), channel_id=1, source_target_pairs={{0,192},{16,208},{32,224},{48,240},{64,128},{80,144},{96,160},{112... | collective-permute-start | bytes 184328 | tf_op jit(solution)/shard_map/ppermute | solution.py:715
  142.1 4.4 %collective-permute-start.11 = (bf16[2,120,128]{2,1,0:T(8,128)(2,1)}, bf16[2,120,128]{2,1,0:T(8,128)(2,1)S(1)}, u32[]{:S(2)}, u32[]{:S(2)}) collective-permute-start(bf16[2,120,128]{2,1,0:T(8,128)(2,1)} %merge.1.a_ref), channel_id=1, source_target_pairs={{0,16},{16,0},{32,48},{48,32},{64,80},{80,64},{96,112},{112,96},{1... | collective-permute-start | bytes 184328 | tf_op jit(solution)/shard_map/ppermute | solution.py:718
  148.2 20.6 %all-to-all-start.5 = ((bf16[8,2,120,128]{3,2,1,0:T(8,128)(2,1)}), bf16[8,2,120,128]{3,2,1,0:T(8,128)(2,1)S(1)}, u32[]{:S(2)}, u32[]{:S(2)}) async-start(bf16[8,2,120,128]{3,2,1,0:T(8,128)(2,1)} %total.1), calls=%async_computation.5 | async-start | bytes 983040 | tf_op jit(solution)/shard_map/all_to_all | solution.py:660

commit v9 on v7

--- a/solution.py
+++ b/solution.py
@@ -579,7 +579,7 @@
     units = x.shape[1] // HEAD * HEAD * 2
     return pl.pallas_call(
         pack_kernel,
-        out_shape=(pltpu.HBM((2, PIECE, LANES), BF),) * (GROUP // 2),
+        out_shape=(jax.ShapeDtypeStruct((2, PIECE, LANES), BF),) * (GROUP // 2),
         in_specs=[pl.BlockSpec(memory_space=pltpu.SMEM), pl.BlockSpec()],
         scratch_shapes=[pltpu.VMEM((units, LANES), F32)],
         compiler_params=params(12),
@@ -598,7 +598,7 @@
 def merge(xs):
     return pl.pallas_call(
         merge_kernel,
-        out_shape=(pltpu.HBM(xs[0].shape[1:], BF),) * 2,
+        out_shape=(jax.ShapeDtypeStruct(xs[0].shape[1:], BF),) * 2,
         compiler_params=params(8),
         cost_estimate=cost(1e6, 1e6),
         name="merge",
@@ -615,7 +615,7 @@
 def total(xs, batch):
     return pl.pallas_call(
         total_kernel,
-        out_shape=pltpu.HBM((batch,) + xs[0].shape, BF),
+        out_shape=jax.ShapeDtypeStruct((batch,) + xs[0].shape, BF),
         compiler_params=params(12),
         cost_estimate=cost(1e6, 1e6),
         name="total",
@@ -713,11 +713,11 @@
     payload, partial = lax.optimization_barrier((payload, partial))
     back = exchange(payload, "seq")
     packed = pack(info, partial)
-    level_parts = [in_hbm(packed[0])] + [
+    level_parts = [packed[0]] + [
         lax.ppermute(packed[k], "dp", hop(2 * k)) for k in range(1, GROUP // 2)
     ]
     keep, send = merge(level_parts)
-    packed = [in_hbm(keep), lax.ppermute(send, "dp", hop(1))]
+    packed = [keep, lax.ppermute(send, "dp", hop(1))]
     summed, back = lax.optimization_barrier((total(packed, batch), back))
     final = exchange(summed, "dp")
     query_grad, key_grad, value_grad = post(back)

time: 163 us -> 162 us (level)
  Pallas kernels: 45.2 us -> 42.3 us
    pallas_call x3, Pallas kernels: 4.42 us -> 1.55 us  [the longest x1 0.81 us: total(): pl.pallas_call(total_kernel, out_shape=jax.ShapeDtypeStruct((batch,) + xs...]
  transfers between devices with their start and end apart: 18 -> 18, of which waited for: 9 -> 9; matrix products, arithmetic and copies ran while one was open for 0% -> 0% of each run, Pallas kernels for 20% -> 18%
where the time goes in v9:
time: 162 us; the launch traced here: 160 us
  waiting for transfers between devices  58.6 us (36%)
  starting transfers between devices  57.7 us (36%)
  Pallas kernels  42.3 us (26%)
    all_to_all x6, starting transfers between devices, exchange(): lax.all_to_all(x, axis, split_axis=0, concat_axis=0, tiled=True, axis_ind...  40.6 us
    all_to_all x6, waiting for transfers between devices, exchange(): lax.all_to_all(x, axis, split_axis=0, concat_axis=0, tiled=True, axis_ind...  30.3 us
    pallas_call x1, Pallas kernels, conv(): pl.pallas_call(conv_kernel_body, out_shape=(pltpu.HBM((rows, width), BF),...  11.9 us
    pallas_call x1, Pallas kernels, bwd(): pl.pallas_call(bwd_kernel, grid=(steps,), out_shape=pltpu.HBM((blocks, 3...  11.8 us
    ppermute x1, waiting for transfers between devices, shards(): left = lax.ppermute(edge_up, 'seq', up)  10.7 us
    pallas_call x1, Pallas kernels, fwd(): pl.pallas_call(fwd_kernel, out_shape=(pltpu.HBM((steps, frames, QT), BF),...  8.55 us
    ppermute x3, starting transfers between devices, shards(): lax.ppermute(packed[k], 'dp', hop(2 * k))  7.85 us
    ppermute x1, waiting for transfers between devices, shards(): level = lax.ppermute(send, 'dp', levels)  6.64 us
  transfers between devices with their start and end apart: 18, of which 9 were waited for; matrix products, arithmetic and copies ran while one was open for 0% of the time, Pallas kernels for 18%

profile of v9, /device:TPU:2, one launch (start us, length us, event | category | flops | bytes accessed | tf_op | source)
XLA Modules:
  0.0 160.1 jit_solution(10674597065039915278)
XLA Ops:
  0.6 2.5 %pre.1 = (bf16[16,288,128]{2,1,0:T(8,128)(2,1)}, bf16[48,1536]{1,0:T(8,128)(2,1)S(1)}, bf16[48,1536]{1,0:T(8,128)(2,1)S(1)}) custom-call(bf16[128,1536]{1,0:T(8,128)(2,1)} %bitcast.13, bf16[128,1536]{1,0:T(8,128)(2,1)} %bitcast.14, bf16[128,1536]{1,0:T(8,128)(2,1)} %bitcast.15, bf16[128,1536]{1,0:T(8,128)(2,1)} %bitcast.16, bf16[128,1536]{1,0:T(8,128)(2,1)} %bitcast.18), custom_call_target="tpu_custom_call" | custom-call | flops 1000000 | bytes 3000000 | tf_op jit(solution)/shard_map/pre/pallas_call | solution.py:72
  3.2 7.5 %all-to-all-start = ((bf16[16,288,128]{2,1,0:T(8,128)(2,1)}), bf16[16,288,128]{2,1,0:T(8,128)(2,1)S(1)}, u32[]{:S(2)}, u32[]{:S(2)}) async-start(bf16[16,288,128]{2,1,0:T(8,128)(2,1)} %get-tuple-element.37), calls=%async_computation | async-start | bytes 2359296 | tf_op jit(solution)/shard_map/all_to_all | solution.py:663
  10.7 2.0 %collective-permute-start = (bf16[48,1536]{1,0:T(8,128)(2,1)S(1)}, bf16[48,1536]{1,0:T(8,128)(2,1)S(1)}, u32[]{:S(2)}, u32[]{:S(2)}) collective-permute-start(bf16[48,1536]{1,0:T(8,128)(2,1)S(1)} %get-tuple-element.38), channel_id=1, source_target_pairs={{0,1},{1,2},{2,3},{3,4},{4,5},{5,6},{6,7},{7,8},{8,9},{9,10},{10,1... | collective-permute-start | bytes 442376 | tf_op jit(solution)/shard_map/ppermute | solution.py:689
  12.7 3.5 %collective-permute-start.1 = (bf16[48,1536]{1,0:T(8,128)(2,1)S(1)}, bf16[48,1536]{1,0:T(8,128)(2,1)S(1)}, u32[]{:S(2)}, u32[]{:S(2)}) collective-permute-start(bf16[48,1536]{1,0:T(8,128)(2,1)S(1)} %get-tuple-element.39), channel_id=1, source_target_pairs={{1,0},{2,1},{3,2},{4,3},{5,4},{6,5},{7,6},{8,7},{9,8},{10,9},{11,1... | collective-permute-start | bytes 442376 | tf_op jit(solution)/shard_map/ppermute | solution.py:690
  16.9 10.7 %collective-permute-done.left_hbm = bf16[48,1536]{1,0:T(8,128)(2,1)S(1)} collective-permute-done((bf16[48,1536]{1,0:T(8,128)(2,1)S(1)}, bf16[48,1536]{1,0:T(8,128)(2,1)S(1)}, u32[]{:S(2)}, u32[]{:S(2)}) %collective-permute-start) | collective-permute-done | bytes 147488 | tf_op jit(solution)/shard_map/ppermute | solution.py:689
  27.6 8.5 %attend.1 = (bf16[4,2048,512]{2,1,0:T(8,128)(2,1)}, f32[96,2048]{1,0:T(8,128)}, f32[8,2048]{1,0:T(8,128)S(1)}, bf16[16,144,128]{2,1,0:T(8,128)(2,1)}) custom-call(s32[1]{0:T(128)S(6)} %copy.16.len_ref, bf16[16,288,128]{2,1,0:T(8,128)(2,1)S(1)} %all-to-all-done.x_ref), custom_call_target="tpu_custom_call" | custom-call | flops 8999999488 | bytes 10000000 | tf_op jit(solution)/shard_map/attend/pallas_call | solution.py:167
  36.2 6.4 %all-to-all-start.1 = ((bf16[16,144,128]{2,1,0:T(8,128)(2,1)}), bf16[16,144,128]{2,1,0:T(8,128)(2,1)S(1)}, u32[]{:S(2)}, u32[]{:S(2)}) async-start(bf16[16,144,128]{2,1,0:T(8,128)(2,1)} %get-tuple-element.41), calls=%async_computation.1 | async-start | bytes 1179648 | tf_op jit(solution)/shard_map/all_to_all | solution.py:663
  42.7 9.1 %all-to-all-done.1.att_ref = bf16[16,144,128]{2,1,0:T(8,128)(2,1)S(1)} async-done(((bf16[16,144,128]{2,1,0:T(8,128)(2,1)}), bf16[16,144,128]{2,1,0:T(8,128)(2,1)S(1)}, u32[]{:S(2)}, u32[]{:S(2)}) %all-to-all-start.1) | async-done | bytes 589856 | tf_op jit(solution)/shard_map/all_to_all | solution.py:663
  51.9 2.0 %collective-permute-start.2 = (bf16[16,96,128]{2,1,0:T(8,128)(2,1)S(1)}, bf16[16,96,128]{2,1,0:T(8,128)(2,1)S(1)}, u32[]{:S(2)}, u32[]{:S(2)}) collective-permute-start(bf16[16,96,128]{2,1,0:T(8,128)(2,1)S(1)} %slice.4.refs_0_), channel_id=1, source_target_pairs={{0,32},{16,48},{32,0},{48,16},{64,96},{80,112},{96,64},{112,80},{1... | collective-permute-start | bytes 1179656 | tf_op jit(solution)/shard_map/ppermute | solution.py:695
  53.9 11.9 %convolve.1 = (bf16[128,1536]{1,0:T(8,128)(2,1)}, bf16[16,128,128]{2,1,0:T(8,128)(2,1)}, bf16[128,768]{1,0:T(8,128)(2,1)}, bf16[128,768]{1,0:T(8,128)(2,1)}) custom-call(s32[5]{0:T(128)S(1)} %stack.19.info_ref, bf16[16,144,128]{2,1,0:T(8,128)(2,1)S(1)} %all-to-all-done.1.att_ref, bf16[128,1536]{1,0:T(8,128)(2,1)} %bitcast.17, bf16[128,1536]{1,0:T(8,128)(2,1)} %bitcast.19, ...), custom_call_target="tpu_custom_call" | custom-call | flops 8999999488 | bytes 10000000 | tf_op jit(solution)/shard_map/convolve/pallas_call | solution.py:349
  65.8 7.3 %all-to-all-start.2 = ((bf16[16,128,128]{2,1,0:T(8,128)(2,1)}), bf16[16,128,128]{2,1,0:T(8,128)(2,1)S(1)}, u32[]{:S(2)}, u32[]{:S(2)}) async-start(bf16[16,128,128]{2,1,0:T(8,128)(2,1)} %get-tuple-element.46), calls=%async_computation.2 | async-start | bytes 1048576 | tf_op jit(solution)/shard_map/all_to_all | solution.py:663
  73.7 0.4 collective-permute-start.5
  74.1 6.6 %collective-permute-done.6.refs_6_ = bf16[128,768]{1,0:T(8,128)(2,1)S(1)} collective-permute-done((bf16[128,768]{1,0:T(8,128)(2,1)}, bf16[128,768]{1,0:T(8,128)(2,1)S(1)}, u32[]{:S(2)}, u32[]{:S(2)}) %collective-permute-start.6) | collective-permute-done | bytes 196640 | tf_op jit(solution)/shard_map/ppermute | solution.py:705
  80.7 1.4 collective-permute-done.7.refs_7_
  82.1 3.0 %outer.1.w_ref = bf16[16,320,128]{2,1,0:T(8,128)(2,1)} custom-call(s32[5]{0:T(128)S(1)} %stack.19.info_ref, bf16[16,96,128]{2,1,0:T(8,128)(2,1)S(1)} %slice.4.refs_0_, bf16[16,96,128]{2,1,0:T(8,128)(2,1)S(1)} %collective-permute-done.3.refs_1_, bf16[16,96,128]{2,1,0:T(8,128)(2,1)S(1)} %collective-permute-done.2.refs_2_, ...), custom_call_target="tpu_custom_call" | custom-call | flops 1000000000 | bytes 4000000 | tf_op jit(solution)/shard_map/outer/pallas_call | solution.py:414
  85.2 0.8 tail.1
  86.0 7.3 %all-to-all-start.3 = ((bf16[16,320,128]{2,1,0:T(8,128)(2,1)}), bf16[16,320,128]{2,1,0:T(8,128)(2,1)S(1)}, u32[]{:S(2)}, u32[]{:S(2)}) async-start(bf16[16,320,128]{2,1,0:T(8,128)(2,1)} %tail.1), calls=%async_computation.3 | async-start | bytes 2621440 | tf_op jit(solution)/shard_map/all_to_all | solution.py:663
  93.3 11.8 %attend_back.1 = bf16[16,288,128]{2,1,0:T(8,128)(2,1)} custom-call(bf16[16,288,128]{2,1,0:T(8,128)(2,1)S(1)} %all-to-all-done.x_ref, bf16[16,128,128]{2,1,0:T(8,128)(2,1)S(1)} %all-to-all-done.2.g_ref, bf16[4,2048,512]{2,1,0:T(8,128)(2,1)} %get-tuple-element.47.e_ref, f32[96,2048]{1,0:T(8,128)} %get-tuple-element.48.o_ref, ...), custom_call_target="tpu_custom_call" | custom-call | flops 20000000000 | bytes 10000000 | tf_op jit(solution)/shard_map/attend_back/pallas_call | solution.py:512
  105.1 6.0 %all-to-all-done.3.x_ref = bf16[16,320,128]{2,1,0:T(8,128)(2,1)S(1)} async-done(((bf16[16,320,128]{2,1,0:T(8,128)(2,1)}), bf16[16,320,128]{2,1,0:T(8,128)(2,1)S(1)}, u32[]{:S(2)}, u32[]{:S(2)}) %all-to-all-start.3) | async-done | bytes 1310752 | tf_op jit(solution)/shard_map/all_to_all | solution.py:663
  111.1 6.6 %all-to-all-start.4 = ((bf16[16,288,128]{2,1,0:T(8,128)(2,1)}), bf16[16,288,128]{2,1,0:T(8,128)(2,1)S(1)}, u32[]{:S(2)}, u32[]{:S(2)}) async-start(bf16[16,288,128]{2,1,0:T(8,128)(2,1)} %attend_back.1), calls=%async_computation.4 | async-start | bytes 2359296 | tf_op jit(solution)/shard_map/all_to_all | solution.py:663
  117.7 0.7 pack.1
  118.4 3.4 %collective-permute-start.8 = (bf16[2,120,128]{2,1,0:T(8,128)(2,1)S(1)}, bf16[2,120,128]{2,1,0:T(8,128)(2,1)S(1)}, u32[]{:S(2)}, u32[]{:S(2)}) collective-permute-start(bf16[2,120,128]{2,1,0:T(8,128)(2,1)S(1)} %get-tuple-element.55), channel_id=1, source_target_pairs={{0,64},{16,80},{32,96},{48,112},{64,0},{80,16},{96,32},{112,48},{1... | collective-permute-start | bytes 184328 | tf_op jit(solution)/shard_map/ppermute | solution.py:717
  121.8 4.5 %collective-permute-start.9 = (bf16[2,120,128]{2,1,0:T(8,128)(2,1)S(1)}, bf16[2,120,128]{2,1,0:T(8,128)(2,1)S(1)}, u32[]{:S(2)}, u32[]{:S(2)}) collective-permute-start(bf16[2,120,128]{2,1,0:T(8,128)(2,1)S(1)} %get-tuple-element.56), channel_id=1, source_target_pairs={{0,128},{16,144},{32,160},{48,176},{64,192},{80,208},{96,224},{112... | collective-permute-start | bytes 184328 | tf_op jit(solution)/shard_map/ppermute | solution.py:717
  126.3 3.6 %collective-permute-done.9.refs_2_ = bf16[2,120,128]{2,1,0:T(8,128)(2,1)S(1)} collective-permute-done((bf16[2,120,128]{2,1,0:T(8,128)(2,1)S(1)}, bf16[2,120,128]{2,1,0:T(8,128)(2,1)S(1)}, u32[]{:S(2)}, u32[]{:S(2)}) %collective-permute-start.9) | collective-permute-done | bytes 61472 | tf_op jit(solution)/shard_map/ppermute | solution.py:717
  129.9 2.7 %collective-permute-done.10.refs_3_ = bf16[2,120,128]{2,1,0:T(8,128)(2,1)S(1)} collective-permute-done((bf16[2,120,128]{2,1,0:T(8,128)(2,1)S(1)}, bf16[2,120,128]{2,1,0:T(8,128)(2,1)S(1)}, u32[]{:S(2)}, u32[]{:S(2)}) %collective-permute-start.10) | collective-permute-done | bytes 61472 | tf_op jit(solution)/shard_map/ppermute | solution.py:717
  132.7 0.8 collective-permute-start.11
  133.4 3.2 %collective-permute-done.11.refs_1_ = bf16[120,128]{1,0:T(8,128)(2,1)S(1)} collective-permute-done((bf16[120,128]{1,0:T(8,128)(2,1)S(1)}, bf16[120,128]{1,0:T(8,128)(2,1)S(1)}, u32[]{:S(2)}, u32[]{:S(2)}) %collective-permute-start.11) | collective-permute-done | bytes 30752 | tf_op jit(solution)/shard_map/ppermute | solution.py:720
  136.6 0.8 total.1
  137.5 5.4 %all-to-all-start.5 = ((bf16[16,120,128]{2,1,0:T(8,128)(2,1)}), bf16[16,120,128]{2,1,0:T(8,128)(2,1)S(1)}, u32[]{:S(2)}, u32[]{:S(2)}) async-start(bf16[16,120,128]{2,1,0:T(8,128)(2,1)} %total.1), calls=%async_computation.5 | async-start | bytes 983040 | tf_op jit(solution)/shard_map/all_to_all | solution.py:663
  142.9 1.2 post.1
  144.1 15.2 %all-to-all-done.5.x_ref = bf16[16,120,128]{2,1,0:T(8,128)(2,1)S(1)} async-done(((bf16[16,120,128]{2,1,0:T(8,128)(2,1)}), bf16[16,120,128]{2,1,0:T(8,128)(2,1)S(1)}, u32[]{:S(2)}, u32[]{:S(2)}) %all-to-all-start.5) | async-done | bytes 491552 | tf_op jit(solution)/shard_map/all_to_all | solution.py:663
  159.2 0.9 unpack.1
  (21 shorter events, 0.7 us)
Async XLA Ops:
  3.2 24.4 %all-to-all-start = ((bf16[16,288,128]{2,1,0:T(8,128)(2,1)}), bf16[16,288,128]{2,1,0:T(8,128)(2,1)S(1)}, u32[]{:S(2)}, u32[]{:S(2)}) async-start(bf16[16,288,128]{2,1,0:T(8,128)(2,1)} %get-tuple-element.37), calls=%async_computation | async-start | bytes 2359296 | tf_op jit(solution)/shard_map/all_to_all | solution.py:663
  10.7 16.9 %collective-permute-start = (bf16[48,1536]{1,0:T(8,128)(2,1)S(1)}, bf16[48,1536]{1,0:T(8,128)(2,1)S(1)}, u32[]{:S(2)}, u32[]{:S(2)}) collective-permute-start(bf16[48,1536]{1,0:T(8,128)(2,1)S(1)} %get-tuple-element.38), channel_id=1, source_target_pairs={{0,1},{1,2},{2,3},{3,4},{4,5},{5,6},{6,7},{7,8},{8,9},{9,10},{10,1... | collective-permute-start | bytes 442376 | tf_op jit(solution)/shard_map/ppermute | solution.py:689
  12.7 14.9 %collective-permute-start.1 = (bf16[48,1536]{1,0:T(8,128)(2,1)S(1)}, bf16[48,1536]{1,0:T(8,128)(2,1)S(1)}, u32[]{:S(2)}, u32[]{:S(2)}) collective-permute-start(bf16[48,1536]{1,0:T(8,128)(2,1)S(1)} %get-tuple-element.39), channel_id=1, source_target_pairs={{1,0},{2,1},{3,2},{4,3},{5,4},{6,5},{7,6},{8,7},{9,8},{10,9},{11,1... | collective-permute-start | bytes 442376 | tf_op jit(solution)/shard_map/ppermute | solution.py:690
  27.6 8.6 %copy-start = (bf16[48,1536]{1,0:T(8,128)(2,1)}, bf16[48,1536]{1,0:T(8,128)(2,1)S(1)}, u32[]{:S(2)}) copy-start(bf16[48,1536]{1,0:T(8,128)(2,1)S(1)} %collective-permute-done.left_hbm) | copy-start | bytes 442372
  27.6 8.6 %copy-start.1 = (bf16[48,1536]{1,0:T(8,128)(2,1)}, bf16[48,1536]{1,0:T(8,128)(2,1)S(1)}, u32[]{:S(2)}) copy-start(bf16[48,1536]{1,0:T(8,128)(2,1)S(1)} %collective-permute-done.1.right_hbm) | copy-start | bytes 442372
  36.2 15.7 %all-to-all-start.1 = ((bf16[16,144,128]{2,1,0:T(8,128)(2,1)}), bf16[16,144,128]{2,1,0:T(8,128)(2,1)S(1)}, u32[]{:S(2)}, u32[]{:S(2)}) async-start(bf16[16,144,128]{2,1,0:T(8,128)(2,1)} %get-tuple-element.41), calls=%async_computation.1 | async-start | bytes 1179648 | tf_op jit(solution)/shard_map/all_to_all | solution.py:663
  51.9 14.0 %collective-permute-start.2 = (bf16[16,96,128]{2,1,0:T(8,128)(2,1)S(1)}, bf16[16,96,128]{2,1,0:T(8,128)(2,1)S(1)}, u32[]{:S(2)}, u32[]{:S(2)}) collective-permute-start(bf16[16,96,128]{2,1,0:T(8,128)(2,1)S(1)} %slice.4.refs_0_), channel_id=1, source_target_pairs={{0,32},{16,48},{32,0},{48,16},{64,96},{80,112},{96,64},{112,80},{1... | collective-permute-start | bytes 1179656 | tf_op jit(solution)/shard_map/ppermute | solution.py:695
  65.8 19.4 %all-to-all-start.2 = ((bf16[16,128,128]{2,1,0:T(8,128)(2,1)}), bf16[16,128,128]{2,1,0:T(8,128)(2,1)S(1)}, u32[]{:S(2)}, u32[]{:S(2)}) async-start(bf16[16,128,128]{2,1,0:T(8,128)(2,1)} %get-tuple-element.46), calls=%async_computation.2 | async-start | bytes 1048576 | tf_op jit(solution)/shard_map/all_to_all | solution.py:663
  73.2 7.5 %collective-permute-start.3 = (bf16[16,96,128]{2,1,0:T(8,128)(2,1)S(1)}, bf16[16,96,128]{2,1,0:T(8,128)(2,1)S(1)}, u32[]{:S(2)}, u32[]{:S(2)}) collective-permute-start(bf16[16,96,128]{2,1,0:T(8,128)(2,1)S(1)} %slice.4.refs_0_), channel_id=1, source_target_pairs={{0,1},{1,0},{2,3},{3,2},{4,5},{5,4},{6,7},{7,6},{8,9},{9,8},{10,11... | collective-permute-start | bytes 1179656 | tf_op jit(solution)/shard_map/ppermute | solution.py:696
  73.3 7.4 %collective-permute-start.6 = (bf16[128,768]{1,0:T(8,128)(2,1)}, bf16[128,768]{1,0:T(8,128)(2,1)S(1)}, u32[]{:S(2)}, u32[]{:S(2)}) collective-permute-start(bf16[128,768]{1,0:T(8,128)(2,1)} %get-tuple-element.52), channel_id=1, source_target_pairs={{0,32},{16,48},{32,0},{48,16},{64,96},{80,112},{96,64},{112,80},{1... | collective-permute-start | bytes 589832 | tf_op jit(solution)/shard_map/ppermute | solution.py:705
  73.4 8.7 %collective-permute-start.4 = (bf16[16,96,128]{2,1,0:T(8,128)(2,1)S(1)}, bf16[16,96,128]{2,1,0:T(8,128)(2,1)S(1)}, u32[]{:S(2)}, u32[]{:S(2)}) collective-permute-start(bf16[16,96,128]{2,1,0:T(8,128)(2,1)S(1)} %collective-permute-done.2.refs_2_), channel_id=1, source_target_pairs={{0,1},{1,0},{2,3},{3,2},{4,5},{5,4},{6,7},{7,6},{8,9},{9,8},{10,11... | collective-permute-start | bytes 1179656 | tf_op jit(solution)/shard_map/ppermute | solution.py:703
  73.7 7.0 %collective-permute-start.5 = (bf16[128,768]{1,0:T(8,128)(2,1)}, bf16[128,768]{1,0:T(8,128)(2,1)S(1)}, u32[]{:S(2)}, u32[]{:S(2)}) collective-permute-start(bf16[128,768]{1,0:T(8,128)(2,1)} %get-tuple-element.51.refs_4_), channel_id=1, source_target_pairs={{0,1},{1,0},{2,3},{3,2},{4,5},{5,4},{6,7},{7,6},{8,9},{9,8},{10,11... | collective-permute-start | bytes 589832 | tf_op jit(solution)/shard_map/ppermute | solution.py:706
  80.7 1.4 collective-permute-start.7
  86.0 25.0 %all-to-all-start.3 = ((bf16[16,320,128]{2,1,0:T(8,128)(2,1)}), bf16[16,320,128]{2,1,0:T(8,128)(2,1)S(1)}, u32[]{:S(2)}, u32[]{:S(2)}) async-start(bf16[16,320,128]{2,1,0:T(8,128)(2,1)} %tail.1), calls=%async_computation.3 | async-start | bytes 2621440 | tf_op jit(solution)/shard_map/all_to_all | solution.py:663
  111.1 26.4 %all-to-all-start.4 = ((bf16[16,288,128]{2,1,0:T(8,128)(2,1)}), bf16[16,288,128]{2,1,0:T(8,128)(2,1)S(1)}, u32[]{:S(2)}, u32[]{:S(2)}) async-start(bf16[16,288,128]{2,1,0:T(8,128)(2,1)} %attend_back.1), calls=%async_computation.4 | async-start | bytes 2359296 | tf_op jit(solution)/shard_map/all_to_all | solution.py:663
  118.4 7.9 %collective-permute-start.8 = (bf16[2,120,128]{2,1,0:T(8,128)(2,1)S(1)}, bf16[2,120,128]{2,1,0:T(8,128)(2,1)S(1)}, u32[]{:S(2)}, u32[]{:S(2)}) collective-permute-start(bf16[2,120,128]{2,1,0:T(8,128)(2,1)S(1)} %get-tuple-element.55), channel_id=1, source_target_pairs={{0,64},{16,80},{32,96},{48,112},{64,0},{80,16},{96,32},{112,48},{1... | collective-permute-start | bytes 184328 | tf_op jit(solution)/shard_map/ppermute | solution.py:717
  121.8 8.1 %collective-permute-start.9 = (bf16[2,120,128]{2,1,0:T(8,128)(2,1)S(1)}, bf16[2,120,128]{2,1,0:T(8,128)(2,1)S(1)}, u32[]{:S(2)}, u32[]{:S(2)}) collective-permute-start(bf16[2,120,128]{2,1,0:T(8,128)(2,1)S(1)} %get-tuple-element.56), channel_id=1, source_target_pairs={{0,128},{16,144},{32,160},{48,176},{64,192},{80,208},{96,224},{112... | collective-permute-start | bytes 184328 | tf_op jit(solution)/shard_map/ppermute | solution.py:717
  126.3 6.3 %collective-permute-start.10 = (bf16[2,120,128]{2,1,0:T(8,128)(2,1)S(1)}, bf16[2,120,128]{2,1,0:T(8,128)(2,1)S(1)}, u32[]{:S(2)}, u32[]{:S(2)}) collective-permute-start(bf16[2,120,128]{2,1,0:T(8,128)(2,1)S(1)} %get-tuple-element.57), channel_id=1, source_target_pairs={{0,192},{16,208},{32,224},{48,240},{64,128},{80,144},{96,160},{112... | collective-permute-start | bytes 184328 | tf_op jit(solution)/shard_map/ppermute | solution.py:717
  132.7 4.0 %collective-permute-start.11 = (bf16[120,128]{1,0:T(8,128)(2,1)S(1)}, bf16[120,128]{1,0:T(8,128)(2,1)S(1)}, u32[]{:S(2)}, u32[]{:S(2)}) collective-permute-start(bf16[120,128]{1,0:T(8,128)(2,1)S(1)} %get-tuple-element.59), channel_id=1, source_target_pairs={{0,16},{16,0},{32,48},{48,32},{64,80},{80,64},{96,112},{112,96},{1... | collective-permute-start | bytes 92168 | tf_op jit(solution)/shard_map/ppermute | solution.py:720
  137.5 21.8 %all-to-all-start.5 = ((bf16[16,120,128]{2,1,0:T(8,128)(2,1)}), bf16[16,120,128]{2,1,0:T(8,128)(2,1)S(1)}, u32[]{:S(2)}, u32[]{:S(2)}) async-start(bf16[16,120,128]{2,1,0:T(8,128)(2,1)} %total.1), calls=%async_computation.5 | async-start | bytes 983040 | tf_op jit(solution)/shard_map/all_to_all | solution.py:663
